TPU v7x, 128 devices: a whole 4x4x4 slice. The times are simulated.
128 devices in a mesh: dp: 16 (over x_hi, y, core), tensor: 8 (over x_lo, z).
Axes of the slice: x: 4 (x_hi: 2, x_lo: 2; x = x_hi * 2 + x_lo), y: 4, z: 4, core: 2. Of those that a mesh axis runs over, the one named last changes fastest.
Arguments:
- gate_pre: bfloat16 [32, 512, 14336], P('dp', None, 'tensor'), may hold values from -6 to 6
- up_val: bfloat16 [32, 512, 14336], P('dp', None, 'tensor'), may hold values from -6 to 6
- layer_in: bfloat16 [32, 512, 4096], P('dp', None, 'tensor'), may hold values from -6 to 6
- out_grad: bfloat16 [32, 512, 4096], P('dp'), may hold values from -0.29882812 to 0.29882812
- down_weight: bfloat16 [14336, 4096], P('tensor', 'dp'), may hold values from -0.09375 to 0.09375
- down_in_proj: bfloat16 [14336, 64], P('tensor'), may hold values from -0.046875 to 0.046875
- down_out_proj: bfloat16 [4096, 64], replicated, may hold values from -0.09375 to 0.09375
- up_in_proj: bfloat16 [4096, 64], P('tensor'), may hold values from -0.09375 to 0.09375
- up_out_proj: bfloat16 [14336, 64], P('tensor'), may hold values from -0.046875 to 0.046875
- counts: int32 [32], P('dp'), may hold values from 128 to 512, as said below
- assignment: int32 [32], P('dp'), may hold values from 0 to 31, each once
- queries: int32 [8], replicated, may hold values from 0 to 31
Outputs:
- projected: float32 [2, 32, 4096], P(None, 'dp')
- gram: float32 [2, 32, 32], replicated
- scores: float32 [2, 8, 32], replicated
Inputs may be any that keep to these rules, and one draw needn't show every extreme that they name: `counts`: some example has 512 live tokens and some has 128.
All inputs are finite; a program needn't handle non-finite values.
Results may differ from a plain program's by a relative error of at most 0.003.
Values may be sent and summed in bfloat16 or wider, within the bound.
No kernel may reach another device: no remote copies, remote signals or barrier semaphores. Data moves between devices by JAX's collectives and lax.ppermute only.
A program may use at most 128 MiB of HBM per device.

v0:
```python
import jax
import jax.numpy as jnp
from jax import lax
from jax.sharding import PartitionSpec as P


def project_rows(projector, data):
    return lax.dot_general(
        projector, data, (((0,), (1,)), ((), ())), preferred_element_type=jnp.float32
    )


def example_terms(left, right, weights):
    masked = left[None, :, :] * weights[:, None, :]
    outer = jnp.einsum("eit,jt->eij", masked, right, precision=lax.Precision.HIGHEST)
    return outer.reshape(outer.shape[0], -1)


def body(
    gate_pre,
    up_val,
    layer_in,
    out_grad,
    down_weight,
    down_in_proj,
    down_out_proj,
    up_in_proj,
    up_out_proj,
    counts,
    assignment,
    queries,
):
    ex_dev, seq_len, width_ff = gate_pre.shape
    tok_rows = ex_dev * seq_len
    act = jax.nn.silu(gate_pre.reshape(tok_rows, width_ff).astype(jnp.float32))
    hidden = (act * up_val.reshape(tok_rows, width_ff).astype(jnp.float32)).astype(jnp.bfloat16)
    grads = out_grad.reshape(tok_rows, -1)
    inputs = layer_in.reshape(tok_rows, -1)
    back = lax.dot_general(
        grads,
        lax.all_gather(down_weight, "dp", axis=1, tiled=True),
        (((1,), (1,)), ((), ())),
        preferred_element_type=jnp.float32,
    )
    delta = (back * act).astype(jnp.bfloat16)
    pieces = [
        project_rows(down_in_proj, hidden),
        project_rows(up_in_proj, inputs),
        project_rows(up_out_proj, delta),
    ]
    local_out = project_rows(down_out_proj, grads)
    partial_value = jnp.stack(pieces)
    summed = lax.psum(partial_value, "tensor")
    positions = jnp.arange(tok_rows, dtype=jnp.int32)
    owner = positions // seq_len
    inside = positions % seq_len
    slots = jnp.arange(ex_dev, dtype=jnp.int32)
    weights = ((owner[None, :] == slots[:, None]) & (inside[None, :] < counts[:, None])).astype(
        jnp.float32
    )
    first = example_terms(summed[0], local_out, weights)
    second = example_terms(summed[1], summed[2], weights)
    mine = jnp.stack([first, second])
    gathered, ids = (
        lax.all_gather(mine, "dp", axis=1, tiled=True),
        lax.all_gather(assignment, "dp", axis=0, tiled=True),
    )
    total = ids.shape[0]
    labels = jnp.arange(total, dtype=jnp.int32)
    placing = (ids[:, None] == labels[None, :]).astype(jnp.float32)
    byid = jnp.einsum("sn,msk->mnk", placing, gathered, precision=lax.Precision.HIGHEST)
    gram = jnp.einsum("mak,mbk->mab", byid, byid, precision=lax.Precision.HIGHEST) / float(
        byid.shape[2]
    )
    norm = jnp.sqrt(jnp.diagonal(gram, axis1=1, axis2=2) + 1e-06)
    picking = (queries[:, None] == labels[None, :]).astype(jnp.float32)
    chosen = jnp.einsum("qa,mab->mqb", picking, gram, precision=lax.Precision.HIGHEST)
    chosen_norm = jnp.einsum("qa,ma->mq", picking, norm, precision=lax.Precision.HIGHEST)
    scores = chosen / (chosen_norm[:, :, None] * norm[:, None, :])
    return (mine, gram, scores)


def solution(mesh):
    return jax.shard_map(
        body,
        mesh=mesh,
        in_specs=(
            P("dp", None, "tensor"),
            P("dp", None, "tensor"),
            P("dp", None, "tensor"),
            P("dp", None, None),
            P("tensor", "dp"),
            P("tensor", None),
            P(),
            P("tensor", None),
            P("tensor", None),
            P("dp"),
            P("dp"),
            P(),
        ),
        out_specs=(P(None, "dp", None), P(), P()),
        check_vma=False,
    )
```

profile of v0, /device:TPU:1, one launch (start us, length us, event | category | flops | bytes accessed | tf_op | source)
XLA Modules:
  0.0 282.8 jit_solution(3797809916032282674)
XLA Ops:
  7.2 0.7 all-gather.3.cloned.1.call-update
  8.0 0.4 copy-done
  8.4 1.4 convolution_bitcast_fusion.1
  9.8 3.9 %convert_multiply_fusion = f32[1024,1792]{1,0:T(8,128)S(1)} fusion(bf16[2,512,1792]{2,1,0:T(8,128)(2,1)} %param.12), kind=kLoop, calls=%fused_computation.1 | loop fusion | flops 9175040 | bytes 11010048 | tf_op jit(solution)/shard_map/jit(silu)/mul | solution.py:35
  13.8 2.9 %copy-done.1 = f32[1024,1792]{1,0:T(8,128)} copy-done((f32[1024,1792]{1,0:T(8,128)}, f32[1024,1792]{1,0:T(8,128)S(1)}, u32[]{:S(2)}) %copy-start.1) | copy-done | bytes 7340056
  16.7 1.2 fusion.7
  17.9 104.3 %all-gather.3.cloned.1.call-done = bf16[1792,4096]{1,0:T(8,128)(2,1)} async-done(((bf16[1792,256]{1,0:T(8,128)(2,1)}), bf16[1792,4096]{1,0:T(8,128)(2,1)}) %all-gather.3.cloned.1.call-update) | async-done | bytes 14680080 | tf_op jit(solution)/shard_map/all_gather | solution.py:41
  122.3 25.3 %fusion.10 = f32[1,64,1024]{2,1,0:T(8,128)S(1)} fusion(bf16[1792,64]{0,1:T(8,128)(2,1)S(1)} %copy-done.7, f32[1024,1792]{1,0:T(8,128)} %copy-done.1, bf16[1024,4096]{1,0:T(8,128)(2,1)} %bitcast.55, bf16[1792,4096]{1,0:T(8,128)(2,1)} %all-gather.3.cloned.1.call-done), kind=kOutput, calls=%fused_computation.14 | convolution fusion | flops 15270936576 | bytes 30900224 | tf_op jit(solution)/shard_map/dot_general | solution.py:8
  147.6 1.0 pad_maximum_fusion
  148.9 6.0 %convolution_bitcast_fusion = f32[64,1024,1]{1,0,2:T(8,128)S(1)} fusion(bf16[4096,64]{0,1:T(8,128)(2,1)S(1)} %copy-done.3, bf16[1024,4096]{1,0:T(8,128)(2,1)} %bitcast.56), kind=kOutput, calls=%fused_computation.12 | convolution fusion | flops 536870912 | bytes 9175040 | tf_op jit(solution)/shard_map/dot_general | solution.py:8
  155.0 61.7 %all-reduce.3.cloned.1.call-done = f32[3,64,1024]{2,1,0:T(8,128)} async-done(((f32[3,64,1024]{2,1,0:T(8,128)}), f32[3,64,1024]{2,1,0:T(8,128)}) %all-reduce.3.cloned.1.call-update) | async-done | bytes 786448 | tf_op jit(solution)/shard_map/psum | solution.py:53
  216.7 1.1 slice_bitcast_fusion.3
  217.8 1.5 fusion.14
  219.4 0.6 fusion.16
  220.1 0.7 pad_maximum_fusion.1
  220.8 0.6 dynamic-slice
  222.3 16.2 %all-reduce = s32[32]{0:T(128)S(1)} all-reduce(s32[32]{0:T(128)S(1)} %dynamic-update-slice), channel_id=1, replica_groups=mesh['dp'=16,'tensor'=8] {'dp'}, use_global_device_ids=true, to_apply=%add | all-reduce | flops 32 | bytes 256
  238.5 1.5 copy.21
  240.0 30.6 %all-gather.5.cloned.1.call-done = f32[2,32,4096]{2,0,1:T(2,128)} async-done(((f32[2,2,4096]{2,0,1:T(2,128)}), f32[2,32,4096]{2,0,1:T(2,128)}) %all-gather.5.cloned.1.call-update) | async-done | bytes 1048592 | tf_op jit(solution)/shard_map/all_gather | solution.py:65
  270.6 2.5 fusion.12
  273.1 1.1 convolution_multiply_fusion
  274.2 0.3 copy.19
  274.5 0.7 gather_fusion
  275.5 0.8 fusion.11
  (35 shorter events, 1.2 us)
Async XLA Ops:
  7.2 1.2 copy-start
  7.2 9.5 %copy-start.4 = (bf16[1792,64]{0,1:T(8,128)(2,1)S(1)}, bf16[1792,64]{0,1:T(8,128)(2,1)}, u32[]{:S(2)}) copy-start(bf16[1792,64]{0,1:T(8,128)(2,1)} %param.17) | copy-start | bytes 688132
  7.2 115.1 %all-gather.3.cloned.1.call-start = ((), (), s32[]{:S(2)}) async-start(), calls=%async_computation | async-start | bytes 15597568 | tf_op jit(solution)/shard_map/all_gather | solution.py:41
  7.9 208.8 %all-reduce.3.cloned.1.call-start = ((), (), s32[]{:S(2)}) async-start(), calls=%async_computation.1 | async-start | bytes 1572864 | tf_op jit(solution)/shard_map/psum | solution.py:53
  8.4 8.3 %copy-start.2 = (bf16[2,512,1792]{2,1,0:T(8,128)(2,1)S(1)}, bf16[2,512,1792]{2,1,0:T(8,128)(2,1)}, u32[]{:S(2)}) copy-start(bf16[2,512,1792]{2,1,0:T(8,128)(2,1)} %param.13) | copy-start | bytes 11010052
  13.8 2.9 %copy-start.1 = (f32[1024,1792]{1,0:T(8,128)}, f32[1024,1792]{1,0:T(8,128)S(1)}, u32[]{:S(2)}) copy-start(f32[1024,1792]{1,0:T(8,128)S(1)} %convert_multiply_fusion) | copy-start | bytes 22020100
  13.8 108.5 %copy-start.7 = (bf16[1792,64]{0,1:T(8,128)(2,1)S(1)}, bf16[1792,64]{0,1:T(8,128)(2,1)}, u32[]{:S(2)}) copy-start(bf16[1792,64]{0,1:T(8,128)(2,1)} %param.20) | copy-start | bytes 688132
  122.3 26.6 %copy-start.6 = (s32[2]{0:T(128)S(1)}, s32[2]{0:T(128)}, u32[]{:S(2)}) copy-start(s32[2]{0:T(128)} %param.21) | copy-start | bytes 28
  122.3 26.7 %copy-start.3 = (bf16[4096,64]{0,1:T(8,128)(2,1)S(1)}, bf16[4096,64]{0,1:T(8,128)(2,1)}, u32[]{:S(2)}) copy-start(bf16[4096,64]{0,1:T(8,128)(2,1)} %param.18) | copy-start | bytes 1572868
  147.6 73.2 %copy-start.10 = (u32[128]{0:T(128)S(1)}, u32[128]{0:T(128)}, u32[]{:S(2)}) copy-start(u32[128]{0:T(128)} %constant.65) | copy-start | bytes 1540
  147.6 74.4 %copy-start.8 = (s32[2]{0:T(128)S(1)}, s32[2]{0:T(128)}, u32[]{:S(2)}) copy-start(s32[2]{0:T(128)} %param.22) | copy-start | bytes 28
  148.6 122.0 %all-gather.5.cloned.1.call-start = ((), (), s32[]{:S(2)}) async-start(), calls=%async_computation.2 | async-start | bytes 1114112 | tf_op jit(solution)/shard_map/all_gather | solution.py:65
  148.9 126.3 %copy-start.9 = (s32[8]{0:T(128)S(1)}, s32[8]{0:T(128)}, u32[]{:S(2)}) copy-start(s32[8]{0:T(128)} %param.23) | copy-start | bytes 100
  274.2 2.1 copy-start.5
Sparse Core Ops, SparseCore 0:
  10.3 111.9 all-gather.2
  148.7 67.9 all-reduce.2
  220.9 49.6 all-gather.4
where the time goes:
time: 283 us
  waiting for transfers between devices  197 us (70%)
  matrix products  40.6 us (14%)
  blocking collectives  16.2 us (6%)
  between operations  14.6 us (5%)
  local copies, waits for them, and re-layouts  8.05 us (3%)
  other arithmetic  5.7 us (2%)
    all_gather x1, waiting for transfers between devices, body(): lax.all_gather(down_weight, 'dp', axis=1, tiled=True)  104 us
    psum x1, waiting for transfers between devices, body(): summed = lax.psum(partial_value, 'tensor')  61.7 us
    dot_general x4, matrix products, project_rows(): lax.dot_general(projector, data, (((0,), (1,)), ((), ())), preferred_elem...  34 us
    all_gather x1, waiting for transfers between devices, body(): lax.all_gather(mine, 'dp', axis=1, tiled=True)  30.6 us
    unnamed x1, blocking collectives  16.2 us
    unnamed x26, local copies, waits for them, and re-layouts  5.73 us
  transfers between devices with their start and end apart: 3, of which 3 were waited for; matrix products, arithmetic and copies ran while one was open for 5% of the time, Pallas kernels for 0%

commit v1 on v0

v1 whole, which is shorter than its diff:
```python
import functools

import jax
import jax.numpy as jnp
from jax import lax
from jax.experimental import pallas as pl
from jax.experimental.pallas import tpu as pltpu
from jax.sharding import PartitionSpec as P

AXES = ("dp", "tensor")
BF16, F32 = jnp.bfloat16, jnp.float32
HIGHEST = lax.Precision.HIGHEST
TILE = 512
EARLY_TILE = 256
NT = (((1,), (1,)), ((), ()))
CHUNKS = ((0, 896),)
SMALL = pl.CostEstimate(flops=1000, bytes_accessed=1000, transcendentals=0)


def coords(i):
    dp, tensor = divmod(i, 8)
    x_hi, rest = divmod(dp, 8)
    y, core = divmod(rest, 2)
    x_lo, z = divmod(tensor, 4)
    return x_hi * 2 + x_lo, y, z, core


def index(x, y, z, core):
    x_hi, x_lo = divmod(x % 4, 2)
    return ((x_hi * 4 + y % 4) * 2 + core) * 8 + x_lo * 4 + z % 4


def pair(v, phase):
    return (v ^ 1) if phase == 0 else (v + (1 if v % 2 else -1)) % 4


def moved(value, to):
    return lax.ppermute(value, AXES, [(i, index(*to(*coords(i)))) for i in range(128)])


def swap_core(v):
    return moved(v, lambda x, y, z, c: (x, y, z, 1 - c))


def swap_y(v, step):
    return moved(v, lambda x, y, z, c: (x, pair(y, step ^ c), z, c))


def swap_z(v, step):
    return moved(v, lambda x, y, z, c: (x, y, pair(z, step ^ c), c))


def swap_x(v, phase):
    return moved(v, lambda x, y, z, c: (pair(x, phase), y, z, c))


def swap_x_far(v):
    return moved(v, lambda x, y, z, c: (x + 2, y, z, c))


def silu(v):
    half = 0.5 * v
    return half + half * jnp.tanh(half)


def after(value, *others):
    def nothing(*refs):
        pass

    anywhere = pl.BlockSpec(memory_space=pl.ANY)
    return pl.pallas_call(
        nothing,
        out_shape=jax.ShapeDtypeStruct(value.shape, value.dtype),
        in_specs=[anywhere] * (1 + len(others)),
        out_specs=anywhere,
        input_output_aliases={0: 0},
        name="after",
    )(value, *others)


def rows_kernel(counts, gate, up, grad, inp, din_t, dout_t, uin_t, _, out):
    i = pl.program_id(0)
    per = 512 // EARLY_TILE
    act = silu(gate[...].astype(F32))
    hidden = (act * up[...].astype(F32)).astype(BF16)
    hid_t = lax.dot_general(din_t[...], hidden, NT, preferred_element_type=F32)
    in_t = lax.dot_general(uin_t[...], inp[...], NT, preferred_element_type=F32)
    out_rows = lax.dot_general(grad[...], dout_t[...], NT, preferred_element_type=F32)
    pos = (i % per) * EARLY_TILE + lax.broadcasted_iota(jnp.int32, (64, EARLY_TILE), 1)
    live = (pos < counts[i // per]).astype(F32)
    first = jnp.dot(hid_t * live, out_rows, precision=HIGHEST, preferred_element_type=F32)
    packed = jnp.concatenate([first[:32], first[32:]], axis=1)
    here = pl.ds(pl.multiple_of((i // per) * 32, 32), 32)

    @pl.when(i % per == 0)
    def _():
        out[here, 1024:] = packed

    @pl.when(i % per != 0)
    def _():
        out[here, 1024:] += packed

    out[:, pl.ds(pl.multiple_of(i * EARLY_TILE, EARLY_TILE), EARLY_TILE)] = in_t * live


def projected_rows(counts, gate, up, grad, inp, din_t, dout_t, uin_t, later_than):
    tokens, width = gate.shape
    row = lambda n: pl.BlockSpec((EARLY_TILE, n), lambda i, s: (i, 0))
    full = lambda a: pl.BlockSpec(a.shape, lambda i, s: (0, 0))
    return pl.pallas_call(
        rows_kernel,
        out_shape=jax.ShapeDtypeStruct((64, tokens + 128), F32),
        grid_spec=pltpu.PrefetchScalarGridSpec(
            num_scalar_prefetch=1,
            grid=(tokens // EARLY_TILE,),
            in_specs=[row(width), row(width), row(grad.shape[1]), row(inp.shape[1]), full(din_t), full(dout_t), full(uin_t), pl.BlockSpec(memory_space=pl.ANY)],
            out_specs=pl.BlockSpec((64, tokens + 128), lambda i, s: (0, 0)),
        ),
        compiler_params=pltpu.CompilerParams(vmem_limit_bytes=56 * 2**20),
        cost_estimate=SMALL,
        name="early_rows",
    )(counts, gate, up, grad, inp, din_t, dout_t, uin_t, later_than)


def back_kernel(n, has_acc, last, has_first, lo, cols, *refs):
    i = pl.program_id(0)
    half = pl.num_programs(0) // 2
    refs = list(refs)
    acc_ref = refs.pop(0) if has_acc else None
    blocks, rest = refs[: 3 * n], refs[3 * n :]
    out = rest[-1]

    def run(side):
        acc = acc_ref[...] if has_acc else None
        for p in range(n):
            term = lax.dot_general(blocks[3 * p + side][...], blocks[3 * p + 2][...], NT, preferred_element_type=F32)
            acc = term if acc is None else acc + term
        if not last:
            out[...] = acc
            return
        width = acc.shape[1]
        gate = rest[side][:, lo : lo + width]
        delta = (acc * silu(gate.astype(F32))).astype(BF16)
        del_rows = lax.dot_general(delta, rest[2][:, lo : lo + width], NT, preferred_element_type=F32)
        second = jnp.dot(rest[3 + side][...], del_rows, precision=HIGHEST, preferred_element_type=F32)
        packed = jnp.concatenate([second[:32], second[32:]], axis=1)

        @pl.when(i % (512 // TILE) == 0)
        def _():
            out[0] = packed + rest[5][0] if has_first else packed

        @pl.when(i % (512 // TILE) != 0)
        def _():
            out[0] += packed

    @pl.when(i < half)
    def _():
        run(0)

    @pl.when(i >= half)
    def _():
        run(1)


def back_step(cols, acc, pieces, grads, tail=None, lo=0):
    mine, theirs = grads
    tokens = mine.shape[0]
    steps = tokens // TILE
    width = pieces[0][0].shape[0]
    feats = pieces[0][0].shape[1]
    own_row = lambda i: jnp.minimum(i, steps - 1)
    other_row = lambda i: jnp.maximum(i - steps, 0)
    args, specs = [], []
    acc_spec = pl.BlockSpec((TILE, width), lambda i, s: (i, 0))
    if acc is not None:
        args.append(acc)
        specs.append(acc_spec)
    for weight, k in pieces:
        args += [mine, theirs, weight]
        specs += [
            pl.BlockSpec((TILE, feats), lambda i, s, k=k: (own_row(i), s[k])),
            pl.BlockSpec((TILE, feats), lambda i, s, k=k: (other_row(i), s[k])),
            pl.BlockSpec((width, feats), lambda i, s: (0, 0)),
        ]
    n = len(pieces)
    if tail is None:
        out_shape = jax.ShapeDtypeStruct((2 * tokens, width), F32)
        out_spec = acc_spec
    else:
        gate_mine, gate_theirs, proj, rows_mine, rows_theirs, first = tail
        hid = gate_mine.shape[1] // 2
        args += [gate_mine, gate_theirs, proj, rows_mine, rows_theirs]
        specs += [
            pl.BlockSpec((TILE, hid), lambda i, s: (own_row(i), s[8])),
            pl.BlockSpec((TILE, hid), lambda i, s: (other_row(i), s[8])),
            pl.BlockSpec((64, hid), lambda i, s: (0, s[8])),
            pl.BlockSpec((64, TILE), lambda i, s: (0, own_row(i))),
            pl.BlockSpec((64, TILE), lambda i, s: (0, other_row(i))),
        ]
        out_spec = pl.BlockSpec((1, 32, 128), lambda i, s: ((i // (512 // TILE) + 2 * s[8]) % 4, 0, 0))
        if first is not None:
            args.append(first)
            specs.append(out_spec)
        out_shape = jax.ShapeDtypeStruct((4, 32, 128), F32)
    return pl.pallas_call(
        functools.partial(back_kernel, n, acc is not None, tail is not None, tail is not None and tail[5] is not None, lo),
        out_shape=out_shape,
        grid_spec=pltpu.PrefetchScalarGridSpec(
            num_scalar_prefetch=1, grid=(2 * steps,), in_specs=specs, out_specs=out_spec
        ),
        compiler_params=pltpu.CompilerParams(vmem_limit_bytes=56 * 2**20),
        cost_estimate=SMALL,
        name="back_last" if tail is not None else "back_part",
    )(cols, *args)


def body(
    gate_pre, up_val, layer_in, out_grad, down_weight, down_in_proj, down_out_proj,
    up_in_proj, up_out_proj, counts, assignment, queries,
):
    ex_dev, seq_len, width_ff = gate_pre.shape
    tokens = ex_dev * seq_len
    half = width_ff // 2
    dp = lax.axis_index("dp")
    core = dp % 2
    y = (dp // 2) % 4
    x_hi = dp // 8

    def partner(v, step):
        odd = (step ^ core) == 0
        return jnp.where(odd, v ^ 1, (v + jnp.where(v % 2 == 1, 1, 3)) % 4)

    y1, y2 = partner(y, 0), partner(y, 1)
    y12 = partner(y2, 0)
    here, there = x_hi * 4, (1 - x_hi) * 4
    cols = jnp.stack(
        [here + y, here + y1, here + y2, there + y, here + y12, there + y2, there + y1, there + y12, core]
    ).astype(jnp.int32)

    gate = gate_pre.reshape(tokens, width_ff)
    up = up_val.reshape(tokens, width_ff)
    grads = out_grad.reshape(tokens, -1)
    inputs = layer_in.reshape(tokens, -1)

    weight_other = swap_core(down_weight)
    ids_other = swap_core(assignment)
    is_even = core == 0
    even = jnp.concatenate([down_weight[:half], weight_other[:half]], axis=1)
    odd = jnp.concatenate([weight_other[half:], down_weight[half:]], axis=1)
    h = jnp.where(is_even, even, odd)

    h_x = swap_x_far(h)
    h_y = swap_y(h, 0)
    h_y2 = swap_y(h, 1)
    gate_other = swap_core(gate)
    grads_other = swap_core(grads)
    both = (grads, grads_other)

    early = projected_rows(
        counts, gate, up, grads, inputs, down_in_proj.T, down_out_proj.T, up_in_proj.T, h
    )
    h_y, h_x, h_y2 = after(h_y, early), after(h_x, early), after(h_y2, early)
    h_xy = swap_x_far(h_y)
    h_yy = swap_y(h_y, 1)
    h_xy2 = swap_y(h_x, 1)
    rows = early + swap_z(early, 0)
    rows_second = swap_z(rows, 1)

    acc = back_step(cols, None, [(h, 0), (h_y, 1), (h_y2, 2), (h_x, 3)], both)
    h_xy = after(h_xy, acc)
    h_xyy = swap_y(h_xy, 1)
    rows = rows + after(rows_second, acc)
    rows = rows + swap_x(rows, 0)
    rows_other = swap_core(rows)
    acc = back_step(cols, acc, [(h_yy, 4), (h_xy2, 5), (h_xy, 6)], both)
    tail = (gate, gate_other, up_out_proj.T, after(rows, acc), rows_other, None)
    second = back_step(cols, acc, [(h_xyy, 7)], both, tail, 0)

    second_other = swap_core(second)
    mine = lax.dynamic_slice_in_dim(second + second_other, core * 16, 16, 1)
    mine = mine + swap_z(mine, 0)
    mine = mine + swap_z(mine, 1)
    mine = mine + swap_x(mine, 0)

    first = rows[:, tokens:].reshape(ex_dev, 32, 128)
    first_other = rows_other[:, tokens:].reshape(ex_dev, 32, 128)
    first_all = jnp.where(is_even, jnp.concatenate([first, first_other]), jnp.concatenate([first_other, first]))
    first_half = lax.dynamic_slice_in_dim(first_all, core * 16, 16, 1)
    ids = jnp.where(is_even, jnp.concatenate([assignment, ids_other]), jnp.concatenate([ids_other, assignment]))
    ids_block = jnp.broadcast_to(jnp.pad(ids, (0, 12))[None, :, None], (1, 16, 128)).astype(BF16)
    load = jnp.concatenate([first_half.astype(BF16), mine.astype(BF16), ids_block])
    load = jnp.stack([load, swap_y(load, 0)])
    load = jnp.concatenate([load, swap_y(load, 1)])
    load = jnp.concatenate([load, swap_x(load, 1)])

    mine_other = swap_core(mine)
    own = lax.dynamic_slice_in_dim(mine, core * ex_dev, ex_dev, 0)
    own_other = lax.dynamic_slice_in_dim(mine_other, core * ex_dev, ex_dev, 0)
    own_rows = jnp.where(is_even, jnp.concatenate([own, own_other], 1), jnp.concatenate([own_other, own], 1))
    out = jnp.stack([first, own_rows]).reshape(2, ex_dev, 32, 2, 64)
    projected = out.transpose(0, 1, 3, 2, 4).reshape(2, ex_dev, 4096)

    flat = load[:, :8].reshape(8, 2, 4, 2048).transpose(1, 0, 2, 3).reshape(2, 32, 2048)
    partial = jnp.einsum("mak,mbk->mab", flat, flat, preferred_element_type=F32)
    slot_ids = load[:, 8, :4, 0].reshape(32).astype(jnp.int32)
    labels = jnp.arange(32, dtype=jnp.int32)
    placing = (slot_ids[None, :] == labels[:, None]).astype(F32)
    by_id = jnp.einsum("as,mst,bt->mab", placing, partial, placing, precision=HIGHEST)
    gram = (by_id + swap_core(by_id)) / 4096.0
    norm = jnp.sqrt(jnp.diagonal(gram, axis1=1, axis2=2) + 1e-06)
    picking = (queries[:, None] == labels[None, :]).astype(F32)
    chosen = jnp.einsum("qa,mab->mqb", picking, gram, precision=HIGHEST)
    chosen_norm = jnp.einsum("qa,ma->mq", picking, norm, precision=HIGHEST)
    scores = chosen / (chosen_norm[:, :, None] * norm[:, None, :])
    return projected, gram, scores


def solution(mesh):
    return jax.shard_map(
        body,
        mesh=mesh,
        in_specs=(
            P("dp", None, "tensor"),
            P("dp", None, "tensor"),
            P("dp", None, "tensor"),
            P("dp", None, None),
            P("tensor", "dp"),
            P("tensor", None),
            P(),
            P("tensor", None),
            P("tensor", None),
            P("dp"),
            P("dp"),
            P(),
        ),
        out_specs=(P(None, "dp", None), P(), P()),
        check_vma=False,
    )
```

time: 283 us -> 144 us (0.51)
  waiting for transfers between devices: 197 us -> 33.9 us
  Pallas kernels: 0 us -> 50.1 us
  starting transfers between devices: 0.3 us -> 43.8 us
  matrix products: 40.6 us -> 1.5 us
  blocking collectives: 16.2 us -> 0 us
  between operations: 14.6 us -> 0.94 us
  other arithmetic: 5.7 us -> 2.62 us
    all_gather x2 -> x0, waiting for transfers between devices: 135 us -> none  [the longest x1 104 us: body(): lax.all_gather(down_weight, 'dp', axis=1, tiled=True)]
    psum x1 -> x0, waiting for transfers between devices: 61.7 us -> none  [body(): summed = lax.psum(partial_value, 'tensor')]
    pallas_call x0 -> x10, Pallas kernels: none -> 50.1 us  [the longest x3 39.6 us: back_step(): pl.pallas_call(functools.partial(back_kernel, n, acc is not None, tail is...]
    ppermute x0 -> x24, starting transfers between devices: none -> 43.8 us  [moved(): lax.ppermute(value, AXES, [(i, index(*to(*coords(i)))) for i in range(128)])]
    dot_general x10 -> x5, matrix products: 40.6 us -> 1.5 us  [the longest x1 0.82 us: body(): chosen = jnp.einsum('qa,mab->mqb', picking, gram, precision=HIGHEST)]
    ppermute x0 -> x24, waiting for transfers between devices: none -> 33.9 us  [moved(): lax.ppermute(value, AXES, [(i, index(*to(*coords(i)))) for i in range(128)])]
    unnamed x1 -> x0, blocking collectives: 16.2 us -> none
    mul x1 -> x0, other arithmetic: 3.95 us -> none  [body(): act = jax.nn.silu(gate_pre.reshape(tok_rows, width_ff).astype(jnp.float32))]
  transfers between devices with their start and end apart: 3 -> 24, of which waited for: 3 -> 12; matrix products, arithmetic and copies ran while one was open for 5% -> 4% of each run, Pallas kernels for 0% -> 28%
where the time goes in v1:
time: 144 us; the launch traced here: 143 us
  Pallas kernels  50.1 us (35%)
  starting transfers between devices  43.8 us (30%)
  waiting for transfers between devices  33.9 us (24%)
  local copies, waits for them, and re-layouts  10.5 us (7%)
  other arithmetic  2.62 us (2%)
  matrix products  1.5 us (1%)
    ppermute x24, starting transfers between devices, moved(): lax.ppermute(value, AXES, [(i, index(*to(*coords(i)))) for i in range(128)])  43.8 us
    pallas_call x3, Pallas kernels, back_step(): pl.pallas_call(functools.partial(back_kernel, n, acc is not None, tail is...  39.6 us
    ppermute x24, waiting for transfers between devices, moved(): lax.ppermute(value, AXES, [(i, index(*to(*coords(i)))) for i in range(128)])  33.9 us
    pallas_call x1, Pallas kernels, projected_rows(): pl.pallas_call(rows_kernel, out_shape=jax.ShapeDtypeStruct((64, tokens +...  10.5 us
    unnamed x26, local copies, waits for them, and re-layouts  5.23 us
  transfers between devices with their start and end apart: 24, of which 12 were waited for; matrix products, arithmetic and copies ran while one was open for 4% of the time, Pallas kernels for 28%

profile of v1, /device:TPU:1, one launch (start us, length us, event | category | flops | bytes accessed | tf_op | source)
XLA Modules:
  0.0 143.3 jit_solution(17404870991415178733)
XLA Ops:
  0.6 1.5 %collective-permute-start.3 = (bf16[1024,4096]{1,0:T(8,128)(2,1)}, bf16[1024,4096]{1,0:T(8,128)(2,1)}, u32[]{:S(2)}, u32[]{:S(2)}) collective-permute-start(bf16[1024,4096]{1,0:T(8,128)(2,1)} %bitcast.49), channel_id=1, source_target_pairs={{0,8},{1,9},{2,10},{3,11},{4,12},{5,13},{6,14},{7,15},{8,0},{9,1},... | collective-permute-start | bytes 25165832 | tf_op jit(solution)/shard_map/ppermute | solution.py:38
  3.9 6.8 %collective-permute-done = bf16[1792,256]{1,0:T(8,128)(2,1)S(1)} collective-permute-done((bf16[1792,256]{1,0:T(8,128)(2,1)}, bf16[1792,256]{1,0:T(8,128)(2,1)S(1)}, u32[]{:S(2)}, u32[]{:S(2)}) %collective-permute-start) | collective-permute-done | bytes 917536 | tf_op jit(solution)/shard_map/ppermute | solution.py:38
  11.0 2.9 %collective-permute-start.4 = (bf16[896,512]{1,0:T(8,128)(2,1)S(1)}, bf16[896,512]{1,0:T(8,128)(2,1)S(1)}, u32[]{:S(2)}, u32[]{:S(2)}) collective-permute-start(bf16[896,512]{1,0:T(8,128)(2,1)S(1)} %maximum_select_fusion._.refs_2_), channel_id=1, source_target_pairs={{0,16},{1,17},{2,18},{3,19},{4,20},{5,21},{6,22},{7,23},{8,56},{9,... | collective-permute-start | bytes 2752520 | tf_op jit(solution)/shard_map/ppermute | solution.py:38
  13.9 2.7 %collective-permute-start.6 = (bf16[896,512]{1,0:T(8,128)(2,1)S(1)}, bf16[896,512]{1,0:T(8,128)(2,1)}, u32[]{:S(2)}, u32[]{:S(2)}) collective-permute-start(bf16[896,512]{1,0:T(8,128)(2,1)S(1)} %maximum_select_fusion._.refs_2_), channel_id=1, source_target_pairs={{0,64},{1,65},{2,66},{3,67},{4,68},{5,69},{6,70},{7,71},{8,72},{9,... | collective-permute-start | bytes 2752520 | tf_op jit(solution)/shard_map/ppermute | solution.py:38
  16.6 10.5 %early_rows.1.refs_1_ = f32[64,1152]{1,0:T(8,128)} custom-call(s32[2]{0:T(128)} %counts.1, bf16[1024,1792]{1,0:T(8,128)(2,1)} %bitcast.60, bf16[1024,1792]{1,0:T(8,128)(2,1)} %bitcast.62, bf16[1024,4096]{1,0:T(8,128)(2,1)} %bitcast.50, bf16[1024,512]{1,0:T(8,128)(2,1)} %bitcast.63, bf16[64,1792]{1,0:T(8,128)(2,1)} %bitcast.71, bf16[64,4096]{1,0:T(8,128)(2,1)} %bitcast.68, ...), custom_call_target="tpu_custom_call" | custom-call | flops 1000 | bytes 1000 | tf_op jit(solution)/shard_map/early_rows/pallas_call | solution.py:110
  27.1 2.6 %collective-permute-done.4.refs_0_ = bf16[896,512]{1,0:T(8,128)(2,1)S(1)} collective-permute-done((bf16[896,512]{1,0:T(8,128)(2,1)S(1)}, bf16[896,512]{1,0:T(8,128)(2,1)S(1)}, u32[]{:S(2)}, u32[]{:S(2)}) %collective-permute-start.4) | collective-permute-done | bytes 917536 | tf_op jit(solution)/shard_map/ppermute | solution.py:38
  30.6 5.2 %collective-permute-start.10 = (bf16[896,512]{1,0:T(8,128)(2,1)}, bf16[896,512]{1,0:T(8,128)(2,1)S(1)}, u32[]{:S(2)}, u32[]{:S(2)}) collective-permute-start(bf16[896,512]{1,0:T(8,128)(2,1)} %after.6.refs_5_), channel_id=1, source_target_pairs={{0,64},{1,65},{2,66},{3,67},{4,68},{5,69},{6,70},{7,71},{8,72},{9,... | collective-permute-start | bytes 2752520 | tf_op jit(solution)/shard_map/ppermute | solution.py:38
  37.0 3.8 %collective-permute-start.1 = (f32[64,1152]{1,0:T(8,128)}, f32[64,1152]{1,0:T(8,128)S(1)}, u32[]{:S(2)}, u32[]{:S(2)}) collective-permute-start(f32[64,1152]{1,0:T(8,128)} %early_rows.1.refs_1_), channel_id=1, source_target_pairs={{0,1},{1,0},{2,3},{3,2},{4,5},{5,4},{6,7},{7,6},{8,11},{9,10},{10,... | collective-permute-start | bytes 884744 | tf_op jit(solution)/shard_map/ppermute | solution.py:38
  42.8 15.1 %back_part.2.refs_1_.refs_0_ = f32[2048,896]{1,0:T(8,128)} custom-call(s32[9]{0:T(128)} %stack.54.cols, bf16[1024,4096]{1,0:T(8,128)(2,1)} %bitcast.51, bf16[1024,4096]{1,0:T(8,128)(2,1)} %collective-permute-done.3.refs_1_.refs_4_.refs_7_.refs_10_.refs_2_.refs_5_.refs_8_, bf16[896,512]{1,0:T(8,128)(2,1)} %copy-done, bf16[1024,4096]{1,0:T(8,128)(2,1)} %bitcast.52, ...), custom_call_target="tpu_custom_call" | custom-call | flops 1000 | bytes 1000 | tf_op jit(solution)/shard_map/back_part/pallas_call | solution.py:205
  59.3 5.9 %collective-permute-done.2.refs_0_ = f32[64,1152]{1,0:T(8,128)S(1)} collective-permute-done((f32[64,1152]{1,0:T(8,128)S(1)}, f32[64,1152]{1,0:T(8,128)S(1)}, u32[]{:S(2)}, u32[]{:S(2)}) %collective-permute-start.2) | collective-permute-done | bytes 294944 | tf_op jit(solution)/shard_map/ppermute | solution.py:38
  66.9 1.9 %collective-permute-start.7 = (f32[64,1152]{1,0:T(8,128)S(1)}, f32[64,1152]{1,0:T(8,128)S(1)}, u32[]{:S(2)}, u32[]{:S(2)}) collective-permute-start(f32[64,1152]{1,0:T(8,128)S(1)} %add.119), channel_id=1, source_target_pairs={{0,4},{1,5},{2,6},{3,7},{4,0},{5,1},{6,2},{7,3},{8,12},{9,13},{10,... | collective-permute-start | bytes 884744 | tf_op jit(solution)/shard_map/ppermute | solution.py:38
  68.7 4.4 %collective-permute-done.7 = f32[64,1152]{1,0:T(8,128)S(1)} collective-permute-done((f32[64,1152]{1,0:T(8,128)S(1)}, f32[64,1152]{1,0:T(8,128)S(1)}, u32[]{:S(2)}, u32[]{:S(2)}) %collective-permute-start.7) | collective-permute-done | bytes 294944 | tf_op jit(solution)/shard_map/ppermute | solution.py:38
  73.2 6.8 %collective-permute-start.13 = (f32[64,1152]{1,0:T(8,128)S(1)}, f32[64,1152]{1,0:T(8,128)S(1)}, u32[]{:S(2)}, u32[]{:S(2)}) collective-permute-start(f32[64,1152]{1,0:T(8,128)S(1)} %add.120.refs_0_), channel_id=1, source_target_pairs={{0,8},{1,9},{2,10},{3,11},{4,12},{5,13},{6,14},{7,15},{8,0},{9,1},... | collective-permute-start | bytes 884744 | tf_op jit(solution)/shard_map/ppermute | solution.py:38
  80.9 13.9 %back_part.3.refs_1_.refs_0_ = f32[2048,896]{1,0:T(8,128)} custom-call(s32[9]{0:T(128)} %stack.54.cols, f32[2048,896]{1,0:T(8,128)} %back_part.2.refs_1_.refs_0_, bf16[1024,4096]{1,0:T(8,128)(2,1)} %bitcast.55, bf16[1024,4096]{1,0:T(8,128)(2,1)} %collective-permute-done.3.refs_1_.refs_4_.refs_7_.refs_10_.refs_2_.refs_5_.refs_8_, bf16[896,512]{1,0:T(8,128)(2,1)} %copy-done.7, ...), custom_call_target="tpu_custom_call" | custom-call | flops 1000 | bytes 1000 | tf_op jit(solution)/shard_map/back_part/pallas_call | solution.py:205
  96.6 10.5 %back_last.1 = f32[4,32,128]{2,1,0:T(8,128)} custom-call(s32[9]{0:T(128)} %stack.54.cols, f32[2048,896]{1,0:T(8,128)} %back_part.3.refs_1_.refs_0_, bf16[1024,4096]{1,0:T(8,128)(2,1)} %bitcast.58, bf16[1024,4096]{1,0:T(8,128)(2,1)} %collective-permute-done.3.refs_1_.refs_4_.refs_7_.refs_10_.refs_2_.refs_5_.refs_8_, bf16[896,512]{1,0:T(8,128)(2,1)} %copy-done.8, ...), custom_call_target="tpu_custom_call" | custom-call | flops 1000 | bytes 1000 | tf_op jit(solution)/shard_map/back_last/pallas_call | solution.py:205
  109.4 2.6 %collective-permute-start.15 = (f32[4,16,128]{2,1,0:T(8,128)S(1)}, f32[4,16,128]{2,1,0:T(8,128)S(1)}, u32[]{:S(2)}, u32[]{:S(2)}) collective-permute-start(f32[4,16,128]{2,1,0:T(8,128)S(1)} %dynamic-slice_add_fusion), channel_id=1, source_target_pairs={{0,1},{1,0},{2,3},{3,2},{4,5},{5,4},{6,7},{7,6},{8,11},{9,10},{10,... | collective-permute-start | bytes 98312 | tf_op jit(solution)/shard_map/ppermute | solution.py:38
  114.2 1.9 %collective-permute-done.16 = f32[4,16,128]{2,1,0:T(8,128)S(1)} collective-permute-done((f32[4,16,128]{2,1,0:T(8,128)S(1)}, f32[4,16,128]{2,1,0:T(8,128)S(1)}, u32[]{:S(2)}, u32[]{:S(2)}) %collective-permute-start.16) | collective-permute-done | bytes 32800 | tf_op jit(solution)/shard_map/ppermute | solution.py:38
  116.2 2.7 %collective-permute-done.17 = f32[4,16,128]{2,1,0:T(8,128)S(1)} collective-permute-done((f32[4,16,128]{2,1,0:T(8,128)S(1)}, f32[4,16,128]{2,1,0:T(8,128)S(1)}, u32[]{:S(2)}, u32[]{:S(2)}) %collective-permute-start.17) | collective-permute-done | bytes 32800 | tf_op jit(solution)/shard_map/ppermute | solution.py:38
  119.2 3.7 %collective-permute-start.18 = (f32[4,16,128]{2,1,0:T(8,128)S(1)}, f32[4,16,128]{2,1,0:T(8,128)S(1)}, u32[]{:S(2)}, u32[]{:S(2)}) collective-permute-start(f32[4,16,128]{2,1,0:T(8,128)S(1)} %get-tuple-element.4), channel_id=1, source_target_pairs={{0,8},{1,9},{2,10},{3,11},{4,12},{5,13},{6,14},{7,15},{8,0},{9,1},... | collective-permute-start | bytes 98312 | tf_op jit(solution)/shard_map/ppermute | solution.py:38
  123.1 1.6 %collective-permute-start.21 = (bf16[2,9,16,128]{3,2,1,0:T(8,128)(2,1)S(1)}, bf16[2,9,16,128]{3,2,1,0:T(8,128)(2,1)S(1)}, u32[]{:S(2)}, u32[]{:S(2)}) collective-permute-start(bf16[2,9,16,128]{3,2,1,0:T(8,128)(2,1)S(1)} %pad_maximum_fusion.2), channel_id=1, source_target_pairs={{0,48},{1,49},{2,50},{3,51},{4,52},{5,53},{6,54},{7,55},{8,24},{9,... | collective-permute-start | bytes 221192 | tf_op jit(solution)/shard_map/ppermute | solution.py:38
  124.8 1.9 %collective-permute-done.21 = bf16[2,9,16,128]{3,2,1,0:T(8,128)(2,1)S(1)} collective-permute-done((bf16[2,9,16,128]{3,2,1,0:T(8,128)(2,1)S(1)}, bf16[2,9,16,128]{3,2,1,0:T(8,128)(2,1)S(1)}, u32[]{:S(2)}, u32[]{:S(2)}) %collective-permute-start.21) | collective-permute-done | bytes 73760 | tf_op jit(solution)/shard_map/ppermute | solution.py:38
  126.8 1.7 %collective-permute-start.22 = (bf16[4,9,16,128]{3,2,1,0:T(8,128)(2,1)S(1)}, bf16[4,9,16,128]{3,2,1,0:T(8,128)(2,1)S(1)}, u32[]{:S(2)}, u32[]{:S(2)}) collective-permute-start(bf16[4,9,16,128]{3,2,1,0:T(8,128)(2,1)S(1)} %pad_maximum_fusion.1), channel_id=1, source_target_pairs={{0,68},{1,69},{2,70},{3,71},{4,64},{5,65},{6,66},{7,67},{8,76},{9,... | collective-permute-start | bytes 442376 | tf_op jit(solution)/shard_map/ppermute | solution.py:38
  128.6 3.6 %collective-permute-done.22 = bf16[4,9,16,128]{3,2,1,0:T(8,128)(2,1)S(1)} collective-permute-done((bf16[4,9,16,128]{3,2,1,0:T(8,128)(2,1)S(1)}, bf16[4,9,16,128]{3,2,1,0:T(8,128)(2,1)S(1)}, u32[]{:S(2)}, u32[]{:S(2)}) %collective-permute-start.22) | collective-permute-done | bytes 147488 | tf_op jit(solution)/shard_map/ppermute | solution.py:38
  133.4 6.9 %collective-permute-start.23 = (f32[2,32,32]{2,1,0:T(8,128)S(1)}, f32[2,32,32]{2,1,0:T(8,128)S(1)}, u32[]{:S(2)}, u32[]{:S(2)}) collective-permute-start(f32[2,32,32]{2,1,0:T(8,128)S(1)} %fusion.8), channel_id=1, source_target_pairs={{0,8},{1,9},{2,10},{3,11},{4,12},{5,13},{6,14},{7,15},{8,0},{9,1},... | collective-permute-start | bytes 24584 | tf_op jit(solution)/shard_map/ppermute | solution.py:38
  (106 shorter events, 21.3 us)
Async XLA Ops:
  0.6 40.3 %collective-permute-start.3 = (bf16[1024,4096]{1,0:T(8,128)(2,1)}, bf16[1024,4096]{1,0:T(8,128)(2,1)}, u32[]{:S(2)}, u32[]{:S(2)}) collective-permute-start(bf16[1024,4096]{1,0:T(8,128)(2,1)} %bitcast.49), channel_id=1, source_target_pairs={{0,8},{1,9},{2,10},{3,11},{4,12},{5,13},{6,14},{7,15},{8,0},{9,1},... | collective-permute-start | bytes 25165832 | tf_op jit(solution)/shard_map/ppermute | solution.py:38
  2.1 8.5 %collective-permute-start = (bf16[1792,256]{1,0:T(8,128)(2,1)}, bf16[1792,256]{1,0:T(8,128)(2,1)S(1)}, u32[]{:S(2)}, u32[]{:S(2)}) collective-permute-start(bf16[1792,256]{1,0:T(8,128)(2,1)} %param.16), channel_id=1, source_target_pairs={{0,8},{1,9},{2,10},{3,11},{4,12},{5,13},{6,14},{7,15},{8,0},{9,1},... | collective-permute-start | bytes 2752520 | tf_op jit(solution)/shard_map/ppermute | solution.py:38
  2.2 93.4 %collective-permute-start.12 = (bf16[1024,1792]{1,0:T(8,128)(2,1)}, bf16[1024,1792]{1,0:T(8,128)(2,1)}, u32[]{:S(2)}, u32[]{:S(2)}) collective-permute-start(bf16[1024,1792]{1,0:T(8,128)(2,1)} %bitcast.59), channel_id=1, source_target_pairs={{0,8},{1,9},{2,10},{3,11},{4,12},{5,13},{6,14},{7,15},{8,0},{9,1},... | collective-permute-start | bytes 11010056 | tf_op jit(solution)/shard_map/ppermute | solution.py:38
  11.0 18.7 %collective-permute-start.4 = (bf16[896,512]{1,0:T(8,128)(2,1)S(1)}, bf16[896,512]{1,0:T(8,128)(2,1)S(1)}, u32[]{:S(2)}, u32[]{:S(2)}) collective-permute-start(bf16[896,512]{1,0:T(8,128)(2,1)S(1)} %maximum_select_fusion._.refs_2_), channel_id=1, source_target_pairs={{0,16},{1,17},{2,18},{3,19},{4,20},{5,21},{6,22},{7,23},{8,56},{9,... | collective-permute-start | bytes 2752520 | tf_op jit(solution)/shard_map/ppermute | solution.py:38
  13.9 23.1 %collective-permute-start.6 = (bf16[896,512]{1,0:T(8,128)(2,1)S(1)}, bf16[896,512]{1,0:T(8,128)(2,1)}, u32[]{:S(2)}, u32[]{:S(2)}) collective-permute-start(bf16[896,512]{1,0:T(8,128)(2,1)S(1)} %maximum_select_fusion._.refs_2_), channel_id=1, source_target_pairs={{0,64},{1,65},{2,66},{3,67},{4,68},{5,69},{6,70},{7,71},{8,72},{9,... | collective-permute-start | bytes 2752520 | tf_op jit(solution)/shard_map/ppermute | solution.py:38
  16.6 24.1 %collective-permute-start.5 = (bf16[896,512]{1,0:T(8,128)(2,1)S(1)}, bf16[896,512]{1,0:T(8,128)(2,1)S(1)}, u32[]{:S(2)}, u32[]{:S(2)}) collective-permute-start(bf16[896,512]{1,0:T(8,128)(2,1)S(1)} %maximum_select_fusion._.refs_2_), channel_id=1, source_target_pairs={{0,48},{1,49},{2,50},{3,51},{4,52},{5,53},{6,54},{7,55},{8,24},{9,... | collective-permute-start | bytes 2752520 | tf_op jit(solution)/shard_map/ppermute | solution.py:38
  30.6 27.3 %collective-permute-start.10 = (bf16[896,512]{1,0:T(8,128)(2,1)}, bf16[896,512]{1,0:T(8,128)(2,1)S(1)}, u32[]{:S(2)}, u32[]{:S(2)}) collective-permute-start(bf16[896,512]{1,0:T(8,128)(2,1)} %after.6.refs_5_), channel_id=1, source_target_pairs={{0,64},{1,65},{2,66},{3,67},{4,68},{5,69},{6,70},{7,71},{8,72},{9,... | collective-permute-start | bytes 2752520 | tf_op jit(solution)/shard_map/ppermute | solution.py:38
  37.0 22.2 %collective-permute-start.1 = (f32[64,1152]{1,0:T(8,128)}, f32[64,1152]{1,0:T(8,128)S(1)}, u32[]{:S(2)}, u32[]{:S(2)}) collective-permute-start(f32[64,1152]{1,0:T(8,128)} %early_rows.1.refs_1_), channel_id=1, source_target_pairs={{0,1},{1,0},{2,3},{3,2},{4,5},{5,4},{6,7},{7,6},{8,11},{9,10},{10,... | collective-permute-start | bytes 884744 | tf_op jit(solution)/shard_map/ppermute | solution.py:38
  40.8 39.2 %collective-permute-start.8 = (bf16[896,512]{1,0:T(8,128)(2,1)}, bf16[896,512]{1,0:T(8,128)(2,1)S(1)}, u32[]{:S(2)}, u32[]{:S(2)}) collective-permute-start(bf16[896,512]{1,0:T(8,128)(2,1)} %after.6.refs_5_), channel_id=1, source_target_pairs={{0,48},{1,49},{2,50},{3,51},{4,52},{5,53},{6,54},{7,55},{8,24},{9,... | collective-permute-start | bytes 2752520 | tf_op jit(solution)/shard_map/ppermute | solution.py:38
  41.0 39.0 %collective-permute-start.9 = (bf16[896,512]{1,0:T(8,128)(2,1)}, bf16[896,512]{1,0:T(8,128)(2,1)}, u32[]{:S(2)}, u32[]{:S(2)}) collective-permute-start(bf16[896,512]{1,0:T(8,128)(2,1)} %after.8.refs_11_), channel_id=1, source_target_pairs={{0,48},{1,49},{2,50},{3,51},{4,52},{5,53},{6,54},{7,55},{8,24},{9,... | collective-permute-start | bytes 2752520 | tf_op jit(solution)/shard_map/ppermute | solution.py:38
  59.0 36.6 %collective-permute-start.11 = (bf16[896,512]{1,0:T(8,128)(2,1)}, bf16[896,512]{1,0:T(8,128)(2,1)S(1)}, u32[]{:S(2)}, u32[]{:S(2)}) collective-permute-start(bf16[896,512]{1,0:T(8,128)(2,1)} %after.10.refs_9_), channel_id=1, source_target_pairs={{0,48},{1,49},{2,50},{3,51},{4,52},{5,53},{6,54},{7,55},{8,24},{9,... | collective-permute-start | bytes 2752520 | tf_op jit(solution)/shard_map/ppermute | solution.py:38
  59.2 5.9 %collective-permute-start.2 = (f32[64,1152]{1,0:T(8,128)S(1)}, f32[64,1152]{1,0:T(8,128)S(1)}, u32[]{:S(2)}, u32[]{:S(2)}) collective-permute-start(f32[64,1152]{1,0:T(8,128)S(1)} %add.103), channel_id=1, source_target_pairs={{0,3},{1,2},{2,1},{3,0},{4,7},{5,6},{6,5},{7,4},{8,9},{9,8},{10,11... | collective-permute-start | bytes 884744 | tf_op jit(solution)/shard_map/ppermute | solution.py:38
  66.9 6.3 %collective-permute-start.7 = (f32[64,1152]{1,0:T(8,128)S(1)}, f32[64,1152]{1,0:T(8,128)S(1)}, u32[]{:S(2)}, u32[]{:S(2)}) collective-permute-start(f32[64,1152]{1,0:T(8,128)S(1)} %add.119), channel_id=1, source_target_pairs={{0,4},{1,5},{2,6},{3,7},{4,0},{5,1},{6,2},{7,3},{8,12},{9,13},{10,... | collective-permute-start | bytes 884744 | tf_op jit(solution)/shard_map/ppermute | solution.py:38
  73.2 21.7 %collective-permute-start.13 = (f32[64,1152]{1,0:T(8,128)S(1)}, f32[64,1152]{1,0:T(8,128)S(1)}, u32[]{:S(2)}, u32[]{:S(2)}) collective-permute-start(f32[64,1152]{1,0:T(8,128)S(1)} %add.120.refs_0_), channel_id=1, source_target_pairs={{0,8},{1,9},{2,10},{3,11},{4,12},{5,13},{6,14},{7,15},{8,0},{9,1},... | collective-permute-start | bytes 884744 | tf_op jit(solution)/shard_map/ppermute | solution.py:38
  107.1 1.5 %collective-permute-start.14 = (f32[4,32,128]{2,1,0:T(8,128)}, f32[4,32,128]{2,1,0:T(8,128)S(1)}, u32[]{:S(2)}, u32[]{:S(2)}) collective-permute-start(f32[4,32,128]{2,1,0:T(8,128)} %back_last.1), channel_id=1, source_target_pairs={{0,8},{1,9},{2,10},{3,11},{4,12},{5,13},{6,14},{7,15},{8,0},{9,1},... | collective-permute-start | bytes 196616 | tf_op jit(solution)/shard_map/ppermute | solution.py:38
  109.4 4.0 %collective-permute-start.15 = (f32[4,16,128]{2,1,0:T(8,128)S(1)}, f32[4,16,128]{2,1,0:T(8,128)S(1)}, u32[]{:S(2)}, u32[]{:S(2)}) collective-permute-start(f32[4,16,128]{2,1,0:T(8,128)S(1)} %dynamic-slice_add_fusion), channel_id=1, source_target_pairs={{0,1},{1,0},{2,3},{3,2},{4,5},{5,4},{6,7},{7,6},{8,11},{9,10},{10,... | collective-permute-start | bytes 98312 | tf_op jit(solution)/shard_map/ppermute | solution.py:38
  112.0 1.4 collective-permute-start.19
  113.4 2.8 %collective-permute-start.16 = (f32[4,16,128]{2,1,0:T(8,128)S(1)}, f32[4,16,128]{2,1,0:T(8,128)S(1)}, u32[]{:S(2)}, u32[]{:S(2)}) collective-permute-start(f32[4,16,128]{2,1,0:T(8,128)S(1)} %add.123), channel_id=1, source_target_pairs={{0,3},{1,2},{2,1},{3,0},{4,7},{5,6},{6,5},{7,4},{8,9},{9,8},{10,11... | collective-permute-start | bytes 98312 | tf_op jit(solution)/shard_map/ppermute | solution.py:38
  116.1 2.8 %collective-permute-start.17 = (f32[4,16,128]{2,1,0:T(8,128)S(1)}, f32[4,16,128]{2,1,0:T(8,128)S(1)}, u32[]{:S(2)}, u32[]{:S(2)}) collective-permute-start(f32[4,16,128]{2,1,0:T(8,128)S(1)} %add.124), channel_id=1, source_target_pairs={{0,4},{1,5},{2,6},{3,7},{4,0},{5,1},{6,2},{7,3},{8,12},{9,13},{10,... | collective-permute-start | bytes 98312 | tf_op jit(solution)/shard_map/ppermute | solution.py:38
  119.0 4.1 %collective-permute-start.20 = (bf16[9,16,128]{2,1,0:T(8,128)(2,1)S(1)}, bf16[9,16,128]{2,1,0:T(8,128)(2,1)S(1)}, u32[]{:S(2)}, u32[]{:S(2)}) collective-permute-start(bf16[9,16,128]{2,1,0:T(8,128)(2,1)S(1)} %get-tuple-element.10), channel_id=1, source_target_pairs={{0,16},{1,17},{2,18},{3,19},{4,20},{5,21},{6,22},{7,23},{8,56},{9,... | collective-permute-start | bytes 110600 | tf_op jit(solution)/shard_map/ppermute | solution.py:38
  119.2 9.2 %collective-permute-start.18 = (f32[4,16,128]{2,1,0:T(8,128)S(1)}, f32[4,16,128]{2,1,0:T(8,128)S(1)}, u32[]{:S(2)}, u32[]{:S(2)}) collective-permute-start(f32[4,16,128]{2,1,0:T(8,128)S(1)} %get-tuple-element.4), channel_id=1, source_target_pairs={{0,8},{1,9},{2,10},{3,11},{4,12},{5,13},{6,14},{7,15},{8,0},{9,1},... | collective-permute-start | bytes 98312 | tf_op jit(solution)/shard_map/ppermute | solution.py:38
  123.1 3.6 %collective-permute-start.21 = (bf16[2,9,16,128]{3,2,1,0:T(8,128)(2,1)S(1)}, bf16[2,9,16,128]{3,2,1,0:T(8,128)(2,1)S(1)}, u32[]{:S(2)}, u32[]{:S(2)}) collective-permute-start(bf16[2,9,16,128]{3,2,1,0:T(8,128)(2,1)S(1)} %pad_maximum_fusion.2), channel_id=1, source_target_pairs={{0,48},{1,49},{2,50},{3,51},{4,52},{5,53},{6,54},{7,55},{8,24},{9,... | collective-permute-start | bytes 221192 | tf_op jit(solution)/shard_map/ppermute | solution.py:38
  126.8 5.4 %collective-permute-start.22 = (bf16[4,9,16,128]{3,2,1,0:T(8,128)(2,1)S(1)}, bf16[4,9,16,128]{3,2,1,0:T(8,128)(2,1)S(1)}, u32[]{:S(2)}, u32[]{:S(2)}) collective-permute-start(bf16[4,9,16,128]{3,2,1,0:T(8,128)(2,1)S(1)} %pad_maximum_fusion.1), channel_id=1, source_target_pairs={{0,68},{1,69},{2,70},{3,71},{4,64},{5,65},{6,66},{7,67},{8,76},{9,... | collective-permute-start | bytes 442376 | tf_op jit(solution)/shard_map/ppermute | solution.py:38
  133.4 7.8 %collective-permute-start.23 = (f32[2,32,32]{2,1,0:T(8,128)S(1)}, f32[2,32,32]{2,1,0:T(8,128)S(1)}, u32[]{:S(2)}, u32[]{:S(2)}) collective-permute-start(f32[2,32,32]{2,1,0:T(8,128)S(1)} %fusion.8), channel_id=1, source_target_pairs={{0,8},{1,9},{2,10},{3,11},{4,12},{5,13},{6,14},{7,15},{8,0},{9,1},... | collective-permute-start | bytes 24584 | tf_op jit(solution)/shard_map/ppermute | solution.py:38
  (13 other events, 88.6 us)

commit v2 on v1

--- a/solution.py
+++ b/solution.py
@@ -14,7 +14,8 @@
 EARLY_TILE = 256
 NT = (((1,), (1,)), ((), ()))
 CHUNKS = ((0, 896),)
-SMALL = pl.CostEstimate(flops=1000, bytes_accessed=1000, transcendentals=0)
+VMEM_LIMIT = 62 * 2**20
+LONG = pl.CostEstimate(flops=10**11, bytes_accessed=10**8, transcendentals=0)
 
 
 def coords(i):
@@ -61,6 +62,16 @@
 def silu(v):
     half = 0.5 * v
     return half + half * jnp.tanh(half)
+
+
+def outer(left, right):
+    left_hi, right_hi = left.astype(BF16), right.astype(BF16)
+    left_lo = (left - left_hi.astype(F32)).astype(BF16)
+    right_lo = (right - right_hi.astype(F32)).astype(BF16)
+    sides = jnp.concatenate([left_hi, left_lo], axis=0), jnp.concatenate([right_hi, right_lo], axis=1)
+    all_four = jnp.dot(*sides, preferred_element_type=F32)
+    n, m = left.shape[0], right.shape[1]
+    return all_four[:n, :m] + (all_four[:n, m:] + all_four[n:, :m]) + all_four[n:, m:]
 
 
 def after(value, *others):
@@ -88,7 +99,7 @@
     out_rows = lax.dot_general(grad[...], dout_t[...], NT, preferred_element_type=F32)
     pos = (i % per) * EARLY_TILE + lax.broadcasted_iota(jnp.int32, (64, EARLY_TILE), 1)
     live = (pos < counts[i // per]).astype(F32)
-    first = jnp.dot(hid_t * live, out_rows, precision=HIGHEST, preferred_element_type=F32)
+    first = outer(hid_t * live, out_rows)
     packed = jnp.concatenate([first[:32], first[32:]], axis=1)
     here = pl.ds(pl.multiple_of((i // per) * 32, 32), 32)
 
@@ -116,17 +127,18 @@
             in_specs=[row(width), row(width), row(grad.shape[1]), row(inp.shape[1]), full(din_t), full(dout_t), full(uin_t), pl.BlockSpec(memory_space=pl.ANY)],
             out_specs=pl.BlockSpec((64, tokens + 128), lambda i, s: (0, 0)),
         ),
-        compiler_params=pltpu.CompilerParams(vmem_limit_bytes=56 * 2**20),
-        cost_estimate=SMALL,
+        compiler_params=pltpu.CompilerParams(vmem_limit_bytes=VMEM_LIMIT),
+        cost_estimate=LONG,
         name="early_rows",
     )(counts, gate, up, grad, inp, din_t, dout_t, uin_t, later_than)
 
 
-def back_kernel(n, has_acc, last, has_first, lo, cols, *refs):
+def back_kernel(n, has_acc, last, has_first, lo, later, cols, *refs):
     i = pl.program_id(0)
     half = pl.num_programs(0) // 2
     refs = list(refs)
     acc_ref = refs.pop(0) if has_acc else None
+    refs = refs[:len(refs) - 1 - later] + refs[-1:]
     blocks, rest = refs[: 3 * n], refs[3 * n :]
     out = rest[-1]
 
@@ -142,7 +154,7 @@
         gate = rest[side][:, lo : lo + width]
         delta = (acc * silu(gate.astype(F32))).astype(BF16)
         del_rows = lax.dot_general(delta, rest[2][:, lo : lo + width], NT, preferred_element_type=F32)
-        second = jnp.dot(rest[3 + side][...], del_rows, precision=HIGHEST, preferred_element_type=F32)
+        second = outer(rest[3 + side][...], del_rows)
         packed = jnp.concatenate([second[:32], second[32:]], axis=1)
 
         @pl.when(i % (512 // TILE) == 0)
@@ -162,7 +174,7 @@
         run(1)
 
 
-def back_step(cols, acc, pieces, grads, tail=None, lo=0):
+def back_step(cols, acc, pieces, grads, tail=None, lo=0, later=()):
     mine, theirs = grads
     tokens = mine.shape[0]
     steps = tokens // TILE
@@ -202,14 +214,16 @@
             args.append(first)
             specs.append(out_spec)
         out_shape = jax.ShapeDtypeStruct((4, 32, 128), F32)
+    args += later
+    specs += [pl.BlockSpec(memory_space=pl.ANY)] * len(later)
     return pl.pallas_call(
-        functools.partial(back_kernel, n, acc is not None, tail is not None, tail is not None and tail[5] is not None, lo),
+        functools.partial(back_kernel, n, acc is not None, tail is not None, tail is not None and tail[5] is not None, lo, len(later)),
         out_shape=out_shape,
         grid_spec=pltpu.PrefetchScalarGridSpec(
             num_scalar_prefetch=1, grid=(2 * steps,), in_specs=specs, out_specs=out_spec
         ),
-        compiler_params=pltpu.CompilerParams(vmem_limit_bytes=56 * 2**20),
-        cost_estimate=SMALL,
+        compiler_params=pltpu.CompilerParams(vmem_limit_bytes=VMEM_LIMIT),
+        cost_estimate=LONG,
         name="back_last" if tail is not None else "back_part",
     )(cols, *args)
 
@@ -252,28 +266,28 @@
     h_x = swap_x_far(h)
     h_y = swap_y(h, 0)
     h_y2 = swap_y(h, 1)
-    gate_other = swap_core(gate)
-    grads_other = swap_core(grads)
-    both = (grads, grads_other)
-
     early = projected_rows(
         counts, gate, up, grads, inputs, down_in_proj.T, down_out_proj.T, up_in_proj.T, h
     )
+    grads_other = swap_core(grads)
+    gate_other = swap_core(gate)
+    both = (grads, grads_other)
     h_y, h_x, h_y2 = after(h_y, early), after(h_x, early), after(h_y2, early)
     h_xy = swap_x_far(h_y)
     h_yy = swap_y(h_y, 1)
     h_xy2 = swap_y(h_x, 1)
     rows = early + swap_z(early, 0)
     rows_second = swap_z(rows, 1)
-
-    acc = back_step(cols, None, [(h, 0), (h_y, 1), (h_y2, 2), (h_x, 3)], both)
+    acc = back_step(cols, None, [(h, 0), (h_y, 1), (h_y2, 2), (h_x, 3)], both, later=(rows,))
+
     h_xy = after(h_xy, acc)
     h_xyy = swap_y(h_xy, 1)
     rows = rows + after(rows_second, acc)
-    rows = rows + swap_x(rows, 0)
+    rows_third = swap_x(rows, 0)
+    acc = back_step(cols, acc, [(h_yy, 4), (h_xy2, 5), (h_xy, 6)], both, later=(rows,))
+    rows = rows + after(rows_third, acc)
     rows_other = swap_core(rows)
-    acc = back_step(cols, acc, [(h_yy, 4), (h_xy2, 5), (h_xy, 6)], both)
-    tail = (gate, gate_other, up_out_proj.T, after(rows, acc), rows_other, None)
+    tail = (gate, gate_other, up_out_proj.T, rows, rows_other, None)
     second = back_step(cols, acc, [(h_xyy, 7)], both, tail, 0)
 
     second_other = swap_core(second)
@@ -307,7 +321,7 @@
     placing = (slot_ids[None, :] == labels[:, None]).astype(F32)
     by_id = jnp.einsum("as,mst,bt->mab", placing, partial, placing, precision=HIGHEST)
     gram = (by_id + swap_core(by_id)) / 4096.0
-    norm = jnp.sqrt(jnp.diagonal(gram, axis1=1, axis2=2) + 1e-06)
+    norm = jnp.sqrt(jnp.sum(gram * jnp.eye(32, dtype=F32), axis=2) + 1e-06)
     picking = (queries[:, None] == labels[None, :]).astype(F32)
     chosen = jnp.einsum("qa,mab->mqb", picking, gram, precision=HIGHEST)
     chosen_norm = jnp.einsum("qa,ma->mq", picking, norm, precision=HIGHEST)

time: 144 us -> 127 us (0.88)
  waiting for transfers between devices: 33.9 us -> 18.5 us
  starting transfers between devices: 43.8 us -> 39.8 us
  other arithmetic: 2.62 us -> 5.46 us
    ppermute x24, waiting for transfers between devices: 33.9 us -> 18.5 us  [moved(): lax.ppermute(value, AXES, [(i, index(*to(*coords(i)))) for i in range(128)])]
    ppermute x24, starting transfers between devices: 43.8 us -> 39.8 us  [moved(): lax.ppermute(value, AXES, [(i, index(*to(*coords(i)))) for i in range(128)])]
    unnamed x26 -> x27, local copies, waits for them, and re-layouts: 5.23 us -> 5.08 us
  transfers between devices with their start and end apart: 24 -> 24, of which waited for: 12 -> 11; matrix products, arithmetic and copies ran while one was open for 4% -> 7% of each run, Pallas kernels for 28% -> 31%
where the time goes in v2:
time: 127 us
  Pallas kernels  50.5 us (40%)
  starting transfers between devices  39.8 us (31%)
  waiting for transfers between devices  18.5 us (15%)
  local copies, waits for them, and re-layouts  10 us (8%)
  other arithmetic  5.46 us (4%)
  matrix products  1.58 us (1%)
    ppermute x24, starting transfers between devices, moved(): lax.ppermute(value, AXES, [(i, index(*to(*coords(i)))) for i in range(128)])  39.8 us
    pallas_call x3, Pallas kernels, back_step(): pl.pallas_call(functools.partial(back_kernel, n, acc is not None, tail is...  39.7 us
    ppermute x24, waiting for transfers between devices, moved(): lax.ppermute(value, AXES, [(i, index(*to(*coords(i)))) for i in range(128)])  18.5 us
    pallas_call x1, Pallas kernels, projected_rows(): pl.pallas_call(rows_kernel, out_shape=jax.ShapeDtypeStruct((64, tokens +...  10.8 us
    unnamed x27, local copies, waits for them, and re-layouts  5.08 us
  transfers between devices with their start and end apart: 24, of which 11 were waited for; matrix products, arithmetic and copies ran while one was open for 7% of the time, Pallas kernels for 31%

profile of v2, /device:TPU:1, one launch (start us, length us, event | category | flops | bytes accessed | tf_op | source)
XLA Modules:
  0.0 126.8 jit_solution(15990909933511388386)
XLA Ops:
  0.6 1.5 %collective-permute-start = (bf16[1792,256]{1,0:T(8,128)(2,1)}, bf16[1792,256]{1,0:T(8,128)(2,1)S(1)}, u32[]{:S(2)}, u32[]{:S(2)}) collective-permute-start(bf16[1792,256]{1,0:T(8,128)(2,1)} %param.16), channel_id=1, source_target_pairs={{0,8},{1,9},{2,10},{3,11},{4,12},{5,13},{6,14},{7,15},{8,0},{9,1},... | collective-permute-start | bytes 2752520 | tf_op jit(solution)/shard_map/ppermute | solution.py:39
  3.4 1.4 %collective-permute-done = bf16[1792,256]{1,0:T(8,128)(2,1)S(1)} collective-permute-done((bf16[1792,256]{1,0:T(8,128)(2,1)}, bf16[1792,256]{1,0:T(8,128)(2,1)S(1)}, u32[]{:S(2)}, u32[]{:S(2)}) %collective-permute-start) | collective-permute-done | bytes 917536 | tf_op jit(solution)/shard_map/ppermute | solution.py:39
  6.1 1.4 %collective-permute-start.5 = (bf16[896,512]{1,0:T(8,128)(2,1)}, bf16[896,512]{1,0:T(8,128)(2,1)}, u32[]{:S(2)}, u32[]{:S(2)}) collective-permute-start(bf16[896,512]{1,0:T(8,128)(2,1)} %maximum_select_fusion._.refs_2_), channel_id=1, source_target_pairs={{0,48},{1,49},{2,50},{3,51},{4,52},{5,53},{6,54},{7,55},{8,24},{9,... | collective-permute-start | bytes 2752520 | tf_op jit(solution)/shard_map/ppermute | solution.py:39
  7.5 2.7 %collective-permute-start.6 = (bf16[896,512]{1,0:T(8,128)(2,1)}, bf16[896,512]{1,0:T(8,128)(2,1)}, u32[]{:S(2)}, u32[]{:S(2)}) collective-permute-start(bf16[896,512]{1,0:T(8,128)(2,1)} %maximum_select_fusion._.refs_2_), channel_id=1, source_target_pairs={{0,64},{1,65},{2,66},{3,67},{4,68},{5,69},{6,70},{7,71},{8,72},{9,... | collective-permute-start | bytes 2752520 | tf_op jit(solution)/shard_map/ppermute | solution.py:39
  10.2 1.9 %collective-permute-start.4 = (bf16[896,512]{1,0:T(8,128)(2,1)}, bf16[896,512]{1,0:T(8,128)(2,1)S(1)}, u32[]{:S(2)}, u32[]{:S(2)}) collective-permute-start(bf16[896,512]{1,0:T(8,128)(2,1)} %maximum_select_fusion._.refs_2_), channel_id=1, source_target_pairs={{0,16},{1,17},{2,18},{3,19},{4,20},{5,21},{6,22},{7,23},{8,56},{9,... | collective-permute-start | bytes 2752520 | tf_op jit(solution)/shard_map/ppermute | solution.py:39
  12.1 10.8 %early_rows.1.refs_1_ = f32[64,1152]{1,0:T(8,128)} custom-call(s32[2]{0:T(128)} %counts.1, bf16[1024,1792]{1,0:T(8,128)(2,1)} %bitcast.63, bf16[1024,1792]{1,0:T(8,128)(2,1)} %bitcast.62, bf16[1024,4096]{1,0:T(8,128)(2,1)} %bitcast.53, bf16[1024,512]{1,0:T(8,128)(2,1)} %bitcast.66, bf16[64,1792]{1,0:T(8,128)(2,1)} %bitcast.68, bf16[64,4096]{1,0:T(8,128)(2,1)} %bitcast.67, ...), custom_call_target="tpu_custom_call" | custom-call | flops 99999997952 | bytes 100000000 | tf_op jit(solution)/shard_map/early_rows/pallas_call | solution.py:121
  22.9 3.8 %collective-permute-start.1 = (f32[64,1152]{1,0:T(8,128)}, f32[64,1152]{1,0:T(8,128)S(1)}, u32[]{:S(2)}, u32[]{:S(2)}) collective-permute-start(f32[64,1152]{1,0:T(8,128)} %early_rows.1.refs_1_), channel_id=1, source_target_pairs={{0,1},{1,0},{2,3},{3,2},{4,5},{5,4},{6,7},{7,6},{8,11},{9,10},{10,... | collective-permute-start | bytes 884744 | tf_op jit(solution)/shard_map/ppermute | solution.py:39
  27.3 4.1 %collective-permute-done.1 = f32[64,1152]{1,0:T(8,128)S(1)} collective-permute-done((f32[64,1152]{1,0:T(8,128)}, f32[64,1152]{1,0:T(8,128)S(1)}, u32[]{:S(2)}, u32[]{:S(2)}) %collective-permute-start.1) | collective-permute-done | bytes 294944 | tf_op jit(solution)/shard_map/ppermute | solution.py:39
  33.4 1.8 %collective-permute-start.10 = (bf16[896,512]{1,0:T(8,128)(2,1)}, bf16[896,512]{1,0:T(8,128)(2,1)S(1)}, u32[]{:S(2)}, u32[]{:S(2)}) collective-permute-start(bf16[896,512]{1,0:T(8,128)(2,1)} %after.6.refs_5_), channel_id=1, source_target_pairs={{0,64},{1,65},{2,66},{3,67},{4,68},{5,69},{6,70},{7,71},{8,72},{9,... | collective-permute-start | bytes 2752520 | tf_op jit(solution)/shard_map/ppermute | solution.py:39
  36.6 15.1 %back_part.2.refs_1_.refs_0_ = f32[2048,896]{1,0:T(8,128)} custom-call(s32[9]{0:T(128)} %stack.54.cols, bf16[1024,4096]{1,0:T(8,128)(2,1)} %bitcast.54, bf16[1024,4096]{1,0:T(8,128)(2,1)} %collective-permute-done.3.refs_1_.refs_4_.refs_7_.refs_10_.refs_2_.refs_5_.refs_8_, bf16[896,512]{1,0:T(8,128)(2,1)} %maximum_select_fusion._.refs_2_, ...), custom_call_target="tpu_custom_call" | custom-call | flops 99999997952 | bytes 100000000 | tf_op jit(solution)/shard_map/back_part/pallas_call | solution.py:219
  55.3 1.6 %collective-permute-start.11 = (bf16[896,512]{1,0:T(8,128)(2,1)}, bf16[896,512]{1,0:T(8,128)(2,1)S(1)}, u32[]{:S(2)}, u32[]{:S(2)}) collective-permute-start(bf16[896,512]{1,0:T(8,128)(2,1)} %after.10.refs_9_), channel_id=1, source_target_pairs={{0,48},{1,49},{2,50},{3,51},{4,52},{5,53},{6,54},{7,55},{8,24},{9,... | collective-permute-start | bytes 2752520 | tf_op jit(solution)/shard_map/ppermute | solution.py:39
  57.8 13.9 %back_part.3.refs_1_.refs_0_ = f32[2048,896]{1,0:T(8,128)} custom-call(s32[9]{0:T(128)} %stack.54.cols, f32[2048,896]{1,0:T(8,128)} %back_part.2.refs_1_.refs_0_, bf16[1024,4096]{1,0:T(8,128)(2,1)} %bitcast.58, bf16[1024,4096]{1,0:T(8,128)(2,1)} %collective-permute-done.3.refs_1_.refs_4_.refs_7_.refs_10_.refs_2_.refs_5_.refs_8_, ...), custom_call_target="tpu_custom_call" | custom-call | flops 99999997952 | bytes 100000000 | tf_op jit(solution)/shard_map/back_part/pallas_call | solution.py:219
  73.8 3.8 %collective-permute-start.13 = (f32[64,1152]{1,0:T(8,128)S(1)}, f32[64,1152]{1,0:T(8,128)S(1)}, u32[]{:S(2)}, u32[]{:S(2)}) collective-permute-start(f32[64,1152]{1,0:T(8,128)S(1)} %add.116.refs_7_), channel_id=1, source_target_pairs={{0,8},{1,9},{2,10},{3,11},{4,12},{5,13},{6,14},{7,15},{8,0},{9,1},... | collective-permute-start | bytes 884744 | tf_op jit(solution)/shard_map/ppermute | solution.py:39
  79.9 10.7 %back_last.1 = f32[4,32,128]{2,1,0:T(8,128)} custom-call(s32[9]{0:T(128)} %stack.54.cols, f32[2048,896]{1,0:T(8,128)} %back_part.3.refs_1_.refs_0_, bf16[1024,4096]{1,0:T(8,128)(2,1)} %bitcast.61, bf16[1024,4096]{1,0:T(8,128)(2,1)} %collective-permute-done.3.refs_1_.refs_4_.refs_7_.refs_10_.refs_2_.refs_5_.refs_8_, bf16[896,512]{1,0:T(8,128)(2,1)} %copy-done.11, ...), custom_call_target="tpu_custom_call" | custom-call | flops 99999997952 | bytes 100000000 | tf_op jit(solution)/shard_map/back_last/pallas_call | solution.py:219
  92.9 1.8 %collective-permute-start.15 = (f32[4,16,128]{2,1,0:T(8,128)S(1)}, f32[4,16,128]{2,1,0:T(8,128)S(1)}, u32[]{:S(2)}, u32[]{:S(2)}) collective-permute-start(f32[4,16,128]{2,1,0:T(8,128)S(1)} %dynamic-slice_add_fusion), channel_id=1, source_target_pairs={{0,1},{1,0},{2,3},{3,2},{4,5},{5,4},{6,7},{7,6},{8,11},{9,10},{10,... | collective-permute-start | bytes 98312 | tf_op jit(solution)/shard_map/ppermute | solution.py:39
  94.7 2.2 %collective-permute-done.15 = f32[4,16,128]{2,1,0:T(8,128)S(1)} collective-permute-done((f32[4,16,128]{2,1,0:T(8,128)S(1)}, f32[4,16,128]{2,1,0:T(8,128)S(1)}, u32[]{:S(2)}, u32[]{:S(2)}) %collective-permute-start.15) | collective-permute-done | bytes 32800 | tf_op jit(solution)/shard_map/ppermute | solution.py:39
  99.7 1.8 %collective-permute-start.17 = (f32[4,16,128]{2,1,0:T(8,128)S(1)}, f32[4,16,128]{2,1,0:T(8,128)S(1)}, u32[]{:S(2)}, u32[]{:S(2)}) collective-permute-start(f32[4,16,128]{2,1,0:T(8,128)S(1)} %add.120), channel_id=1, source_target_pairs={{0,4},{1,5},{2,6},{3,7},{4,0},{5,1},{6,2},{7,3},{8,12},{9,13},{10,... | collective-permute-start | bytes 98312 | tf_op jit(solution)/shard_map/ppermute | solution.py:39
  102.8 2.2 %collective-permute-start.20 = (bf16[9,16,128]{2,1,0:T(8,128)(2,1)S(1)}, bf16[9,16,128]{2,1,0:T(8,128)(2,1)S(1)}, u32[]{:S(2)}, u32[]{:S(2)}) collective-permute-start(bf16[9,16,128]{2,1,0:T(8,128)(2,1)S(1)} %get-tuple-element.18), channel_id=1, source_target_pairs={{0,16},{1,17},{2,18},{3,19},{4,20},{5,21},{6,22},{7,23},{8,56},{9,... | collective-permute-start | bytes 110600 | tf_op jit(solution)/shard_map/ppermute | solution.py:39
  105.1 1.7 %collective-permute-start.18 = (f32[4,16,128]{2,1,0:T(8,128)S(1)}, f32[4,16,128]{2,1,0:T(8,128)S(1)}, u32[]{:S(2)}, u32[]{:S(2)}) collective-permute-start(f32[4,16,128]{2,1,0:T(8,128)S(1)} %get-tuple-element.10), channel_id=1, source_target_pairs={{0,8},{1,9},{2,10},{3,11},{4,12},{5,13},{6,14},{7,15},{8,0},{9,1},... | collective-permute-start | bytes 98312 | tf_op jit(solution)/shard_map/ppermute | solution.py:39
  107.0 1.5 %collective-permute-start.21 = (bf16[2,9,16,128]{3,2,1,0:T(8,128)(2,1)S(1)}, bf16[2,9,16,128]{3,2,1,0:T(8,128)(2,1)S(1)}, u32[]{:S(2)}, u32[]{:S(2)}) collective-permute-start(bf16[2,9,16,128]{3,2,1,0:T(8,128)(2,1)S(1)} %pad_maximum_fusion.2), channel_id=1, source_target_pairs={{0,48},{1,49},{2,50},{3,51},{4,52},{5,53},{6,54},{7,55},{8,24},{9,... | collective-permute-start | bytes 221192 | tf_op jit(solution)/shard_map/ppermute | solution.py:39
  108.6 1.9 %collective-permute-done.21 = bf16[2,9,16,128]{3,2,1,0:T(8,128)(2,1)S(1)} collective-permute-done((bf16[2,9,16,128]{3,2,1,0:T(8,128)(2,1)S(1)}, bf16[2,9,16,128]{3,2,1,0:T(8,128)(2,1)S(1)}, u32[]{:S(2)}, u32[]{:S(2)}) %collective-permute-start.21) | collective-permute-done | bytes 73760 | tf_op jit(solution)/shard_map/ppermute | solution.py:39
  110.5 2.2 %collective-permute-start.22 = (bf16[4,9,16,128]{3,2,1,0:T(8,128)(2,1)S(1)}, bf16[4,9,16,128]{3,2,1,0:T(8,128)(2,1)S(1)}, u32[]{:S(2)}, u32[]{:S(2)}) collective-permute-start(bf16[4,9,16,128]{3,2,1,0:T(8,128)(2,1)S(1)} %pad_maximum_fusion.1), channel_id=1, source_target_pairs={{0,68},{1,69},{2,70},{3,71},{4,64},{5,65},{6,66},{7,67},{8,76},{9,... | collective-permute-start | bytes 442376 | tf_op jit(solution)/shard_map/ppermute | solution.py:39
  112.9 3.0 %collective-permute-done.22 = bf16[4,9,16,128]{3,2,1,0:T(8,128)(2,1)S(1)} collective-permute-done((bf16[4,9,16,128]{3,2,1,0:T(8,128)(2,1)S(1)}, bf16[4,9,16,128]{3,2,1,0:T(8,128)(2,1)S(1)}, u32[]{:S(2)}, u32[]{:S(2)}) %collective-permute-start.22) | collective-permute-done | bytes 147488 | tf_op jit(solution)/shard_map/ppermute | solution.py:39
  117.2 6.9 %collective-permute-start.23 = (f32[2,32,32]{1,2,0:T(8,128)S(1)}, f32[2,32,32]{1,2,0:T(8,128)S(1)}, u32[]{:S(2)}, u32[]{:S(2)}) collective-permute-start(f32[2,32,32]{1,2,0:T(8,128)S(1)} %fusion.8), channel_id=1, source_target_pairs={{0,8},{1,9},{2,10},{3,11},{4,12},{5,13},{6,14},{7,15},{8,0},{9,1},... | collective-permute-start | bytes 24584 | tf_op jit(solution)/shard_map/ppermute | solution.py:39
  (104 shorter events, 26.3 us)
Async XLA Ops:
  0.6 4.2 %collective-permute-start = (bf16[1792,256]{1,0:T(8,128)(2,1)}, bf16[1792,256]{1,0:T(8,128)(2,1)S(1)}, u32[]{:S(2)}, u32[]{:S(2)}) collective-permute-start(bf16[1792,256]{1,0:T(8,128)(2,1)} %param.16), channel_id=1, source_target_pairs={{0,8},{1,9},{2,10},{3,11},{4,12},{5,13},{6,14},{7,15},{8,0},{9,1},... | collective-permute-start | bytes 2752520 | tf_op jit(solution)/shard_map/ppermute | solution.py:39
  2.1 33.2 %collective-permute-start.3 = (bf16[1024,4096]{1,0:T(8,128)(2,1)}, bf16[1024,4096]{1,0:T(8,128)(2,1)}, u32[]{:S(2)}, u32[]{:S(2)}) collective-permute-start(bf16[1024,4096]{1,0:T(8,128)(2,1)} %bitcast.52), channel_id=1, source_target_pairs={{0,8},{1,9},{2,10},{3,11},{4,12},{5,13},{6,14},{7,15},{8,0},{9,1},... | collective-permute-start | bytes 25165832 | tf_op jit(solution)/shard_map/ppermute | solution.py:39
  6.1 27.3 %collective-permute-start.5 = (bf16[896,512]{1,0:T(8,128)(2,1)}, bf16[896,512]{1,0:T(8,128)(2,1)}, u32[]{:S(2)}, u32[]{:S(2)}) collective-permute-start(bf16[896,512]{1,0:T(8,128)(2,1)} %maximum_select_fusion._.refs_2_), channel_id=1, source_target_pairs={{0,48},{1,49},{2,50},{3,51},{4,52},{5,53},{6,54},{7,55},{8,24},{9,... | collective-permute-start | bytes 2752520 | tf_op jit(solution)/shard_map/ppermute | solution.py:39
  7.5 27.7 %collective-permute-start.6 = (bf16[896,512]{1,0:T(8,128)(2,1)}, bf16[896,512]{1,0:T(8,128)(2,1)}, u32[]{:S(2)}, u32[]{:S(2)}) collective-permute-start(bf16[896,512]{1,0:T(8,128)(2,1)} %maximum_select_fusion._.refs_2_), channel_id=1, source_target_pairs={{0,64},{1,65},{2,66},{3,67},{4,68},{5,69},{6,70},{7,71},{8,72},{9,... | collective-permute-start | bytes 2752520 | tf_op jit(solution)/shard_map/ppermute | solution.py:39
  10.2 22.2 %collective-permute-start.4 = (bf16[896,512]{1,0:T(8,128)(2,1)}, bf16[896,512]{1,0:T(8,128)(2,1)S(1)}, u32[]{:S(2)}, u32[]{:S(2)}) collective-permute-start(bf16[896,512]{1,0:T(8,128)(2,1)} %maximum_select_fusion._.refs_2_), channel_id=1, source_target_pairs={{0,16},{1,17},{2,18},{3,19},{4,20},{5,21},{6,22},{7,23},{8,56},{9,... | collective-permute-start | bytes 2752520 | tf_op jit(solution)/shard_map/ppermute | solution.py:39
  22.9 8.5 %collective-permute-start.1 = (f32[64,1152]{1,0:T(8,128)}, f32[64,1152]{1,0:T(8,128)S(1)}, u32[]{:S(2)}, u32[]{:S(2)}) collective-permute-start(f32[64,1152]{1,0:T(8,128)} %early_rows.1.refs_1_), channel_id=1, source_target_pairs={{0,1},{1,0},{2,3},{3,2},{4,5},{5,4},{6,7},{7,6},{8,11},{9,10},{10,... | collective-permute-start | bytes 884744 | tf_op jit(solution)/shard_map/ppermute | solution.py:39
  31.4 46.3 %collective-permute-start.12 = (bf16[1024,1792]{1,0:T(8,128)(2,1)}, bf16[1024,1792]{1,0:T(8,128)(2,1)}, u32[]{:S(2)}, u32[]{:S(2)}) collective-permute-start(bf16[1024,1792]{1,0:T(8,128)(2,1)} %bitcast.64), channel_id=1, source_target_pairs={{0,8},{1,9},{2,10},{3,11},{4,12},{5,13},{6,14},{7,15},{8,0},{9,1},... | collective-permute-start | bytes 11010056 | tf_op jit(solution)/shard_map/ppermute | solution.py:39
  32.4 19.4 %collective-permute-start.2 = (f32[64,1152]{1,0:T(8,128)S(1)}, f32[64,1152]{1,0:T(8,128)S(1)}, u32[]{:S(2)}, u32[]{:S(2)}) collective-permute-start(f32[64,1152]{1,0:T(8,128)S(1)} %add.99.refs_12_), channel_id=1, source_target_pairs={{0,3},{1,2},{2,1},{3,0},{4,7},{5,6},{6,5},{7,4},{8,9},{9,8},{10,11... | collective-permute-start | bytes 884744 | tf_op jit(solution)/shard_map/ppermute | solution.py:39
  33.4 21.0 %collective-permute-start.10 = (bf16[896,512]{1,0:T(8,128)(2,1)}, bf16[896,512]{1,0:T(8,128)(2,1)S(1)}, u32[]{:S(2)}, u32[]{:S(2)}) collective-permute-start(bf16[896,512]{1,0:T(8,128)(2,1)} %after.6.refs_5_), channel_id=1, source_target_pairs={{0,64},{1,65},{2,66},{3,67},{4,68},{5,69},{6,70},{7,71},{8,72},{9,... | collective-permute-start | bytes 2752520 | tf_op jit(solution)/shard_map/ppermute | solution.py:39
  35.1 22.7 %collective-permute-start.8 = (bf16[896,512]{1,0:T(8,128)(2,1)}, bf16[896,512]{1,0:T(8,128)(2,1)}, u32[]{:S(2)}, u32[]{:S(2)}) collective-permute-start(bf16[896,512]{1,0:T(8,128)(2,1)} %after.6.refs_5_), channel_id=1, source_target_pairs={{0,48},{1,49},{2,50},{3,51},{4,52},{5,53},{6,54},{7,55},{8,24},{9,... | collective-permute-start | bytes 2752520 | tf_op jit(solution)/shard_map/ppermute | solution.py:39
  35.4 22.4 %collective-permute-start.9 = (bf16[896,512]{1,0:T(8,128)(2,1)}, bf16[896,512]{1,0:T(8,128)(2,1)}, u32[]{:S(2)}, u32[]{:S(2)}) collective-permute-start(bf16[896,512]{1,0:T(8,128)(2,1)} %after.8.refs_11_), channel_id=1, source_target_pairs={{0,48},{1,49},{2,50},{3,51},{4,52},{5,53},{6,54},{7,55},{8,24},{9,... | collective-permute-start | bytes 2752520 | tf_op jit(solution)/shard_map/ppermute | solution.py:39
  53.8 18.0 %collective-permute-start.7 = (f32[64,1152]{1,0:T(8,128)S(1)}, f32[64,1152]{1,0:T(8,128)S(1)}, u32[]{:S(2)}, u32[]{:S(2)}) collective-permute-start(f32[64,1152]{1,0:T(8,128)S(1)} %add.115.refs_10_), channel_id=1, source_target_pairs={{0,4},{1,5},{2,6},{3,7},{4,0},{5,1},{6,2},{7,3},{8,12},{9,13},{10,... | collective-permute-start | bytes 884744 | tf_op jit(solution)/shard_map/ppermute | solution.py:39
  55.3 23.5 %collective-permute-start.11 = (bf16[896,512]{1,0:T(8,128)(2,1)}, bf16[896,512]{1,0:T(8,128)(2,1)S(1)}, u32[]{:S(2)}, u32[]{:S(2)}) collective-permute-start(bf16[896,512]{1,0:T(8,128)(2,1)} %after.10.refs_9_), channel_id=1, source_target_pairs={{0,48},{1,49},{2,50},{3,51},{4,52},{5,53},{6,54},{7,55},{8,24},{9,... | collective-permute-start | bytes 2752520 | tf_op jit(solution)/shard_map/ppermute | solution.py:39
  73.8 5.0 %collective-permute-start.13 = (f32[64,1152]{1,0:T(8,128)S(1)}, f32[64,1152]{1,0:T(8,128)S(1)}, u32[]{:S(2)}, u32[]{:S(2)}) collective-permute-start(f32[64,1152]{1,0:T(8,128)S(1)} %add.116.refs_7_), channel_id=1, source_target_pairs={{0,8},{1,9},{2,10},{3,11},{4,12},{5,13},{6,14},{7,15},{8,0},{9,1},... | collective-permute-start | bytes 884744 | tf_op jit(solution)/shard_map/ppermute | solution.py:39
  90.6 1.6 %collective-permute-start.14 = (f32[4,32,128]{2,1,0:T(8,128)}, f32[4,32,128]{2,1,0:T(8,128)S(1)}, u32[]{:S(2)}, u32[]{:S(2)}) collective-permute-start(f32[4,32,128]{2,1,0:T(8,128)} %back_last.1), channel_id=1, source_target_pairs={{0,8},{1,9},{2,10},{3,11},{4,12},{5,13},{6,14},{7,15},{8,0},{9,1},... | collective-permute-start | bytes 196616 | tf_op jit(solution)/shard_map/ppermute | solution.py:39
  92.9 4.0 %collective-permute-start.15 = (f32[4,16,128]{2,1,0:T(8,128)S(1)}, f32[4,16,128]{2,1,0:T(8,128)S(1)}, u32[]{:S(2)}, u32[]{:S(2)}) collective-permute-start(f32[4,16,128]{2,1,0:T(8,128)S(1)} %dynamic-slice_add_fusion), channel_id=1, source_target_pairs={{0,1},{1,0},{2,3},{3,2},{4,5},{5,4},{6,7},{7,6},{8,11},{9,10},{10,... | collective-permute-start | bytes 98312 | tf_op jit(solution)/shard_map/ppermute | solution.py:39
  94.7 2.2 %collective-permute-start.19 = (s32[2]{0:T(128)S(1)}, s32[2]{0:T(128)S(1)}, u32[]{:S(2)}, u32[]{:S(2)}) collective-permute-start(s32[2]{0:T(128)S(1)} %copy-done.10), channel_id=1, source_target_pairs={{0,8},{1,9},{2,10},{3,11},{4,12},{5,13},{6,14},{7,15},{8,0},{9,1},... | collective-permute-start | bytes 32 | tf_op jit(solution)/shard_map/ppermute | solution.py:39
  96.9 2.8 %collective-permute-start.16 = (f32[4,16,128]{2,1,0:T(8,128)S(1)}, f32[4,16,128]{2,1,0:T(8,128)S(1)}, u32[]{:S(2)}, u32[]{:S(2)}) collective-permute-start(f32[4,16,128]{2,1,0:T(8,128)S(1)} %add.119), channel_id=1, source_target_pairs={{0,3},{1,2},{2,1},{3,0},{4,7},{5,6},{6,5},{7,4},{8,9},{9,8},{10,11... | collective-permute-start | bytes 98312 | tf_op jit(solution)/shard_map/ppermute | solution.py:39
  99.7 3.1 %collective-permute-start.17 = (f32[4,16,128]{2,1,0:T(8,128)S(1)}, f32[4,16,128]{2,1,0:T(8,128)S(1)}, u32[]{:S(2)}, u32[]{:S(2)}) collective-permute-start(f32[4,16,128]{2,1,0:T(8,128)S(1)} %add.120), channel_id=1, source_target_pairs={{0,4},{1,5},{2,6},{3,7},{4,0},{5,1},{6,2},{7,3},{8,12},{9,13},{10,... | collective-permute-start | bytes 98312 | tf_op jit(solution)/shard_map/ppermute | solution.py:39
  102.8 4.1 %collective-permute-start.20 = (bf16[9,16,128]{2,1,0:T(8,128)(2,1)S(1)}, bf16[9,16,128]{2,1,0:T(8,128)(2,1)S(1)}, u32[]{:S(2)}, u32[]{:S(2)}) collective-permute-start(bf16[9,16,128]{2,1,0:T(8,128)(2,1)S(1)} %get-tuple-element.18), channel_id=1, source_target_pairs={{0,16},{1,17},{2,18},{3,19},{4,20},{5,21},{6,22},{7,23},{8,56},{9,... | collective-permute-start | bytes 110600 | tf_op jit(solution)/shard_map/ppermute | solution.py:39
  105.1 7.7 %collective-permute-start.18 = (f32[4,16,128]{2,1,0:T(8,128)S(1)}, f32[4,16,128]{2,1,0:T(8,128)S(1)}, u32[]{:S(2)}, u32[]{:S(2)}) collective-permute-start(f32[4,16,128]{2,1,0:T(8,128)S(1)} %get-tuple-element.10), channel_id=1, source_target_pairs={{0,8},{1,9},{2,10},{3,11},{4,12},{5,13},{6,14},{7,15},{8,0},{9,1},... | collective-permute-start | bytes 98312 | tf_op jit(solution)/shard_map/ppermute | solution.py:39
  107.0 3.5 %collective-permute-start.21 = (bf16[2,9,16,128]{3,2,1,0:T(8,128)(2,1)S(1)}, bf16[2,9,16,128]{3,2,1,0:T(8,128)(2,1)S(1)}, u32[]{:S(2)}, u32[]{:S(2)}) collective-permute-start(bf16[2,9,16,128]{3,2,1,0:T(8,128)(2,1)S(1)} %pad_maximum_fusion.2), channel_id=1, source_target_pairs={{0,48},{1,49},{2,50},{3,51},{4,52},{5,53},{6,54},{7,55},{8,24},{9,... | collective-permute-start | bytes 221192 | tf_op jit(solution)/shard_map/ppermute | solution.py:39
  110.5 5.4 %collective-permute-start.22 = (bf16[4,9,16,128]{3,2,1,0:T(8,128)(2,1)S(1)}, bf16[4,9,16,128]{3,2,1,0:T(8,128)(2,1)S(1)}, u32[]{:S(2)}, u32[]{:S(2)}) collective-permute-start(bf16[4,9,16,128]{3,2,1,0:T(8,128)(2,1)S(1)} %pad_maximum_fusion.1), channel_id=1, source_target_pairs={{0,68},{1,69},{2,70},{3,71},{4,64},{5,65},{6,66},{7,67},{8,76},{9,... | collective-permute-start | bytes 442376 | tf_op jit(solution)/shard_map/ppermute | solution.py:39
  117.2 7.8 %collective-permute-start.23 = (f32[2,32,32]{1,2,0:T(8,128)S(1)}, f32[2,32,32]{1,2,0:T(8,128)S(1)}, u32[]{:S(2)}, u32[]{:S(2)}) collective-permute-start(f32[2,32,32]{1,2,0:T(8,128)S(1)} %fusion.8), channel_id=1, source_target_pairs={{0,8},{1,9},{2,10},{3,11},{4,12},{5,13},{6,14},{7,15},{8,0},{9,1},... | collective-permute-start | bytes 24584 | tf_op jit(solution)/shard_map/ppermute | solution.py:39
  (13 other events, 67.4 us)

commit v3 on v2

--- a/solution.py
+++ b/solution.py
@@ -133,7 +133,7 @@
     )(counts, gate, up, grad, inp, din_t, dout_t, uin_t, later_than)
 
 
-def back_kernel(n, has_acc, last, has_first, lo, later, cols, *refs):
+def back_kernel(n, has_acc, last, lo, later, cols, *refs):
     i = pl.program_id(0)
     half = pl.num_programs(0) // 2
     refs = list(refs)
@@ -154,12 +154,12 @@
         gate = rest[side][:, lo : lo + width]
         delta = (acc * silu(gate.astype(F32))).astype(BF16)
         del_rows = lax.dot_general(delta, rest[2][:, lo : lo + width], NT, preferred_element_type=F32)
-        second = outer(rest[3 + side][...], del_rows)
+        second = outer(rest[3 + 2 * side][...] + rest[4 + 2 * side][...], del_rows)
         packed = jnp.concatenate([second[:32], second[32:]], axis=1)
 
         @pl.when(i % (512 // TILE) == 0)
         def _():
-            out[0] = packed + rest[5][0] if has_first else packed
+            out[0] = packed
 
         @pl.when(i % (512 // TILE) != 0)
         def _():
@@ -199,25 +199,25 @@
         out_shape = jax.ShapeDtypeStruct((2 * tokens, width), F32)
         out_spec = acc_spec
     else:
-        gate_mine, gate_theirs, proj, rows_mine, rows_theirs, first = tail
-        hid = gate_mine.shape[1] // 2
-        args += [gate_mine, gate_theirs, proj, rows_mine, rows_theirs]
+        hid = tail[0].shape[1] // 2
+        args += tail
+        mine_rows = pl.BlockSpec((64, TILE), lambda i, s: (0, own_row(i)))
+        their_rows = pl.BlockSpec((64, TILE), lambda i, s: (0, other_row(i)))
         specs += [
             pl.BlockSpec((TILE, hid), lambda i, s: (own_row(i), s[8])),
             pl.BlockSpec((TILE, hid), lambda i, s: (other_row(i), s[8])),
             pl.BlockSpec((64, hid), lambda i, s: (0, s[8])),
-            pl.BlockSpec((64, TILE), lambda i, s: (0, own_row(i))),
-            pl.BlockSpec((64, TILE), lambda i, s: (0, other_row(i))),
+            mine_rows,
+            mine_rows,
+            their_rows,
+            their_rows,
         ]
         out_spec = pl.BlockSpec((1, 32, 128), lambda i, s: ((i // (512 // TILE) + 2 * s[8]) % 4, 0, 0))
-        if first is not None:
-            args.append(first)
-            specs.append(out_spec)
         out_shape = jax.ShapeDtypeStruct((4, 32, 128), F32)
     args += later
     specs += [pl.BlockSpec(memory_space=pl.ANY)] * len(later)
     return pl.pallas_call(
-        functools.partial(back_kernel, n, acc is not None, tail is not None, tail is not None and tail[5] is not None, lo, len(later)),
+        functools.partial(back_kernel, n, acc is not None, tail is not None, lo, len(later)),
         out_shape=out_shape,
         grid_spec=pltpu.PrefetchScalarGridSpec(
             num_scalar_prefetch=1, grid=(2 * steps,), in_specs=specs, out_specs=out_spec
@@ -283,11 +283,11 @@
     h_xy = after(h_xy, acc)
     h_xyy = swap_y(h_xy, 1)
     rows = rows + after(rows_second, acc)
-    rows_third = swap_x(rows, 0)
+    rows_x = swap_x(rows, 0)
+    rows_core = swap_core(rows)
+    rows_x_core = moved(rows, lambda x, y, z, c: (pair(x, 0), y, z, 1 - c))
     acc = back_step(cols, acc, [(h_yy, 4), (h_xy2, 5), (h_xy, 6)], both, later=(rows,))
-    rows = rows + after(rows_third, acc)
-    rows_other = swap_core(rows)
-    tail = (gate, gate_other, up_out_proj.T, rows, rows_other, None)
+    tail = (gate, gate_other, up_out_proj.T, rows, rows_x, rows_core, rows_x_core)
     second = back_step(cols, acc, [(h_xyy, 7)], both, tail, 0)
 
     second_other = swap_core(second)
@@ -296,16 +296,16 @@
     mine = mine + swap_z(mine, 1)
     mine = mine + swap_x(mine, 0)
 
-    first = rows[:, tokens:].reshape(ex_dev, 32, 128)
-    first_other = rows_other[:, tokens:].reshape(ex_dev, 32, 128)
+    first = (rows[:, tokens:] + rows_x[:, tokens:]).reshape(ex_dev, 32, 128)
+    first_other = (rows_core[:, tokens:] + rows_x_core[:, tokens:]).reshape(ex_dev, 32, 128)
     first_all = jnp.where(is_even, jnp.concatenate([first, first_other]), jnp.concatenate([first_other, first]))
     first_half = lax.dynamic_slice_in_dim(first_all, core * 16, 16, 1)
     ids = jnp.where(is_even, jnp.concatenate([assignment, ids_other]), jnp.concatenate([ids_other, assignment]))
     ids_block = jnp.broadcast_to(jnp.pad(ids, (0, 12))[None, :, None], (1, 16, 128)).astype(BF16)
     load = jnp.concatenate([first_half.astype(BF16), mine.astype(BF16), ids_block])
-    load = jnp.stack([load, swap_y(load, 0)])
+    load = jnp.stack([load, swap_x(load, 1)])
+    load = jnp.concatenate([load, swap_y(load, 0)])
     load = jnp.concatenate([load, swap_y(load, 1)])
-    load = jnp.concatenate([load, swap_x(load, 1)])
 
     mine_other = swap_core(mine)
     own = lax.dynamic_slice_in_dim(mine, core * ex_dev, ex_dev, 0)

time: 127 us -> 124 us (0.976)
  local copies, waits for them, and re-layouts: 10 us -> 6.12 us
  waiting for transfers between devices: 18.5 us -> 20 us
    unnamed x27 -> x23, local copies, waits for them, and re-layouts: 5.08 us -> 2.61 us
    ppermute x24 -> x25, waiting for transfers between devices: 18.5 us -> 20 us  [moved(): lax.ppermute(value, AXES, [(i, index(*to(*coords(i)))) for i in range(128)])]
    slice x2 -> x0, local copies, waits for them, and re-layouts: 1.52 us -> none  [the longest x1 0.76 us: body(): first = rows[:, tokens:].reshape(ex_dev, 32, 128)]
    ppermute x24 -> x25, starting transfers between devices: 39.8 us -> 39.1 us  [moved(): lax.ppermute(value, AXES, [(i, index(*to(*coords(i)))) for i in range(128)])]
  transfers between devices with their start and end apart: 24 -> 25, of which waited for: 11 -> 9; matrix products, arithmetic and copies ran while one was open for 7% -> 6% of each run, Pallas kernels for 31% -> 41%
where the time goes in v3:
time: 124 us
  Pallas kernels  50.6 us (41%)
  starting transfers between devices  39.1 us (32%)
  waiting for transfers between devices  20 us (16%)
  local copies, waits for them, and re-layouts  6.12 us (5%)
  other arithmetic  5.09 us (4%)
  matrix products  1.58 us (1%)
    pallas_call x3, Pallas kernels, back_step(): pl.pallas_call(functools.partial(back_kernel, n, acc is not None, tail is...  39.9 us
    ppermute x25, starting transfers between devices, moved(): lax.ppermute(value, AXES, [(i, index(*to(*coords(i)))) for i in range(128)])  39.1 us
    ppermute x25, waiting for transfers between devices, moved(): lax.ppermute(value, AXES, [(i, index(*to(*coords(i)))) for i in range(128)])  20 us
    pallas_call x1, Pallas kernels, projected_rows(): pl.pallas_call(rows_kernel, out_shape=jax.ShapeDtypeStruct((64, tokens +...  10.8 us
    unnamed x23, local copies, waits for them, and re-layouts  2.61 us
  transfers between devices with their start and end apart: 25, of which 9 were waited for; matrix products, arithmetic and copies ran while one was open for 6% of the time, Pallas kernels for 41%

profile of v3, /device:TPU:1, one launch (start us, length us, event | category | flops | bytes accessed | tf_op | source)
XLA Modules:
  0.0 123.5 jit_solution(10249104645941879941)
XLA Ops:
  0.6 1.5 %collective-permute-start = (bf16[1792,256]{1,0:T(8,128)(2,1)}, bf16[1792,256]{1,0:T(8,128)(2,1)S(1)}, u32[]{:S(2)}, u32[]{:S(2)}) collective-permute-start(bf16[1792,256]{1,0:T(8,128)(2,1)} %param.16), channel_id=1, source_target_pairs={{0,8},{1,9},{2,10},{3,11},{4,12},{5,13},{6,14},{7,15},{8,0},{9,1},... | collective-permute-start | bytes 2752520 | tf_op jit(solution)/shard_map/ppermute | solution.py:39
  2.2 1.2 fusion.24
  3.4 1.4 %collective-permute-done = bf16[1792,256]{1,0:T(8,128)(2,1)S(1)} collective-permute-done((bf16[1792,256]{1,0:T(8,128)(2,1)}, bf16[1792,256]{1,0:T(8,128)(2,1)S(1)}, u32[]{:S(2)}, u32[]{:S(2)}) %collective-permute-start) | collective-permute-done | bytes 917536 | tf_op jit(solution)/shard_map/ppermute | solution.py:39
  5.1 2.9 %collective-permute-start.4 = (bf16[896,512]{1,0:T(8,128)(2,1)S(1)}, bf16[896,512]{1,0:T(8,128)(2,1)}, u32[]{:S(2)}, u32[]{:S(2)}) collective-permute-start(bf16[896,512]{1,0:T(8,128)(2,1)S(1)} %maximum_select_fusion._.refs_2_), channel_id=1, source_target_pairs={{0,16},{1,17},{2,18},{3,19},{4,20},{5,21},{6,22},{7,23},{8,56},{9,... | collective-permute-start | bytes 2752520 | tf_op jit(solution)/shard_map/ppermute | solution.py:39
  8.0 2.7 %collective-permute-start.6 = (bf16[896,512]{1,0:T(8,128)(2,1)S(1)}, bf16[896,512]{1,0:T(8,128)(2,1)}, u32[]{:S(2)}, u32[]{:S(2)}) collective-permute-start(bf16[896,512]{1,0:T(8,128)(2,1)S(1)} %maximum_select_fusion._.refs_2_), channel_id=1, source_target_pairs={{0,64},{1,65},{2,66},{3,67},{4,68},{5,69},{6,70},{7,71},{8,72},{9,... | collective-permute-start | bytes 2752520 | tf_op jit(solution)/shard_map/ppermute | solution.py:39
  10.8 10.8 %early_rows.1.refs_1_ = f32[64,1152]{1,0:T(8,128)} custom-call(s32[2]{0:T(128)} %counts.1, bf16[1024,1792]{1,0:T(8,128)(2,1)} %bitcast.63, bf16[1024,1792]{1,0:T(8,128)(2,1)} %bitcast.62, bf16[1024,4096]{1,0:T(8,128)(2,1)} %bitcast.53, bf16[1024,512]{1,0:T(8,128)(2,1)} %bitcast.66, bf16[64,1792]{1,0:T(8,128)(2,1)} %bitcast.68, bf16[64,4096]{1,0:T(8,128)(2,1)} %bitcast.67, ...), custom_call_target="tpu_custom_call" | custom-call | flops 99999997952 | bytes 100000000 | tf_op jit(solution)/shard_map/early_rows/pallas_call | solution.py:121
  21.5 3.8 %collective-permute-start.1 = (f32[64,1152]{1,0:T(8,128)}, f32[64,1152]{1,0:T(8,128)S(1)}, u32[]{:S(2)}, u32[]{:S(2)}) collective-permute-start(f32[64,1152]{1,0:T(8,128)} %early_rows.1.refs_1_), channel_id=1, source_target_pairs={{0,1},{1,0},{2,3},{3,2},{4,5},{5,4},{6,7},{7,6},{8,11},{9,10},{10,... | collective-permute-start | bytes 884744 | tf_op jit(solution)/shard_map/ppermute | solution.py:39
  26.0 4.0 %collective-permute-done.1 = f32[64,1152]{1,0:T(8,128)S(1)} collective-permute-done((f32[64,1152]{1,0:T(8,128)}, f32[64,1152]{1,0:T(8,128)S(1)}, u32[]{:S(2)}, u32[]{:S(2)}) %collective-permute-start.1) | collective-permute-done | bytes 294944 | tf_op jit(solution)/shard_map/ppermute | solution.py:39
  31.2 1.7 %collective-permute-start.2 = (f32[64,1152]{1,0:T(8,128)S(1)}, f32[64,1152]{1,0:T(8,128)S(1)}, u32[]{:S(2)}, u32[]{:S(2)}) collective-permute-start(f32[64,1152]{1,0:T(8,128)S(1)} %add.102.refs_12_), channel_id=1, source_target_pairs={{0,3},{1,2},{2,1},{3,0},{4,7},{5,6},{6,5},{7,4},{8,9},{9,8},{10,11... | collective-permute-start | bytes 884744 | tf_op jit(solution)/shard_map/ppermute | solution.py:39
  33.5 1.9 %collective-permute-start.9 = (bf16[896,512]{1,0:T(8,128)(2,1)}, bf16[896,512]{1,0:T(8,128)(2,1)}, u32[]{:S(2)}, u32[]{:S(2)}) collective-permute-start(bf16[896,512]{1,0:T(8,128)(2,1)} %after.7.refs_11_), channel_id=1, source_target_pairs={{0,48},{1,49},{2,50},{3,51},{4,52},{5,53},{6,54},{7,55},{8,24},{9,... | collective-permute-start | bytes 2752520 | tf_op jit(solution)/shard_map/ppermute | solution.py:39
  35.5 15.1 %back_part.2.refs_1_.refs_0_ = f32[2048,896]{1,0:T(8,128)} custom-call(s32[9]{0:T(128)} %stack.54.cols, bf16[1024,4096]{1,0:T(8,128)(2,1)} %bitcast.54, bf16[1024,4096]{1,0:T(8,128)(2,1)} %collective-permute-done.3.refs_1_.refs_4_.refs_7_.refs_10_.refs_2_.refs_5_.refs_8_, bf16[896,512]{1,0:T(8,128)(2,1)} %copy-done.4, bf16[1024,4096]{1,0:T(8,128)(2,1)} %bitcast.55, ...), custom_call_target="tpu_custom_call" | custom-call | flops 99999997952 | bytes 100000000 | tf_op jit(solution)/shard_map/back_part/pallas_call | solution.py:219
  53.8 4.5 %collective-permute-start.13 = (f32[64,1152]{1,0:T(8,128)S(1)}, f32[64,1152]{1,0:T(8,128)S(1)}, u32[]{:S(2)}, u32[]{:S(2)}) collective-permute-start(f32[64,1152]{1,0:T(8,128)S(1)} %add.118.refs_10_.refs_7_), channel_id=1, source_target_pairs={{0,8},{1,9},{2,10},{3,11},{4,12},{5,13},{6,14},{7,15},{8,0},{9,1},... | collective-permute-start | bytes 884744 | tf_op jit(solution)/shard_map/ppermute | solution.py:39
  58.3 1.5 %collective-permute-start.14 = (f32[64,1152]{1,0:T(8,128)S(1)}, f32[64,1152]{1,0:T(8,128)S(1)}, u32[]{:S(2)}, u32[]{:S(2)}) collective-permute-start(f32[64,1152]{1,0:T(8,128)S(1)} %add.118.refs_10_.refs_7_), channel_id=1, source_target_pairs={{0,12},{1,13},{2,14},{3,15},{4,8},{5,9},{6,10},{7,11},{8,4},{9,5},... | collective-permute-start | bytes 884744 | tf_op jit(solution)/shard_map/ppermute | solution.py:39
  59.8 1.7 %collective-permute-start.11 = (bf16[896,512]{1,0:T(8,128)(2,1)}, bf16[896,512]{1,0:T(8,128)(2,1)}, u32[]{:S(2)}, u32[]{:S(2)}) collective-permute-start(bf16[896,512]{1,0:T(8,128)(2,1)} %after.9.refs_9_), channel_id=1, source_target_pairs={{0,48},{1,49},{2,50},{3,51},{4,52},{5,53},{6,54},{7,55},{8,24},{9,... | collective-permute-start | bytes 2752520 | tf_op jit(solution)/shard_map/ppermute | solution.py:39
  61.6 13.9 %back_part.3.refs_0_ = f32[2048,896]{1,0:T(8,128)} custom-call(s32[9]{0:T(128)} %stack.54.cols, f32[2048,896]{1,0:T(8,128)} %back_part.2.refs_1_.refs_0_, bf16[1024,4096]{1,0:T(8,128)(2,1)} %bitcast.58, bf16[1024,4096]{1,0:T(8,128)(2,1)} %collective-permute-done.3.refs_1_.refs_4_.refs_7_.refs_10_.refs_2_.refs_5_.refs_8_, ...), custom_call_target="tpu_custom_call" | custom-call | flops 99999997952 | bytes 100000000 | tf_op jit(solution)/shard_map/back_part/pallas_call | solution.py:219
  76.7 10.8 %back_last.1 = f32[4,32,128]{2,1,0:T(8,128)} custom-call(s32[9]{0:T(128)} %stack.54.cols, f32[2048,896]{1,0:T(8,128)} %back_part.3.refs_0_, bf16[1024,4096]{1,0:T(8,128)(2,1)} %bitcast.61, bf16[1024,4096]{1,0:T(8,128)(2,1)} %collective-permute-done.3.refs_1_.refs_4_.refs_7_.refs_10_.refs_2_.refs_5_.refs_8_, ...), custom_call_target="tpu_custom_call" | custom-call | flops 99999997952 | bytes 100000000 | tf_op jit(solution)/shard_map/back_last/pallas_call | solution.py:219
  89.8 3.1 %collective-permute-start.16 = (f32[4,16,128]{2,1,0:T(8,128)S(1)}, f32[4,16,128]{2,1,0:T(8,128)S(1)}, u32[]{:S(2)}, u32[]{:S(2)}) collective-permute-start(f32[4,16,128]{2,1,0:T(8,128)S(1)} %dynamic-slice_add_fusion), channel_id=1, source_target_pairs={{0,1},{1,0},{2,3},{3,2},{4,5},{5,4},{6,7},{7,6},{8,11},{9,10},{10,... | collective-permute-start | bytes 98312 | tf_op jit(solution)/shard_map/ppermute | solution.py:39
  95.0 2.0 %collective-permute-done.17 = f32[4,16,128]{2,1,0:T(8,128)S(1)} collective-permute-done((f32[4,16,128]{2,1,0:T(8,128)S(1)}, f32[4,16,128]{2,1,0:T(8,128)S(1)}, u32[]{:S(2)}, u32[]{:S(2)}) %collective-permute-start.17) | collective-permute-done | bytes 32800 | tf_op jit(solution)/shard_map/ppermute | solution.py:39
  97.4 2.4 %collective-permute-done.18 = f32[4,16,128]{2,1,0:T(8,128)S(1)} collective-permute-done((f32[4,16,128]{2,1,0:T(8,128)S(1)}, f32[4,16,128]{2,1,0:T(8,128)S(1)}, u32[]{:S(2)}, u32[]{:S(2)}) %collective-permute-start.18) | collective-permute-done | bytes 32800 | tf_op jit(solution)/shard_map/ppermute | solution.py:39
  99.9 1.9 %collective-permute-start.21 = (bf16[9,16,128]{2,1,0:T(8,128)(2,1)S(1)}, bf16[9,16,128]{2,1,0:T(8,128)(2,1)S(1)}, u32[]{:S(2)}, u32[]{:S(2)}) collective-permute-start(bf16[9,16,128]{2,1,0:T(8,128)(2,1)S(1)} %get-tuple-element.18), channel_id=1, source_target_pairs={{0,68},{1,69},{2,70},{3,71},{4,64},{5,65},{6,66},{7,67},{8,76},{9,... | collective-permute-start | bytes 110600 | tf_op jit(solution)/shard_map/ppermute | solution.py:39
  101.9 3.9 %collective-permute-start.19 = (f32[4,16,128]{2,1,0:T(8,128)S(1)}, f32[4,16,128]{2,1,0:T(8,128)S(1)}, u32[]{:S(2)}, u32[]{:S(2)}) collective-permute-start(f32[4,16,128]{2,1,0:T(8,128)S(1)} %get-tuple-element.10), channel_id=1, source_target_pairs={{0,8},{1,9},{2,10},{3,11},{4,12},{5,13},{6,14},{7,15},{8,0},{9,1},... | collective-permute-start | bytes 98312 | tf_op jit(solution)/shard_map/ppermute | solution.py:39
  106.2 4.1 %collective-permute-done.22 = bf16[2,9,16,128]{3,2,1,0:T(8,128)(2,1)S(1)} collective-permute-done((bf16[2,9,16,128]{3,2,1,0:T(8,128)(2,1)S(1)}, bf16[2,9,16,128]{3,2,1,0:T(8,128)(2,1)S(1)}, u32[]{:S(2)}, u32[]{:S(2)}) %collective-permute-start.22) | collective-permute-done | bytes 73760 | tf_op jit(solution)/shard_map/ppermute | solution.py:39
  110.5 3.8 %collective-permute-done.23 = bf16[4,9,16,128]{3,2,1,0:T(8,128)(2,1)S(1)} collective-permute-done((bf16[4,9,16,128]{3,2,1,0:T(8,128)(2,1)S(1)}, bf16[4,9,16,128]{3,2,1,0:T(8,128)(2,1)S(1)}, u32[]{:S(2)}, u32[]{:S(2)}) %collective-permute-start.23) | collective-permute-done | bytes 147488 | tf_op jit(solution)/shard_map/ppermute | solution.py:39
  115.7 5.3 %collective-permute-start.24 = (f32[2,32,32]{1,2,0:T(8,128)S(1)}, f32[2,32,32]{1,2,0:T(8,128)S(1)}, u32[]{:S(2)}, u32[]{:S(2)}) collective-permute-start(f32[2,32,32]{1,2,0:T(8,128)S(1)} %fusion.8), channel_id=1, source_target_pairs={{0,8},{1,9},{2,10},{3,11},{4,12},{5,13},{6,14},{7,15},{8,0},{9,1},... | collective-permute-start | bytes 24584 | tf_op jit(solution)/shard_map/ppermute | solution.py:39
  (100 shorter events, 16.6 us)
Async XLA Ops:
  0.6 4.2 %collective-permute-start = (bf16[1792,256]{1,0:T(8,128)(2,1)}, bf16[1792,256]{1,0:T(8,128)(2,1)S(1)}, u32[]{:S(2)}, u32[]{:S(2)}) collective-permute-start(bf16[1792,256]{1,0:T(8,128)(2,1)} %param.16), channel_id=1, source_target_pairs={{0,8},{1,9},{2,10},{3,11},{4,12},{5,13},{6,14},{7,15},{8,0},{9,1},... | collective-permute-start | bytes 2752520 | tf_op jit(solution)/shard_map/ppermute | solution.py:39
  2.1 31.4 %collective-permute-start.3 = (bf16[1024,4096]{1,0:T(8,128)(2,1)}, bf16[1024,4096]{1,0:T(8,128)(2,1)}, u32[]{:S(2)}, u32[]{:S(2)}) collective-permute-start(bf16[1024,4096]{1,0:T(8,128)(2,1)} %bitcast.52), channel_id=1, source_target_pairs={{0,8},{1,9},{2,10},{3,11},{4,12},{5,13},{6,14},{7,15},{8,0},{9,1},... | collective-permute-start | bytes 25165832 | tf_op jit(solution)/shard_map/ppermute | solution.py:39
  5.1 26.0 %collective-permute-start.4 = (bf16[896,512]{1,0:T(8,128)(2,1)S(1)}, bf16[896,512]{1,0:T(8,128)(2,1)}, u32[]{:S(2)}, u32[]{:S(2)}) collective-permute-start(bf16[896,512]{1,0:T(8,128)(2,1)S(1)} %maximum_select_fusion._.refs_2_), channel_id=1, source_target_pairs={{0,16},{1,17},{2,18},{3,19},{4,20},{5,21},{6,22},{7,23},{8,56},{9,... | collective-permute-start | bytes 2752520 | tf_op jit(solution)/shard_map/ppermute | solution.py:39
  8.0 24.9 %collective-permute-start.5 = (bf16[896,512]{1,0:T(8,128)(2,1)S(1)}, bf16[896,512]{1,0:T(8,128)(2,1)}, u32[]{:S(2)}, u32[]{:S(2)}) collective-permute-start(bf16[896,512]{1,0:T(8,128)(2,1)S(1)} %maximum_select_fusion._.refs_2_), channel_id=1, source_target_pairs={{0,48},{1,49},{2,50},{3,51},{4,52},{5,53},{6,54},{7,55},{8,24},{9,... | collective-permute-start | bytes 2752520 | tf_op jit(solution)/shard_map/ppermute | solution.py:39
  8.0 25.3 %collective-permute-start.6 = (bf16[896,512]{1,0:T(8,128)(2,1)S(1)}, bf16[896,512]{1,0:T(8,128)(2,1)}, u32[]{:S(2)}, u32[]{:S(2)}) collective-permute-start(bf16[896,512]{1,0:T(8,128)(2,1)S(1)} %maximum_select_fusion._.refs_2_), channel_id=1, source_target_pairs={{0,64},{1,65},{2,66},{3,67},{4,68},{5,69},{6,70},{7,71},{8,72},{9,... | collective-permute-start | bytes 2752520 | tf_op jit(solution)/shard_map/ppermute | solution.py:39
  21.5 8.5 %collective-permute-start.1 = (f32[64,1152]{1,0:T(8,128)}, f32[64,1152]{1,0:T(8,128)S(1)}, u32[]{:S(2)}, u32[]{:S(2)}) collective-permute-start(f32[64,1152]{1,0:T(8,128)} %early_rows.1.refs_1_), channel_id=1, source_target_pairs={{0,1},{1,0},{2,3},{3,2},{4,5},{5,4},{6,7},{7,6},{8,11},{9,10},{10,... | collective-permute-start | bytes 884744 | tf_op jit(solution)/shard_map/ppermute | solution.py:39
  30.0 45.5 %collective-permute-start.12 = (bf16[1024,1792]{1,0:T(8,128)(2,1)}, bf16[1024,1792]{1,0:T(8,128)(2,1)}, u32[]{:S(2)}, u32[]{:S(2)}) collective-permute-start(bf16[1024,1792]{1,0:T(8,128)(2,1)} %bitcast.64), channel_id=1, source_target_pairs={{0,8},{1,9},{2,10},{3,11},{4,12},{5,13},{6,14},{7,15},{8,0},{9,1},... | collective-permute-start | bytes 11010056 | tf_op jit(solution)/shard_map/ppermute | solution.py:39
  31.2 19.4 %collective-permute-start.2 = (f32[64,1152]{1,0:T(8,128)S(1)}, f32[64,1152]{1,0:T(8,128)S(1)}, u32[]{:S(2)}, u32[]{:S(2)}) collective-permute-start(f32[64,1152]{1,0:T(8,128)S(1)} %add.102.refs_12_), channel_id=1, source_target_pairs={{0,3},{1,2},{2,1},{3,0},{4,7},{5,6},{6,5},{7,4},{8,9},{9,8},{10,11... | collective-permute-start | bytes 884744 | tf_op jit(solution)/shard_map/ppermute | solution.py:39
  32.9 25.4 %collective-permute-start.8 = (bf16[896,512]{1,0:T(8,128)(2,1)}, bf16[896,512]{1,0:T(8,128)(2,1)}, u32[]{:S(2)}, u32[]{:S(2)}) collective-permute-start(bf16[896,512]{1,0:T(8,128)(2,1)} %after.5.refs_5_), channel_id=1, source_target_pairs={{0,48},{1,49},{2,50},{3,51},{4,52},{5,53},{6,54},{7,55},{8,24},{9,... | collective-permute-start | bytes 2752520 | tf_op jit(solution)/shard_map/ppermute | solution.py:39
  33.3 20.5 %collective-permute-start.10 = (bf16[896,512]{1,0:T(8,128)(2,1)}, bf16[896,512]{1,0:T(8,128)(2,1)S(1)}, u32[]{:S(2)}, u32[]{:S(2)}) collective-permute-start(bf16[896,512]{1,0:T(8,128)(2,1)} %after.5.refs_5_), channel_id=1, source_target_pairs={{0,64},{1,65},{2,66},{3,67},{4,68},{5,69},{6,70},{7,71},{8,72},{9,... | collective-permute-start | bytes 2752520 | tf_op jit(solution)/shard_map/ppermute | solution.py:39
  33.5 26.3 %collective-permute-start.9 = (bf16[896,512]{1,0:T(8,128)(2,1)}, bf16[896,512]{1,0:T(8,128)(2,1)}, u32[]{:S(2)}, u32[]{:S(2)}) collective-permute-start(bf16[896,512]{1,0:T(8,128)(2,1)} %after.7.refs_11_), channel_id=1, source_target_pairs={{0,48},{1,49},{2,50},{3,51},{4,52},{5,53},{6,54},{7,55},{8,24},{9,... | collective-permute-start | bytes 2752520 | tf_op jit(solution)/shard_map/ppermute | solution.py:39
  52.7 23.1 %collective-permute-start.7 = (f32[64,1152]{1,0:T(8,128)S(1)}, f32[64,1152]{1,0:T(8,128)S(1)}, u32[]{:S(2)}, u32[]{:S(2)}) collective-permute-start(f32[64,1152]{1,0:T(8,128)S(1)} %add.118.refs_10_.refs_7_), channel_id=1, source_target_pairs={{0,4},{1,5},{2,6},{3,7},{4,0},{5,1},{6,2},{7,3},{8,12},{9,13},{10,... | collective-permute-start | bytes 884744 | tf_op jit(solution)/shard_map/ppermute | solution.py:39
  53.8 22.0 %collective-permute-start.13 = (f32[64,1152]{1,0:T(8,128)S(1)}, f32[64,1152]{1,0:T(8,128)S(1)}, u32[]{:S(2)}, u32[]{:S(2)}) collective-permute-start(f32[64,1152]{1,0:T(8,128)S(1)} %add.118.refs_10_.refs_7_), channel_id=1, source_target_pairs={{0,8},{1,9},{2,10},{3,11},{4,12},{5,13},{6,14},{7,15},{8,0},{9,1},... | collective-permute-start | bytes 884744 | tf_op jit(solution)/shard_map/ppermute | solution.py:39
  58.3 17.5 %collective-permute-start.14 = (f32[64,1152]{1,0:T(8,128)S(1)}, f32[64,1152]{1,0:T(8,128)S(1)}, u32[]{:S(2)}, u32[]{:S(2)}) collective-permute-start(f32[64,1152]{1,0:T(8,128)S(1)} %add.118.refs_10_.refs_7_), channel_id=1, source_target_pairs={{0,12},{1,13},{2,14},{3,15},{4,8},{5,9},{6,10},{7,11},{8,4},{9,5},... | collective-permute-start | bytes 884744 | tf_op jit(solution)/shard_map/ppermute | solution.py:39
  59.8 16.0 %collective-permute-start.11 = (bf16[896,512]{1,0:T(8,128)(2,1)}, bf16[896,512]{1,0:T(8,128)(2,1)}, u32[]{:S(2)}, u32[]{:S(2)}) collective-permute-start(bf16[896,512]{1,0:T(8,128)(2,1)} %after.9.refs_9_), channel_id=1, source_target_pairs={{0,48},{1,49},{2,50},{3,51},{4,52},{5,53},{6,54},{7,55},{8,24},{9,... | collective-permute-start | bytes 2752520 | tf_op jit(solution)/shard_map/ppermute | solution.py:39
  75.5 12.5 %collective-permute-start.20 = (s32[2]{0:T(128)S(1)}, s32[2]{0:T(128)S(1)}, u32[]{:S(2)}, u32[]{:S(2)}) collective-permute-start(s32[2]{0:T(128)S(1)} %copy-done.9), channel_id=1, source_target_pairs={{0,8},{1,9},{2,10},{3,11},{4,12},{5,13},{6,14},{7,15},{8,0},{9,1},... | collective-permute-start | bytes 32 | tf_op jit(solution)/shard_map/ppermute | solution.py:39
  89.8 4.4 %collective-permute-start.16 = (f32[4,16,128]{2,1,0:T(8,128)S(1)}, f32[4,16,128]{2,1,0:T(8,128)S(1)}, u32[]{:S(2)}, u32[]{:S(2)}) collective-permute-start(f32[4,16,128]{2,1,0:T(8,128)S(1)} %dynamic-slice_add_fusion), channel_id=1, source_target_pairs={{0,1},{1,0},{2,3},{3,2},{4,5},{5,4},{6,7},{7,6},{8,11},{9,10},{10,... | collective-permute-start | bytes 98312 | tf_op jit(solution)/shard_map/ppermute | solution.py:39
  94.2 2.8 %collective-permute-start.17 = (f32[4,16,128]{2,1,0:T(8,128)S(1)}, f32[4,16,128]{2,1,0:T(8,128)S(1)}, u32[]{:S(2)}, u32[]{:S(2)}) collective-permute-start(f32[4,16,128]{2,1,0:T(8,128)S(1)} %add.122), channel_id=1, source_target_pairs={{0,3},{1,2},{2,1},{3,0},{4,7},{5,6},{6,5},{7,4},{8,9},{9,8},{10,11... | collective-permute-start | bytes 98312 | tf_op jit(solution)/shard_map/ppermute | solution.py:39
  97.0 2.8 %collective-permute-start.18 = (f32[4,16,128]{2,1,0:T(8,128)S(1)}, f32[4,16,128]{2,1,0:T(8,128)S(1)}, u32[]{:S(2)}, u32[]{:S(2)}) collective-permute-start(f32[4,16,128]{2,1,0:T(8,128)S(1)} %add.123), channel_id=1, source_target_pairs={{0,4},{1,5},{2,6},{3,7},{4,0},{5,1},{6,2},{7,3},{8,12},{9,13},{10,... | collective-permute-start | bytes 98312 | tf_op jit(solution)/shard_map/ppermute | solution.py:39
  99.9 5.9 %collective-permute-start.21 = (bf16[9,16,128]{2,1,0:T(8,128)(2,1)S(1)}, bf16[9,16,128]{2,1,0:T(8,128)(2,1)S(1)}, u32[]{:S(2)}, u32[]{:S(2)}) collective-permute-start(bf16[9,16,128]{2,1,0:T(8,128)(2,1)S(1)} %get-tuple-element.18), channel_id=1, source_target_pairs={{0,68},{1,69},{2,70},{3,71},{4,64},{5,65},{6,66},{7,67},{8,76},{9,... | collective-permute-start | bytes 110600 | tf_op jit(solution)/shard_map/ppermute | solution.py:39
  101.9 8.5 %collective-permute-start.19 = (f32[4,16,128]{2,1,0:T(8,128)S(1)}, f32[4,16,128]{2,1,0:T(8,128)S(1)}, u32[]{:S(2)}, u32[]{:S(2)}) collective-permute-start(f32[4,16,128]{2,1,0:T(8,128)S(1)} %get-tuple-element.10), channel_id=1, source_target_pairs={{0,8},{1,9},{2,10},{3,11},{4,12},{5,13},{6,14},{7,15},{8,0},{9,1},... | collective-permute-start | bytes 98312 | tf_op jit(solution)/shard_map/ppermute | solution.py:39
  105.8 4.5 %collective-permute-start.22 = (bf16[2,9,16,128]{3,2,1,0:T(8,128)(2,1)S(1)}, bf16[2,9,16,128]{3,2,1,0:T(8,128)(2,1)S(1)}, u32[]{:S(2)}, u32[]{:S(2)}) collective-permute-start(bf16[2,9,16,128]{3,2,1,0:T(8,128)(2,1)S(1)} %pad_maximum_fusion.2), channel_id=1, source_target_pairs={{0,16},{1,17},{2,18},{3,19},{4,20},{5,21},{6,22},{7,23},{8,56},{9,... | collective-permute-start | bytes 221192 | tf_op jit(solution)/shard_map/ppermute | solution.py:39
  110.3 4.1 %collective-permute-start.23 = (bf16[4,9,16,128]{3,2,1,0:T(8,128)(2,1)S(1)}, bf16[4,9,16,128]{3,2,1,0:T(8,128)(2,1)S(1)}, u32[]{:S(2)}, u32[]{:S(2)}) collective-permute-start(bf16[4,9,16,128]{3,2,1,0:T(8,128)(2,1)S(1)} %pad_maximum_fusion.1), channel_id=1, source_target_pairs={{0,48},{1,49},{2,50},{3,51},{4,52},{5,53},{6,54},{7,55},{8,24},{9,... | collective-permute-start | bytes 442376 | tf_op jit(solution)/shard_map/ppermute | solution.py:39
  115.7 6.1 %collective-permute-start.24 = (f32[2,32,32]{1,2,0:T(8,128)S(1)}, f32[2,32,32]{1,2,0:T(8,128)S(1)}, u32[]{:S(2)}, u32[]{:S(2)}) collective-permute-start(f32[2,32,32]{1,2,0:T(8,128)S(1)} %fusion.8), channel_id=1, source_target_pairs={{0,8},{1,9},{2,10},{3,11},{4,12},{5,13},{6,14},{7,15},{8,0},{9,1},... | collective-permute-start | bytes 24584 | tf_op jit(solution)/shard_map/ppermute | solution.py:39
  (12 other events, 81.3 us)

commit v4 on v3

--- a/solution.py
+++ b/solution.py
@@ -14,7 +14,8 @@
 EARLY_TILE = 256
 NT = (((1,), (1,)), ((), ()))
 CHUNKS = ((0, 896),)
-VMEM_LIMIT = 62 * 2**20
+VMEM_LIMIT = 60 * 2**20
+BACK_LIMIT = 50 * 2**20
 LONG = pl.CostEstimate(flops=10**11, bytes_accessed=10**8, transcendentals=0)
 
 
@@ -137,6 +138,8 @@
     i = pl.program_id(0)
     half = pl.num_programs(0) // 2
     refs = list(refs)
+    if not last:
+        refs.pop()[...] = jnp.zeros((8, 128), F32)
     acc_ref = refs.pop(0) if has_acc else None
     refs = refs[:len(refs) - 1 - later] + refs[-1:]
     blocks, rest = refs[: 3 * n], refs[3 * n :]
@@ -196,8 +199,8 @@
         ]
     n = len(pieces)
     if tail is None:
-        out_shape = jax.ShapeDtypeStruct((2 * tokens, width), F32)
-        out_spec = acc_spec
+        out_shape = (jax.ShapeDtypeStruct((2 * tokens, width), F32), jax.ShapeDtypeStruct((8, 128), F32))
+        out_spec = (acc_spec, pl.BlockSpec((8, 128), lambda i, s: (0, 0)))
     else:
         hid = tail[0].shape[1] // 2
         args += tail
@@ -222,7 +225,8 @@
         grid_spec=pltpu.PrefetchScalarGridSpec(
             num_scalar_prefetch=1, grid=(2 * steps,), in_specs=specs, out_specs=out_spec
         ),
-        compiler_params=pltpu.CompilerParams(vmem_limit_bytes=VMEM_LIMIT),
+        input_output_aliases={1: 0} if acc is not None and tail is None else {},
+        compiler_params=pltpu.CompilerParams(vmem_limit_bytes=BACK_LIMIT),
         cost_estimate=LONG,
         name="back_last" if tail is not None else "back_part",
     )(cols, *args)
@@ -278,15 +282,15 @@
     h_xy2 = swap_y(h_x, 1)
     rows = early + swap_z(early, 0)
     rows_second = swap_z(rows, 1)
-    acc = back_step(cols, None, [(h, 0), (h_y, 1), (h_y2, 2), (h_x, 3)], both, later=(rows,))
-
-    h_xy = after(h_xy, acc)
+    acc, done = back_step(cols, None, [(h, 0), (h_y, 1), (h_y2, 2), (h_x, 3)], both, later=(rows,))
+
+    h_xy = after(h_xy, done)
     h_xyy = swap_y(h_xy, 1)
-    rows = rows + after(rows_second, acc)
+    rows = rows + after(rows_second, done)
     rows_x = swap_x(rows, 0)
     rows_core = swap_core(rows)
     rows_x_core = moved(rows, lambda x, y, z, c: (pair(x, 0), y, z, 1 - c))
-    acc = back_step(cols, acc, [(h_yy, 4), (h_xy2, 5), (h_xy, 6)], both, later=(rows,))
+    acc, _ = back_step(cols, acc, [(h_yy, 4), (h_xy2, 5), (h_xy, 6)], both, later=(rows,))
     tail = (gate, gate_other, up_out_proj.T, rows, rows_x, rows_core, rows_x_core)
     second = back_step(cols, acc, [(h_xyy, 7)], both, tail, 0)
 

time: 124 us -> 124 us (level)
  local copies, waits for them, and re-layouts: 6.12 us -> 9.69 us
  Pallas kernels: 50.6 us -> 47.8 us
  waiting for transfers between devices: 20 us -> 21.8 us
  other arithmetic: 5.09 us -> 3.74 us
  starting transfers between devices: 39.1 us -> 37.8 us
    unnamed x23 -> x27, local copies, waits for them, and re-layouts: 2.61 us -> 6.78 us
    pallas_call x3, Pallas kernels: 39.9 us -> 37.1 us  [back_step(): pl.pallas_call(functools.partial(back_kernel, n, acc is not None, tail is...]
    ppermute x25, waiting for transfers between devices: 20 us -> 21.8 us  [moved(): lax.ppermute(value, AXES, [(i, index(*to(*coords(i)))) for i in range(128)])]
    ppermute x25, starting transfers between devices: 39.1 us -> 37.8 us  [moved(): lax.ppermute(value, AXES, [(i, index(*to(*coords(i)))) for i in range(128)])]
  transfers between devices with their start and end apart: 25 -> 25, of which waited for: 9 -> 8; matrix products, arithmetic and copies ran while one was open for 6% -> 5% of each run, Pallas kernels for 41% -> 39%
where the time goes in v4:
time: 124 us; the launch traced here: 123 us
  Pallas kernels  47.8 us (39%)
  starting transfers between devices  37.8 us (30%)
  waiting for transfers between devices  21.8 us (18%)
  local copies, waits for them, and re-layouts  9.69 us (8%)
  other arithmetic  3.74 us (3%)
  matrix products  1.58 us (1%)
    ppermute x25, starting transfers between devices, moved(): lax.ppermute(value, AXES, [(i, index(*to(*coords(i)))) for i in range(128)])  37.8 us
    pallas_call x3, Pallas kernels, back_step(): pl.pallas_call(functools.partial(back_kernel, n, acc is not None, tail is...  37.1 us
    ppermute x25, waiting for transfers between devices, moved(): lax.ppermute(value, AXES, [(i, index(*to(*coords(i)))) for i in range(128)])  21.8 us
    pallas_call x1, Pallas kernels, projected_rows(): pl.pallas_call(rows_kernel, out_shape=jax.ShapeDtypeStruct((64, tokens +...  10.8 us
    unnamed x27, local copies, waits for them, and re-layouts  6.78 us
  transfers between devices with their start and end apart: 25, of which 8 were waited for; matrix products, arithmetic and copies ran while one was open for 5% of the time, Pallas kernels for 39%

profile of v4, /device:TPU:1, one launch (start us, length us, event | category | flops | bytes accessed | tf_op | source)
XLA Modules:
  0.0 123.3 jit_solution(1866345309937639981)
XLA Ops:
  0.6 1.5 %collective-permute-start = (bf16[1792,256]{1,0:T(8,128)(2,1)}, bf16[1792,256]{1,0:T(8,128)(2,1)S(1)}, u32[]{:S(2)}, u32[]{:S(2)}) collective-permute-start(bf16[1792,256]{1,0:T(8,128)(2,1)} %param.16), channel_id=1, source_target_pairs={{0,8},{1,9},{2,10},{3,11},{4,12},{5,13},{6,14},{7,15},{8,0},{9,1},... | collective-permute-start | bytes 2752520 | tf_op jit(solution)/shard_map/ppermute | solution.py:40
  2.2 1.2 fusion.24
  3.4 1.4 %collective-permute-done = bf16[1792,256]{1,0:T(8,128)(2,1)S(1)} collective-permute-done((bf16[1792,256]{1,0:T(8,128)(2,1)}, bf16[1792,256]{1,0:T(8,128)(2,1)S(1)}, u32[]{:S(2)}, u32[]{:S(2)}) %collective-permute-start) | collective-permute-done | bytes 917536 | tf_op jit(solution)/shard_map/ppermute | solution.py:40
  6.1 2.8 %collective-permute-start.4 = (bf16[896,512]{1,0:T(8,128)(2,1)}, bf16[896,512]{1,0:T(8,128)(2,1)S(1)}, u32[]{:S(2)}, u32[]{:S(2)}) collective-permute-start(bf16[896,512]{1,0:T(8,128)(2,1)} %maximum_select_fusion._.refs_2_), channel_id=1, source_target_pairs={{0,16},{1,17},{2,18},{3,19},{4,20},{5,21},{6,22},{7,23},{8,56},{9,... | collective-permute-start | bytes 2752520 | tf_op jit(solution)/shard_map/ppermute | solution.py:40
  8.9 2.7 %collective-permute-start.6 = (bf16[896,512]{1,0:T(8,128)(2,1)}, bf16[896,512]{1,0:T(8,128)(2,1)S(1)}, u32[]{:S(2)}, u32[]{:S(2)}) collective-permute-start(bf16[896,512]{1,0:T(8,128)(2,1)} %maximum_select_fusion._.refs_2_), channel_id=1, source_target_pairs={{0,64},{1,65},{2,66},{3,67},{4,68},{5,69},{6,70},{7,71},{8,72},{9,... | collective-permute-start | bytes 2752520 | tf_op jit(solution)/shard_map/ppermute | solution.py:40
  11.6 10.8 %early_rows.1.refs_1_ = f32[64,1152]{1,0:T(8,128)} custom-call(s32[2]{0:T(128)} %counts.1, bf16[1024,1792]{1,0:T(8,128)(2,1)} %bitcast.64, bf16[1024,1792]{1,0:T(8,128)(2,1)} %bitcast.63, bf16[1024,4096]{1,0:T(8,128)(2,1)} %bitcast.54, bf16[1024,512]{1,0:T(8,128)(2,1)} %bitcast.67, bf16[64,1792]{1,0:T(8,128)(2,1)} %bitcast.69, bf16[64,4096]{1,0:T(8,128)(2,1)} %bitcast.68, ...), custom_call_target="tpu_custom_call" | custom-call | flops 99999997952 | bytes 100000000 | tf_op jit(solution)/shard_map/early_rows/pallas_call | solution.py:122
  22.4 3.8 %collective-permute-start.1 = (f32[64,1152]{1,0:T(8,128)}, f32[64,1152]{1,0:T(8,128)S(1)}, u32[]{:S(2)}, u32[]{:S(2)}) collective-permute-start(f32[64,1152]{1,0:T(8,128)} %early_rows.1.refs_1_), channel_id=1, source_target_pairs={{0,1},{1,0},{2,3},{3,2},{4,5},{5,4},{6,7},{7,6},{8,11},{9,10},{10,... | collective-permute-start | bytes 884744 | tf_op jit(solution)/shard_map/ppermute | solution.py:40
  26.2 4.5 %collective-permute-done.1 = f32[64,1152]{1,0:T(8,128)S(1)} collective-permute-done((f32[64,1152]{1,0:T(8,128)}, f32[64,1152]{1,0:T(8,128)S(1)}, u32[]{:S(2)}, u32[]{:S(2)}) %collective-permute-start.1) | collective-permute-done | bytes 294944 | tf_op jit(solution)/shard_map/ppermute | solution.py:40
  32.0 1.7 %collective-permute-start.2 = (f32[64,1152]{1,0:T(8,128)S(1)}, f32[64,1152]{1,0:T(8,128)S(1)}, u32[]{:S(2)}, u32[]{:S(2)}) collective-permute-start(f32[64,1152]{1,0:T(8,128)S(1)} %add.102.refs_12_), channel_id=1, source_target_pairs={{0,3},{1,2},{2,1},{3,0},{4,7},{5,6},{6,5},{7,4},{8,9},{9,8},{10,11... | collective-permute-start | bytes 884744 | tf_op jit(solution)/shard_map/ppermute | solution.py:40
  38.8 14.2 %back_part.2 = (f32[2048,896]{1,0:T(8,128)}, f32[8,128]{1,0:T(8,128)S(1)}) custom-call(s32[9]{0:T(128)S(1)} %stack.54.cols, bf16[1024,4096]{1,0:T(8,128)(2,1)} %bitcast.55, bf16[1024,4096]{1,0:T(8,128)(2,1)} %collective-permute-done.3.refs_1_.refs_4_.refs_7_.refs_10_.refs_2_.refs_5_.refs_8_, bf16[896,512]{1,0:T(8,128)(2,1)} %maximum_select_fusion._.refs_2_, ...), custom_call_target="tpu_custom_call" | custom-call | flops 99999997952 | bytes 100000000 | tf_op jit(solution)/shard_map/back_part/pallas_call | solution.py:222
  55.8 4.7 %collective-permute-start.13 = (f32[64,1152]{1,0:T(8,128)S(1)}, f32[64,1152]{1,0:T(8,128)S(1)}, u32[]{:S(2)}, u32[]{:S(2)}) collective-permute-start(f32[64,1152]{1,0:T(8,128)S(1)} %add.118.refs_10_.refs_7_), channel_id=1, source_target_pairs={{0,8},{1,9},{2,10},{3,11},{4,12},{5,13},{6,14},{7,15},{8,0},{9,1},... | collective-permute-start | bytes 884744 | tf_op jit(solution)/shard_map/ppermute | solution.py:40
  60.6 1.4 %collective-permute-start.14 = (f32[64,1152]{1,0:T(8,128)S(1)}, f32[64,1152]{1,0:T(8,128)S(1)}, u32[]{:S(2)}, u32[]{:S(2)}) collective-permute-start(f32[64,1152]{1,0:T(8,128)S(1)} %add.118.refs_10_.refs_7_), channel_id=1, source_target_pairs={{0,12},{1,13},{2,14},{3,15},{4,8},{5,9},{6,10},{7,11},{8,4},{9,5},... | collective-permute-start | bytes 884744 | tf_op jit(solution)/shard_map/ppermute | solution.py:40
  62.0 1.2 copy-done.1
  63.2 13.5 %back_part.3 = (f32[2048,896]{1,0:T(8,128)}, f32[8,128]{1,0:T(8,128)}) custom-call(s32[9]{0:T(128)S(1)} %stack.54.cols, f32[2048,896]{1,0:T(8,128)} %get-tuple-element.7.refs_0_, bf16[1024,4096]{1,0:T(8,128)(2,1)} %bitcast.59, ...), custom_call_target="tpu_custom_call", output_to_operand_aliasing={{0}: (1, {})} | custom-call | flops 99999997952 | bytes 100000000 | tf_op jit(solution)/shard_map/back_part/pallas_call | solution.py:222
  76.7 2.0 %collective-permute-start.20 = (s32[2]{0:T(128)S(1)}, s32[2]{0:T(128)S(1)}, u32[]{:S(2)}, u32[]{:S(2)}) collective-permute-start(s32[2]{0:T(128)S(1)} %copy-done.11), channel_id=1, source_target_pairs={{0,8},{1,9},{2,10},{3,11},{4,12},{5,13},{6,14},{7,15},{8,0},{9,1},... | collective-permute-start | bytes 32 | tf_op jit(solution)/shard_map/ppermute | solution.py:40
  78.8 9.4 %back_last.1 = f32[4,32,128]{2,1,0:T(8,128)S(1)} custom-call(s32[9]{0:T(128)S(1)} %stack.54.cols, f32[2048,896]{1,0:T(8,128)} %get-tuple-element.8.refs_0_, bf16[1024,4096]{1,0:T(8,128)(2,1)} %bitcast.62, bf16[1024,4096]{1,0:T(8,128)(2,1)} %collective-permute-done.3.refs_1_.refs_4_.refs_7_.refs_10_.refs_2_.refs_5_.refs_8_, ...), custom_call_target="tpu_custom_call" | custom-call | flops 99999997952 | bytes 100000000 | tf_op jit(solution)/shard_map/back_last/pallas_call | solution.py:222
  90.4 3.1 %collective-permute-done.16 = f32[4,16,128]{2,1,0:T(8,128)S(1)} collective-permute-done((f32[4,16,128]{2,1,0:T(8,128)S(1)}, f32[4,16,128]{2,1,0:T(8,128)S(1)}, u32[]{:S(2)}, u32[]{:S(2)}) %collective-permute-start.16) | collective-permute-done | bytes 32800 | tf_op jit(solution)/shard_map/ppermute | solution.py:40
  93.6 2.7 %collective-permute-done.17 = f32[4,16,128]{2,1,0:T(8,128)S(1)} collective-permute-done((f32[4,16,128]{2,1,0:T(8,128)S(1)}, f32[4,16,128]{2,1,0:T(8,128)S(1)}, u32[]{:S(2)}, u32[]{:S(2)}) %collective-permute-start.17) | collective-permute-done | bytes 32800 | tf_op jit(solution)/shard_map/ppermute | solution.py:40
  96.9 2.1 %collective-permute-done.18 = f32[4,16,128]{2,1,0:T(8,128)S(1)} collective-permute-done((f32[4,16,128]{2,1,0:T(8,128)S(1)}, f32[4,16,128]{2,1,0:T(8,128)S(1)}, u32[]{:S(2)}, u32[]{:S(2)}) %collective-permute-start.18) | collective-permute-done | bytes 32800 | tf_op jit(solution)/shard_map/ppermute | solution.py:40
  100.4 4.0 %collective-permute-start.19 = (f32[4,16,128]{2,1,0:T(8,128)S(1)}, f32[4,16,128]{2,1,0:T(8,128)S(1)}, u32[]{:S(2)}, u32[]{:S(2)}) collective-permute-start(f32[4,16,128]{2,1,0:T(8,128)S(1)} %get-tuple-element.16), channel_id=1, source_target_pairs={{0,8},{1,9},{2,10},{3,11},{4,12},{5,13},{6,14},{7,15},{8,0},{9,1},... | collective-permute-start | bytes 98312 | tf_op jit(solution)/shard_map/ppermute | solution.py:40
  104.4 1.9 %collective-permute-start.22 = (bf16[2,9,16,128]{3,2,1,0:T(8,128)(2,1)S(1)}, bf16[2,9,16,128]{3,2,1,0:T(8,128)(2,1)S(1)}, u32[]{:S(2)}, u32[]{:S(2)}) collective-permute-start(bf16[2,9,16,128]{3,2,1,0:T(8,128)(2,1)S(1)} %pad_maximum_fusion.2), channel_id=1, source_target_pairs={{0,16},{1,17},{2,18},{3,19},{4,20},{5,21},{6,22},{7,23},{8,56},{9,... | collective-permute-start | bytes 221192 | tf_op jit(solution)/shard_map/ppermute | solution.py:40
  106.4 2.5 %collective-permute-done.22 = bf16[2,9,16,128]{3,2,1,0:T(8,128)(2,1)S(1)} collective-permute-done((bf16[2,9,16,128]{3,2,1,0:T(8,128)(2,1)S(1)}, bf16[2,9,16,128]{3,2,1,0:T(8,128)(2,1)S(1)}, u32[]{:S(2)}, u32[]{:S(2)}) %collective-permute-start.22) | collective-permute-done | bytes 73760 | tf_op jit(solution)/shard_map/ppermute | solution.py:40
  109.2 4.2 %collective-permute-done.23 = bf16[4,9,16,128]{3,2,1,0:T(8,128)(2,1)S(1)} collective-permute-done((bf16[4,9,16,128]{3,2,1,0:T(8,128)(2,1)S(1)}, bf16[4,9,16,128]{3,2,1,0:T(8,128)(2,1)S(1)}, u32[]{:S(2)}, u32[]{:S(2)}) %collective-permute-start.23) | collective-permute-done | bytes 147488 | tf_op jit(solution)/shard_map/ppermute | solution.py:40
  114.7 6.1 %collective-permute-start.24 = (f32[2,32,32]{1,2,0:T(8,128)S(1)}, f32[2,32,32]{1,2,0:T(8,128)S(1)}, u32[]{:S(2)}, u32[]{:S(2)}) collective-permute-start(f32[2,32,32]{1,2,0:T(8,128)S(1)} %fusion.8), channel_id=1, source_target_pairs={{0,8},{1,9},{2,10},{3,11},{4,12},{5,13},{6,14},{7,15},{8,0},{9,1},... | collective-permute-start | bytes 24584 | tf_op jit(solution)/shard_map/ppermute | solution.py:40
  (104 shorter events, 18.9 us)
Async XLA Ops:
  0.6 4.2 %collective-permute-start = (bf16[1792,256]{1,0:T(8,128)(2,1)}, bf16[1792,256]{1,0:T(8,128)(2,1)S(1)}, u32[]{:S(2)}, u32[]{:S(2)}) collective-permute-start(bf16[1792,256]{1,0:T(8,128)(2,1)} %param.16), channel_id=1, source_target_pairs={{0,8},{1,9},{2,10},{3,11},{4,12},{5,13},{6,14},{7,15},{8,0},{9,1},... | collective-permute-start | bytes 2752520 | tf_op jit(solution)/shard_map/ppermute | solution.py:40
  2.1 33.5 %collective-permute-start.3 = (bf16[1024,4096]{1,0:T(8,128)(2,1)}, bf16[1024,4096]{1,0:T(8,128)(2,1)}, u32[]{:S(2)}, u32[]{:S(2)}) collective-permute-start(bf16[1024,4096]{1,0:T(8,128)(2,1)} %bitcast.53), channel_id=1, source_target_pairs={{0,8},{1,9},{2,10},{3,11},{4,12},{5,13},{6,14},{7,15},{8,0},{9,1},... | collective-permute-start | bytes 25165832 | tf_op jit(solution)/shard_map/ppermute | solution.py:40
  6.1 25.9 %collective-permute-start.4 = (bf16[896,512]{1,0:T(8,128)(2,1)}, bf16[896,512]{1,0:T(8,128)(2,1)S(1)}, u32[]{:S(2)}, u32[]{:S(2)}) collective-permute-start(bf16[896,512]{1,0:T(8,128)(2,1)} %maximum_select_fusion._.refs_2_), channel_id=1, source_target_pairs={{0,16},{1,17},{2,18},{3,19},{4,20},{5,21},{6,22},{7,23},{8,56},{9,... | collective-permute-start | bytes 2752520 | tf_op jit(solution)/shard_map/ppermute | solution.py:40
  8.9 24.9 %collective-permute-start.5 = (bf16[896,512]{1,0:T(8,128)(2,1)}, bf16[896,512]{1,0:T(8,128)(2,1)S(1)}, u32[]{:S(2)}, u32[]{:S(2)}) collective-permute-start(bf16[896,512]{1,0:T(8,128)(2,1)} %maximum_select_fusion._.refs_2_), channel_id=1, source_target_pairs={{0,48},{1,49},{2,50},{3,51},{4,52},{5,53},{6,54},{7,55},{8,24},{9,... | collective-permute-start | bytes 2752520 | tf_op jit(solution)/shard_map/ppermute | solution.py:40
  8.9 25.8 %collective-permute-start.6 = (bf16[896,512]{1,0:T(8,128)(2,1)}, bf16[896,512]{1,0:T(8,128)(2,1)S(1)}, u32[]{:S(2)}, u32[]{:S(2)}) collective-permute-start(bf16[896,512]{1,0:T(8,128)(2,1)} %maximum_select_fusion._.refs_2_), channel_id=1, source_target_pairs={{0,64},{1,65},{2,66},{3,67},{4,68},{5,69},{6,70},{7,71},{8,72},{9,... | collective-permute-start | bytes 2752520 | tf_op jit(solution)/shard_map/ppermute | solution.py:40
  22.4 8.4 %collective-permute-start.1 = (f32[64,1152]{1,0:T(8,128)}, f32[64,1152]{1,0:T(8,128)S(1)}, u32[]{:S(2)}, u32[]{:S(2)}) collective-permute-start(f32[64,1152]{1,0:T(8,128)} %early_rows.1.refs_1_), channel_id=1, source_target_pairs={{0,1},{1,0},{2,3},{3,2},{4,5},{5,4},{6,7},{7,6},{8,11},{9,10},{10,... | collective-permute-start | bytes 884744 | tf_op jit(solution)/shard_map/ppermute | solution.py:40
  30.8 45.9 %collective-permute-start.12 = (bf16[1024,1792]{1,0:T(8,128)(2,1)}, bf16[1024,1792]{1,0:T(8,128)(2,1)}, u32[]{:S(2)}, u32[]{:S(2)}) collective-permute-start(bf16[1024,1792]{1,0:T(8,128)(2,1)} %bitcast.65), channel_id=1, source_target_pairs={{0,8},{1,9},{2,10},{3,11},{4,12},{5,13},{6,14},{7,15},{8,0},{9,1},... | collective-permute-start | bytes 11010056 | tf_op jit(solution)/shard_map/ppermute | solution.py:40
  32.0 21.6 %collective-permute-start.2 = (f32[64,1152]{1,0:T(8,128)S(1)}, f32[64,1152]{1,0:T(8,128)S(1)}, u32[]{:S(2)}, u32[]{:S(2)}) collective-permute-start(f32[64,1152]{1,0:T(8,128)S(1)} %add.102.refs_12_), channel_id=1, source_target_pairs={{0,3},{1,2},{2,1},{3,0},{4,7},{5,6},{6,5},{7,4},{8,9},{9,8},{10,11... | collective-permute-start | bytes 884744 | tf_op jit(solution)/shard_map/ppermute | solution.py:40
  33.8 26.8 %collective-permute-start.8 = (bf16[896,512]{1,0:T(8,128)(2,1)}, bf16[896,512]{1,0:T(8,128)(2,1)}, u32[]{:S(2)}, u32[]{:S(2)}) collective-permute-start(bf16[896,512]{1,0:T(8,128)(2,1)} %after.5.refs_5_), channel_id=1, source_target_pairs={{0,48},{1,49},{2,50},{3,51},{4,52},{5,53},{6,54},{7,55},{8,24},{9,... | collective-permute-start | bytes 2752520 | tf_op jit(solution)/shard_map/ppermute | solution.py:40
  34.7 21.1 %collective-permute-start.10 = (bf16[896,512]{1,0:T(8,128)(2,1)}, bf16[896,512]{1,0:T(8,128)(2,1)S(1)}, u32[]{:S(2)}, u32[]{:S(2)}) collective-permute-start(bf16[896,512]{1,0:T(8,128)(2,1)} %after.5.refs_5_), channel_id=1, source_target_pairs={{0,64},{1,65},{2,66},{3,67},{4,68},{5,69},{6,70},{7,71},{8,72},{9,... | collective-permute-start | bytes 2752520 | tf_op jit(solution)/shard_map/ppermute | solution.py:40
  35.7 26.3 %collective-permute-start.9 = (bf16[896,512]{1,0:T(8,128)(2,1)}, bf16[896,512]{1,0:T(8,128)(2,1)}, u32[]{:S(2)}, u32[]{:S(2)}) collective-permute-start(bf16[896,512]{1,0:T(8,128)(2,1)} %after.7.refs_11_), channel_id=1, source_target_pairs={{0,48},{1,49},{2,50},{3,51},{4,52},{5,53},{6,54},{7,55},{8,24},{9,... | collective-permute-start | bytes 2752520 | tf_op jit(solution)/shard_map/ppermute | solution.py:40
  55.3 23.4 %collective-permute-start.7 = (f32[64,1152]{1,0:T(8,128)S(1)}, f32[64,1152]{1,0:T(8,128)S(1)}, u32[]{:S(2)}, u32[]{:S(2)}) collective-permute-start(f32[64,1152]{1,0:T(8,128)S(1)} %add.118.refs_10_.refs_7_), channel_id=1, source_target_pairs={{0,4},{1,5},{2,6},{3,7},{4,0},{5,1},{6,2},{7,3},{8,12},{9,13},{10,... | collective-permute-start | bytes 884744 | tf_op jit(solution)/shard_map/ppermute | solution.py:40
  55.8 23.0 %collective-permute-start.13 = (f32[64,1152]{1,0:T(8,128)S(1)}, f32[64,1152]{1,0:T(8,128)S(1)}, u32[]{:S(2)}, u32[]{:S(2)}) collective-permute-start(f32[64,1152]{1,0:T(8,128)S(1)} %add.118.refs_10_.refs_7_), channel_id=1, source_target_pairs={{0,8},{1,9},{2,10},{3,11},{4,12},{5,13},{6,14},{7,15},{8,0},{9,1},... | collective-permute-start | bytes 884744 | tf_op jit(solution)/shard_map/ppermute | solution.py:40
  60.6 18.2 %collective-permute-start.14 = (f32[64,1152]{1,0:T(8,128)S(1)}, f32[64,1152]{1,0:T(8,128)S(1)}, u32[]{:S(2)}, u32[]{:S(2)}) collective-permute-start(f32[64,1152]{1,0:T(8,128)S(1)} %add.118.refs_10_.refs_7_), channel_id=1, source_target_pairs={{0,12},{1,13},{2,14},{3,15},{4,8},{5,9},{6,10},{7,11},{8,4},{9,5},... | collective-permute-start | bytes 884744 | tf_op jit(solution)/shard_map/ppermute | solution.py:40
  62.0 16.8 %collective-permute-start.11 = (bf16[896,512]{1,0:T(8,128)(2,1)}, bf16[896,512]{1,0:T(8,128)(2,1)S(1)}, u32[]{:S(2)}, u32[]{:S(2)}) collective-permute-start(bf16[896,512]{1,0:T(8,128)(2,1)} %after.9.refs_9_), channel_id=1, source_target_pairs={{0,48},{1,49},{2,50},{3,51},{4,52},{5,53},{6,54},{7,55},{8,24},{9,... | collective-permute-start | bytes 2752520 | tf_op jit(solution)/shard_map/ppermute | solution.py:40
  76.7 11.6 %collective-permute-start.20 = (s32[2]{0:T(128)S(1)}, s32[2]{0:T(128)S(1)}, u32[]{:S(2)}, u32[]{:S(2)}) collective-permute-start(s32[2]{0:T(128)S(1)} %copy-done.11), channel_id=1, source_target_pairs={{0,8},{1,9},{2,10},{3,11},{4,12},{5,13},{6,14},{7,15},{8,0},{9,1},... | collective-permute-start | bytes 32 | tf_op jit(solution)/shard_map/ppermute | solution.py:40
  89.5 4.0 %collective-permute-start.16 = (f32[4,16,128]{2,1,0:T(8,128)S(1)}, f32[4,16,128]{2,1,0:T(8,128)S(1)}, u32[]{:S(2)}, u32[]{:S(2)}) collective-permute-start(f32[4,16,128]{2,1,0:T(8,128)S(1)} %dynamic-slice_add_fusion), channel_id=1, source_target_pairs={{0,1},{1,0},{2,3},{3,2},{4,5},{5,4},{6,7},{7,6},{8,11},{9,10},{10,... | collective-permute-start | bytes 98312 | tf_op jit(solution)/shard_map/ppermute | solution.py:40
  93.5 2.8 %collective-permute-start.17 = (f32[4,16,128]{2,1,0:T(8,128)S(1)}, f32[4,16,128]{2,1,0:T(8,128)S(1)}, u32[]{:S(2)}, u32[]{:S(2)}) collective-permute-start(f32[4,16,128]{2,1,0:T(8,128)S(1)} %add.122), channel_id=1, source_target_pairs={{0,3},{1,2},{2,1},{3,0},{4,7},{5,6},{6,5},{7,4},{8,9},{9,8},{10,11... | collective-permute-start | bytes 98312 | tf_op jit(solution)/shard_map/ppermute | solution.py:40
  96.3 2.8 %collective-permute-start.18 = (f32[4,16,128]{2,1,0:T(8,128)S(1)}, f32[4,16,128]{2,1,0:T(8,128)S(1)}, u32[]{:S(2)}, u32[]{:S(2)}) collective-permute-start(f32[4,16,128]{2,1,0:T(8,128)S(1)} %add.123), channel_id=1, source_target_pairs={{0,4},{1,5},{2,6},{3,7},{4,0},{5,1},{6,2},{7,3},{8,12},{9,13},{10,... | collective-permute-start | bytes 98312 | tf_op jit(solution)/shard_map/ppermute | solution.py:40
  99.2 5.2 %collective-permute-start.21 = (bf16[9,16,128]{2,1,0:T(8,128)(2,1)S(1)}, bf16[9,16,128]{2,1,0:T(8,128)(2,1)S(1)}, u32[]{:S(2)}, u32[]{:S(2)}) collective-permute-start(bf16[9,16,128]{2,1,0:T(8,128)(2,1)S(1)} %get-tuple-element.24), channel_id=1, source_target_pairs={{0,68},{1,69},{2,70},{3,71},{4,64},{5,65},{6,66},{7,67},{8,76},{9,... | collective-permute-start | bytes 110600 | tf_op jit(solution)/shard_map/ppermute | solution.py:40
  100.4 8.6 %collective-permute-start.19 = (f32[4,16,128]{2,1,0:T(8,128)S(1)}, f32[4,16,128]{2,1,0:T(8,128)S(1)}, u32[]{:S(2)}, u32[]{:S(2)}) collective-permute-start(f32[4,16,128]{2,1,0:T(8,128)S(1)} %get-tuple-element.16), channel_id=1, source_target_pairs={{0,8},{1,9},{2,10},{3,11},{4,12},{5,13},{6,14},{7,15},{8,0},{9,1},... | collective-permute-start | bytes 98312 | tf_op jit(solution)/shard_map/ppermute | solution.py:40
  104.4 4.5 %collective-permute-start.22 = (bf16[2,9,16,128]{3,2,1,0:T(8,128)(2,1)S(1)}, bf16[2,9,16,128]{3,2,1,0:T(8,128)(2,1)S(1)}, u32[]{:S(2)}, u32[]{:S(2)}) collective-permute-start(bf16[2,9,16,128]{3,2,1,0:T(8,128)(2,1)S(1)} %pad_maximum_fusion.2), channel_id=1, source_target_pairs={{0,16},{1,17},{2,18},{3,19},{4,20},{5,21},{6,22},{7,23},{8,56},{9,... | collective-permute-start | bytes 221192 | tf_op jit(solution)/shard_map/ppermute | solution.py:40
  108.9 4.4 %collective-permute-start.23 = (bf16[4,9,16,128]{3,2,1,0:T(8,128)(2,1)S(1)}, bf16[4,9,16,128]{3,2,1,0:T(8,128)(2,1)S(1)}, u32[]{:S(2)}, u32[]{:S(2)}) collective-permute-start(bf16[4,9,16,128]{3,2,1,0:T(8,128)(2,1)S(1)} %pad_maximum_fusion.1), channel_id=1, source_target_pairs={{0,48},{1,49},{2,50},{3,51},{4,52},{5,53},{6,54},{7,55},{8,24},{9,... | collective-permute-start | bytes 442376 | tf_op jit(solution)/shard_map/ppermute | solution.py:40
  114.7 6.9 %collective-permute-start.24 = (f32[2,32,32]{1,2,0:T(8,128)S(1)}, f32[2,32,32]{1,2,0:T(8,128)S(1)}, u32[]{:S(2)}, u32[]{:S(2)}) collective-permute-start(f32[2,32,32]{1,2,0:T(8,128)S(1)} %fusion.8), channel_id=1, source_target_pairs={{0,8},{1,9},{2,10},{3,11},{4,12},{5,13},{6,14},{7,15},{8,0},{9,1},... | collective-permute-start | bytes 24584 | tf_op jit(solution)/shard_map/ppermute | solution.py:40
  (14 other events, 80.5 us)

commit v5 on v4

--- a/solution.py
+++ b/solution.py
@@ -16,6 +16,7 @@
 CHUNKS = ((0, 896),)
 VMEM_LIMIT = 60 * 2**20
 BACK_LIMIT = 50 * 2**20
+SHORT = pl.CostEstimate(flops=46 * 10**8, bytes_accessed=1000, transcendentals=0)
 LONG = pl.CostEstimate(flops=10**11, bytes_accessed=10**8, transcendentals=0)
 
 
@@ -88,6 +89,21 @@
         input_output_aliases={0: 0},
         name="after",
     )(value, *others)
+
+
+def added(left, right):
+    def add(left, right, out):
+        out[...] = left[...] + right[...]
+
+    vmem = pl.BlockSpec(memory_space=pltpu.VMEM)
+    return pl.pallas_call(
+        add,
+        out_shape=jax.ShapeDtypeStruct(left.shape, left.dtype),
+        in_specs=[vmem, vmem],
+        out_specs=vmem,
+        cost_estimate=SHORT,
+        name="added",
+    )(left, right)
 
 
 def rows_kernel(counts, gate, up, grad, inp, din_t, dout_t, uin_t, _, out):
@@ -177,7 +193,7 @@
         run(1)
 
 
-def back_step(cols, acc, pieces, grads, tail=None, lo=0, later=()):
+def back_step(cols, acc, pieces, grads, tail=None, lo=0, later=(), cost=LONG):
     mine, theirs = grads
     tokens = mine.shape[0]
     steps = tokens // TILE
@@ -227,7 +243,7 @@
         ),
         input_output_aliases={1: 0} if acc is not None and tail is None else {},
         compiler_params=pltpu.CompilerParams(vmem_limit_bytes=BACK_LIMIT),
-        cost_estimate=LONG,
+        cost_estimate=cost,
         name="back_last" if tail is not None else "back_part",
     )(cols, *args)
 
@@ -276,13 +292,14 @@
     grads_other = swap_core(grads)
     gate_other = swap_core(gate)
     both = (grads, grads_other)
-    h_y, h_x, h_y2 = after(h_y, early), after(h_x, early), after(h_y2, early)
+    h_y = after(h_y, early)
     h_xy = swap_x_far(h_y)
     h_yy = swap_y(h_y, 1)
+    rows = added(early, swap_z(early, 0))
+    h_x, h_y2 = after(h_x, rows), after(h_y2, rows)
     h_xy2 = swap_y(h_x, 1)
-    rows = early + swap_z(early, 0)
     rows_second = swap_z(rows, 1)
-    acc, done = back_step(cols, None, [(h, 0), (h_y, 1), (h_y2, 2), (h_x, 3)], both, later=(rows,))
+    acc, done = back_step(cols, None, [(h, 0), (h_y, 1), (h_y2, 2), (h_x, 3)], both, later=(rows,), cost=SHORT)
 
     h_xy = after(h_xy, done)
     h_xyy = swap_y(h_xy, 1)

time: 124 us -> 124 us (level)
  starting transfers between devices: 37.8 us -> 33.1 us
  waiting for transfers between devices: 21.8 us -> 24.9 us
  Pallas kernels: 47.8 us -> 49.9 us
    ppermute x25, starting transfers between devices: 37.8 us -> 33.1 us  [moved(): lax.ppermute(value, AXES, [(i, index(*to(*coords(i)))) for i in range(128)])]
    ppermute x25, waiting for transfers between devices: 21.8 us -> 24.9 us  [moved(): lax.ppermute(value, AXES, [(i, index(*to(*coords(i)))) for i in range(128)])]
    pallas_call x0 -> x1, Pallas kernels: none -> 1.81 us  [added(): pl.pallas_call(add, out_shape=jax.ShapeDtypeStruct(left.shape, left.dtype...]
  transfers between devices with their start and end apart: 25 -> 25, of which waited for: 8 -> 9; matrix products, arithmetic and copies ran while one was open for 5% -> 4% of each run, Pallas kernels for 39% -> 40%
where the time goes in v5:
time: 124 us
  Pallas kernels  49.9 us (40%)
  starting transfers between devices  33.1 us (27%)
  waiting for transfers between devices  24.9 us (20%)
  local copies, waits for them, and re-layouts  10.9 us (9%)
  other arithmetic  2.74 us (2%)
  matrix products  1.58 us (1%)
    pallas_call x3, Pallas kernels, back_step(): pl.pallas_call(functools.partial(back_kernel, n, acc is not None, tail is...  37.3 us
    ppermute x25, starting transfers between devices, moved(): lax.ppermute(value, AXES, [(i, index(*to(*coords(i)))) for i in range(128)])  33.1 us
    ppermute x25, waiting for transfers between devices, moved(): lax.ppermute(value, AXES, [(i, index(*to(*coords(i)))) for i in range(128)])  24.9 us
    pallas_call x1, Pallas kernels, projected_rows(): pl.pallas_call(rows_kernel, out_shape=jax.ShapeDtypeStruct((64, tokens +...  10.8 us
    unnamed x27, local copies, waits for them, and re-layouts  7.97 us
  transfers between devices with their start and end apart: 25, of which 9 were waited for; matrix products, arithmetic and copies ran while one was open for 4% of the time, Pallas kernels for 40%

profile of v5, /device:TPU:1, one launch (start us, length us, event | category | flops | bytes accessed | tf_op | source)
XLA Modules:
  0.0 124.0 jit_solution(12770262921772282535)
XLA Ops:
  0.6 1.5 %collective-permute-start = (bf16[1792,256]{1,0:T(8,128)(2,1)}, bf16[1792,256]{1,0:T(8,128)(2,1)S(1)}, u32[]{:S(2)}, u32[]{:S(2)}) collective-permute-start(bf16[1792,256]{1,0:T(8,128)(2,1)} %param.16), channel_id=1, source_target_pairs={{0,8},{1,9},{2,10},{3,11},{4,12},{5,13},{6,14},{7,15},{8,0},{9,1},... | collective-permute-start | bytes 2752520 | tf_op jit(solution)/shard_map/ppermute | solution.py:41
  2.2 1.2 fusion.24
  3.4 1.4 %collective-permute-done = bf16[1792,256]{1,0:T(8,128)(2,1)S(1)} collective-permute-done((bf16[1792,256]{1,0:T(8,128)(2,1)}, bf16[1792,256]{1,0:T(8,128)(2,1)S(1)}, u32[]{:S(2)}, u32[]{:S(2)}) %collective-permute-start) | collective-permute-done | bytes 917536 | tf_op jit(solution)/shard_map/ppermute | solution.py:41
  6.1 2.8 %collective-permute-start.4 = (bf16[896,512]{1,0:T(8,128)(2,1)}, bf16[896,512]{1,0:T(8,128)(2,1)S(1)}, u32[]{:S(2)}, u32[]{:S(2)}) collective-permute-start(bf16[896,512]{1,0:T(8,128)(2,1)} %maximum_select_fusion._.refs_2_), channel_id=1, source_target_pairs={{0,16},{1,17},{2,18},{3,19},{4,20},{5,21},{6,22},{7,23},{8,56},{9,... | collective-permute-start | bytes 2752520 | tf_op jit(solution)/shard_map/ppermute | solution.py:41
  8.9 2.7 %collective-permute-start.6 = (bf16[896,512]{1,0:T(8,128)(2,1)}, bf16[896,512]{1,0:T(8,128)(2,1)S(1)}, u32[]{:S(2)}, u32[]{:S(2)}) collective-permute-start(bf16[896,512]{1,0:T(8,128)(2,1)} %maximum_select_fusion._.refs_2_), channel_id=1, source_target_pairs={{0,64},{1,65},{2,66},{3,67},{4,68},{5,69},{6,70},{7,71},{8,72},{9,... | collective-permute-start | bytes 2752520 | tf_op jit(solution)/shard_map/ppermute | solution.py:41
  11.6 10.8 %early_rows.1.left.refs_1_ = f32[64,1152]{1,0:T(8,128)} custom-call(s32[2]{0:T(128)} %counts.1, bf16[1024,1792]{1,0:T(8,128)(2,1)} %bitcast.64, bf16[1024,1792]{1,0:T(8,128)(2,1)} %bitcast.63, bf16[1024,4096]{1,0:T(8,128)(2,1)} %bitcast.47, bf16[1024,512]{1,0:T(8,128)(2,1)} %bitcast.67, bf16[64,1792]{1,0:T(8,128)(2,1)} %bitcast.69, ...), custom_call_target="tpu_custom_call" | custom-call | flops 99999997952 | bytes 100000000 | tf_op jit(solution)/shard_map/early_rows/pallas_call | solution.py:138
  22.4 3.8 %collective-permute-start.1 = (f32[64,1152]{1,0:T(8,128)}, f32[64,1152]{1,0:T(8,128)S(1)}, u32[]{:S(2)}, u32[]{:S(2)}) collective-permute-start(f32[64,1152]{1,0:T(8,128)} %early_rows.1.left.refs_1_), channel_id=1, source_target_pairs={{0,1},{1,0},{2,3},{3,2},{4,5},{5,4},{6,7},{7,6},{8,11},{9,10},{10,... | collective-permute-start | bytes 884744 | tf_op jit(solution)/shard_map/ppermute | solution.py:41
  27.4 3.4 %collective-permute-done.1.right = f32[64,1152]{1,0:T(8,128)S(1)} collective-permute-done((f32[64,1152]{1,0:T(8,128)}, f32[64,1152]{1,0:T(8,128)S(1)}, u32[]{:S(2)}, u32[]{:S(2)}) %collective-permute-start.1) | collective-permute-done | bytes 294944 | tf_op jit(solution)/shard_map/ppermute | solution.py:41
  31.5 1.8 %added.1.refs_1_.refs_12_ = f32[64,1152]{1,0:T(8,128)} custom-call(f32[64,1152]{1,0:T(8,128)} %early_rows.1.left.refs_1_, f32[64,1152]{1,0:T(8,128)} %copy-done.11), custom_call_target="tpu_custom_call" | custom-call | flops 4600000000 | bytes 1000 | tf_op jit(solution)/shard_map/added/pallas_call | solution.py:99
  34.4 1.5 %collective-permute-start.9 = (bf16[896,512]{1,0:T(8,128)(2,1)}, bf16[896,512]{1,0:T(8,128)(2,1)}, u32[]{:S(2)}, u32[]{:S(2)}) collective-permute-start(bf16[896,512]{1,0:T(8,128)(2,1)} %after.7.refs_11_), channel_id=1, source_target_pairs={{0,48},{1,49},{2,50},{3,51},{4,52},{5,53},{6,54},{7,55},{8,24},{9,... | collective-permute-start | bytes 2752520 | tf_op jit(solution)/shard_map/ppermute | solution.py:41
  35.9 3.1 %collective-permute-done.5.refs_0_ = bf16[896,512]{1,0:T(8,128)(2,1)S(1)} collective-permute-done((bf16[896,512]{1,0:T(8,128)(2,1)}, bf16[896,512]{1,0:T(8,128)(2,1)S(1)}, u32[]{:S(2)}, u32[]{:S(2)}) %collective-permute-start.5) | collective-permute-done | bytes 917536 | tf_op jit(solution)/shard_map/ppermute | solution.py:41
  42.4 14.2 %back_part.2 = (f32[2048,896]{1,0:T(8,128)}, f32[8,128]{1,0:T(8,128)S(1)}) custom-call(s32[9]{0:T(128)S(1)} %stack.54.cols, bf16[1024,4096]{1,0:T(8,128)(2,1)} %bitcast.48, bf16[1024,4096]{1,0:T(8,128)(2,1)} %collective-permute-done.3.refs_1_.refs_4_.refs_7_.refs_10_.refs_2_.refs_5_.refs_8_, bf16[896,512]{1,0:T(8,128)(2,1)} %maximum_select_fusion._.refs_2_, ...), custom_call_target="tpu_custom_call" | custom-call | flops 4600000000 | bytes 1000 | tf_op jit(solution)/shard_map/back_part/pallas_call | solution.py:238
  59.3 2.6 %collective-permute-start.13 = (f32[64,1152]{1,0:T(8,128)S(1)}, f32[64,1152]{1,0:T(8,128)S(1)}, u32[]{:S(2)}, u32[]{:S(2)}) collective-permute-start(f32[64,1152]{1,0:T(8,128)S(1)} %add.114.refs_10_.refs_7_), channel_id=1, source_target_pairs={{0,8},{1,9},{2,10},{3,11},{4,12},{5,13},{6,14},{7,15},{8,0},{9,1},... | collective-permute-start | bytes 884744 | tf_op jit(solution)/shard_map/ppermute | solution.py:41
  62.8 13.8 %back_part.3 = (f32[2048,896]{1,0:T(8,128)}, f32[8,128]{1,0:T(8,128)}) custom-call(s32[9]{0:T(128)S(1)} %stack.54.cols, f32[2048,896]{1,0:T(8,128)} %get-tuple-element.7.refs_0_, bf16[1024,4096]{1,0:T(8,128)(2,1)} %bitcast.52, ...), custom_call_target="tpu_custom_call", output_to_operand_aliasing={{0}: (1, {})} | custom-call | flops 99999997952 | bytes 100000000 | tf_op jit(solution)/shard_map/back_part/pallas_call | solution.py:238
  76.6 2.9 %collective-permute-start.20 = (s32[2]{0:T(128)S(1)}, s32[2]{0:T(128)S(1)}, u32[]{:S(2)}, u32[]{:S(2)}) collective-permute-start(s32[2]{0:T(128)S(1)} %copy-done.10), channel_id=1, source_target_pairs={{0,8},{1,9},{2,10},{3,11},{4,12},{5,13},{6,14},{7,15},{8,0},{9,1},... | collective-permute-start | bytes 32 | tf_op jit(solution)/shard_map/ppermute | solution.py:41
  79.5 9.3 %back_last.1 = f32[4,32,128]{2,1,0:T(8,128)S(1)} custom-call(s32[9]{0:T(128)S(1)} %stack.54.cols, f32[2048,896]{1,0:T(8,128)} %get-tuple-element.8.refs_0_, bf16[1024,4096]{1,0:T(8,128)(2,1)} %bitcast.55, bf16[1024,4096]{1,0:T(8,128)(2,1)} %collective-permute-done.3.refs_1_.refs_4_.refs_7_.refs_10_.refs_2_.refs_5_.refs_8_, ...), custom_call_target="tpu_custom_call" | custom-call | flops 99999997952 | bytes 100000000 | tf_op jit(solution)/shard_map/back_last/pallas_call | solution.py:238
  90.6 3.5 %collective-permute-done.16 = f32[4,16,128]{2,1,0:T(8,128)S(1)} collective-permute-done((f32[4,16,128]{2,1,0:T(8,128)S(1)}, f32[4,16,128]{2,1,0:T(8,128)S(1)}, u32[]{:S(2)}, u32[]{:S(2)}) %collective-permute-start.16) | collective-permute-done | bytes 32800 | tf_op jit(solution)/shard_map/ppermute | solution.py:41
  94.2 2.7 %collective-permute-done.17 = f32[4,16,128]{2,1,0:T(8,128)S(1)} collective-permute-done((f32[4,16,128]{2,1,0:T(8,128)S(1)}, f32[4,16,128]{2,1,0:T(8,128)S(1)}, u32[]{:S(2)}, u32[]{:S(2)}) %collective-permute-start.17) | collective-permute-done | bytes 32800 | tf_op jit(solution)/shard_map/ppermute | solution.py:41
  97.2 2.4 %collective-permute-done.18 = f32[4,16,128]{2,1,0:T(8,128)S(1)} collective-permute-done((f32[4,16,128]{2,1,0:T(8,128)S(1)}, f32[4,16,128]{2,1,0:T(8,128)S(1)}, u32[]{:S(2)}, u32[]{:S(2)}) %collective-permute-start.18) | collective-permute-done | bytes 32800 | tf_op jit(solution)/shard_map/ppermute | solution.py:41
  100.9 4.0 %collective-permute-start.19 = (f32[4,16,128]{2,1,0:T(8,128)S(1)}, f32[4,16,128]{2,1,0:T(8,128)S(1)}, u32[]{:S(2)}, u32[]{:S(2)}) collective-permute-start(f32[4,16,128]{2,1,0:T(8,128)S(1)} %get-tuple-element.16), channel_id=1, source_target_pairs={{0,8},{1,9},{2,10},{3,11},{4,12},{5,13},{6,14},{7,15},{8,0},{9,1},... | collective-permute-start | bytes 98312 | tf_op jit(solution)/shard_map/ppermute | solution.py:41
  104.9 1.6 %collective-permute-start.22 = (bf16[2,9,16,128]{3,2,1,0:T(8,128)(2,1)S(1)}, bf16[2,9,16,128]{3,2,1,0:T(8,128)(2,1)S(1)}, u32[]{:S(2)}, u32[]{:S(2)}) collective-permute-start(bf16[2,9,16,128]{3,2,1,0:T(8,128)(2,1)S(1)} %pad_maximum_fusion.2), channel_id=1, source_target_pairs={{0,16},{1,17},{2,18},{3,19},{4,20},{5,21},{6,22},{7,23},{8,56},{9,... | collective-permute-start | bytes 221192 | tf_op jit(solution)/shard_map/ppermute | solution.py:41
  106.6 2.8 %collective-permute-done.22 = bf16[2,9,16,128]{3,2,1,0:T(8,128)(2,1)S(1)} collective-permute-done((bf16[2,9,16,128]{3,2,1,0:T(8,128)(2,1)S(1)}, bf16[2,9,16,128]{3,2,1,0:T(8,128)(2,1)S(1)}, u32[]{:S(2)}, u32[]{:S(2)}) %collective-permute-start.22) | collective-permute-done | bytes 73760 | tf_op jit(solution)/shard_map/ppermute | solution.py:41
  109.7 4.3 %collective-permute-done.23 = bf16[4,9,16,128]{3,2,1,0:T(8,128)(2,1)S(1)} collective-permute-done((bf16[4,9,16,128]{3,2,1,0:T(8,128)(2,1)S(1)}, bf16[4,9,16,128]{3,2,1,0:T(8,128)(2,1)S(1)}, u32[]{:S(2)}, u32[]{:S(2)}) %collective-permute-start.23) | collective-permute-done | bytes 147488 | tf_op jit(solution)/shard_map/ppermute | solution.py:41
  115.3 6.1 %collective-permute-start.24 = (f32[2,32,32]{1,2,0:T(8,128)S(1)}, f32[2,32,32]{1,2,0:T(8,128)S(1)}, u32[]{:S(2)}, u32[]{:S(2)}) collective-permute-start(f32[2,32,32]{1,2,0:T(8,128)S(1)} %fusion.8), channel_id=1, source_target_pairs={{0,8},{1,9},{2,10},{3,11},{4,12},{5,13},{6,14},{7,15},{8,0},{9,1},... | collective-permute-start | bytes 24584 | tf_op jit(solution)/shard_map/ppermute | solution.py:41
  (104 shorter events, 18.9 us)
Async XLA Ops:
  0.6 4.2 %collective-permute-start = (bf16[1792,256]{1,0:T(8,128)(2,1)}, bf16[1792,256]{1,0:T(8,128)(2,1)S(1)}, u32[]{:S(2)}, u32[]{:S(2)}) collective-permute-start(bf16[1792,256]{1,0:T(8,128)(2,1)} %param.16), channel_id=1, source_target_pairs={{0,8},{1,9},{2,10},{3,11},{4,12},{5,13},{6,14},{7,15},{8,0},{9,1},... | collective-permute-start | bytes 2752520 | tf_op jit(solution)/shard_map/ppermute | solution.py:41
  2.1 37.9 %collective-permute-start.3 = (bf16[1024,4096]{1,0:T(8,128)(2,1)}, bf16[1024,4096]{1,0:T(8,128)(2,1)}, u32[]{:S(2)}, u32[]{:S(2)}) collective-permute-start(bf16[1024,4096]{1,0:T(8,128)(2,1)} %bitcast.46), channel_id=1, source_target_pairs={{0,8},{1,9},{2,10},{3,11},{4,12},{5,13},{6,14},{7,15},{8,0},{9,1},... | collective-permute-start | bytes 25165832 | tf_op jit(solution)/shard_map/ppermute | solution.py:41
  6.1 20.1 %collective-permute-start.4 = (bf16[896,512]{1,0:T(8,128)(2,1)}, bf16[896,512]{1,0:T(8,128)(2,1)S(1)}, u32[]{:S(2)}, u32[]{:S(2)}) collective-permute-start(bf16[896,512]{1,0:T(8,128)(2,1)} %maximum_select_fusion._.refs_2_), channel_id=1, source_target_pairs={{0,16},{1,17},{2,18},{3,19},{4,20},{5,21},{6,22},{7,23},{8,56},{9,... | collective-permute-start | bytes 2752520 | tf_op jit(solution)/shard_map/ppermute | solution.py:41
  8.9 24.5 %collective-permute-start.6 = (bf16[896,512]{1,0:T(8,128)(2,1)}, bf16[896,512]{1,0:T(8,128)(2,1)S(1)}, u32[]{:S(2)}, u32[]{:S(2)}) collective-permute-start(bf16[896,512]{1,0:T(8,128)(2,1)} %maximum_select_fusion._.refs_2_), channel_id=1, source_target_pairs={{0,64},{1,65},{2,66},{3,67},{4,68},{5,69},{6,70},{7,71},{8,72},{9,... | collective-permute-start | bytes 2752520 | tf_op jit(solution)/shard_map/ppermute | solution.py:41
  22.4 8.4 %collective-permute-start.1 = (f32[64,1152]{1,0:T(8,128)}, f32[64,1152]{1,0:T(8,128)S(1)}, u32[]{:S(2)}, u32[]{:S(2)}) collective-permute-start(f32[64,1152]{1,0:T(8,128)} %early_rows.1.left.refs_1_), channel_id=1, source_target_pairs={{0,1},{1,0},{2,3},{3,2},{4,5},{5,4},{6,7},{7,6},{8,11},{9,10},{10,... | collective-permute-start | bytes 884744 | tf_op jit(solution)/shard_map/ppermute | solution.py:41
  26.2 12.9 %collective-permute-start.5 = (bf16[896,512]{1,0:T(8,128)(2,1)}, bf16[896,512]{1,0:T(8,128)(2,1)S(1)}, u32[]{:S(2)}, u32[]{:S(2)}) collective-permute-start(bf16[896,512]{1,0:T(8,128)(2,1)} %maximum_select_fusion._.refs_2_), channel_id=1, source_target_pairs={{0,48},{1,49},{2,50},{3,51},{4,52},{5,53},{6,54},{7,55},{8,24},{9,... | collective-permute-start | bytes 2752520 | tf_op jit(solution)/shard_map/ppermute | solution.py:41
  27.1 32.1 %collective-permute-start.10 = (bf16[896,512]{1,0:T(8,128)(2,1)}, bf16[896,512]{1,0:T(8,128)(2,1)}, u32[]{:S(2)}, u32[]{:S(2)}) collective-permute-start(bf16[896,512]{1,0:T(8,128)(2,1)} %after.5.refs_5_), channel_id=1, source_target_pairs={{0,64},{1,65},{2,66},{3,67},{4,68},{5,69},{6,70},{7,71},{8,72},{9,... | collective-permute-start | bytes 2752520 | tf_op jit(solution)/shard_map/ppermute | solution.py:41
  33.3 28.5 %collective-permute-start.8 = (bf16[896,512]{1,0:T(8,128)(2,1)S(1)}, bf16[896,512]{1,0:T(8,128)(2,1)}, u32[]{:S(2)}, u32[]{:S(2)}) collective-permute-start(bf16[896,512]{1,0:T(8,128)(2,1)S(1)} %copy-done.6), channel_id=1, source_target_pairs={{0,48},{1,49},{2,50},{3,51},{4,52},{5,53},{6,54},{7,55},{8,24},{9,... | collective-permute-start | bytes 2752520 | tf_op jit(solution)/shard_map/ppermute | solution.py:41
  34.4 28.4 %collective-permute-start.9 = (bf16[896,512]{1,0:T(8,128)(2,1)}, bf16[896,512]{1,0:T(8,128)(2,1)}, u32[]{:S(2)}, u32[]{:S(2)}) collective-permute-start(bf16[896,512]{1,0:T(8,128)(2,1)} %after.7.refs_11_), channel_id=1, source_target_pairs={{0,48},{1,49},{2,50},{3,51},{4,52},{5,53},{6,54},{7,55},{8,24},{9,... | collective-permute-start | bytes 2752520 | tf_op jit(solution)/shard_map/ppermute | solution.py:41
  39.0 37.5 %collective-permute-start.12 = (bf16[1024,1792]{1,0:T(8,128)(2,1)}, bf16[1024,1792]{1,0:T(8,128)(2,1)}, u32[]{:S(2)}, u32[]{:S(2)}) collective-permute-start(bf16[1024,1792]{1,0:T(8,128)(2,1)} %bitcast.65), channel_id=1, source_target_pairs={{0,8},{1,9},{2,10},{3,11},{4,12},{5,13},{6,14},{7,15},{8,0},{9,1},... | collective-permute-start | bytes 11010056 | tf_op jit(solution)/shard_map/ppermute | solution.py:41
  40.0 17.1 %collective-permute-start.2 = (f32[64,1152]{1,0:T(8,128)S(1)}, f32[64,1152]{1,0:T(8,128)S(1)}, u32[]{:S(2)}, u32[]{:S(2)}) collective-permute-start(f32[64,1152]{1,0:T(8,128)S(1)} %copy-done), channel_id=1, source_target_pairs={{0,3},{1,2},{2,1},{3,0},{4,7},{5,6},{6,5},{7,4},{8,9},{9,8},{10,11... | collective-permute-start | bytes 884744 | tf_op jit(solution)/shard_map/ppermute | solution.py:41
  58.9 20.6 %collective-permute-start.7 = (f32[64,1152]{1,0:T(8,128)S(1)}, f32[64,1152]{1,0:T(8,128)S(1)}, u32[]{:S(2)}, u32[]{:S(2)}) collective-permute-start(f32[64,1152]{1,0:T(8,128)S(1)} %add.114.refs_10_.refs_7_), channel_id=1, source_target_pairs={{0,4},{1,5},{2,6},{3,7},{4,0},{5,1},{6,2},{7,3},{8,12},{9,13},{10,... | collective-permute-start | bytes 884744 | tf_op jit(solution)/shard_map/ppermute | solution.py:41
  59.3 20.2 %collective-permute-start.13 = (f32[64,1152]{1,0:T(8,128)S(1)}, f32[64,1152]{1,0:T(8,128)S(1)}, u32[]{:S(2)}, u32[]{:S(2)}) collective-permute-start(f32[64,1152]{1,0:T(8,128)S(1)} %add.114.refs_10_.refs_7_), channel_id=1, source_target_pairs={{0,8},{1,9},{2,10},{3,11},{4,12},{5,13},{6,14},{7,15},{8,0},{9,1},... | collective-permute-start | bytes 884744 | tf_op jit(solution)/shard_map/ppermute | solution.py:41
  61.8 17.6 %collective-permute-start.14 = (f32[64,1152]{1,0:T(8,128)S(1)}, f32[64,1152]{1,0:T(8,128)S(1)}, u32[]{:S(2)}, u32[]{:S(2)}) collective-permute-start(f32[64,1152]{1,0:T(8,128)S(1)} %add.114.refs_10_.refs_7_), channel_id=1, source_target_pairs={{0,12},{1,13},{2,14},{3,15},{4,8},{5,9},{6,10},{7,11},{8,4},{9,5},... | collective-permute-start | bytes 884744 | tf_op jit(solution)/shard_map/ppermute | solution.py:41
  62.8 16.7 %collective-permute-start.11 = (bf16[896,512]{1,0:T(8,128)(2,1)}, bf16[896,512]{1,0:T(8,128)(2,1)S(1)}, u32[]{:S(2)}, u32[]{:S(2)}) collective-permute-start(bf16[896,512]{1,0:T(8,128)(2,1)} %after.9.refs_9_), channel_id=1, source_target_pairs={{0,48},{1,49},{2,50},{3,51},{4,52},{5,53},{6,54},{7,55},{8,24},{9,... | collective-permute-start | bytes 2752520 | tf_op jit(solution)/shard_map/ppermute | solution.py:41
  76.6 12.3 %collective-permute-start.20 = (s32[2]{0:T(128)S(1)}, s32[2]{0:T(128)S(1)}, u32[]{:S(2)}, u32[]{:S(2)}) collective-permute-start(s32[2]{0:T(128)S(1)} %copy-done.10), channel_id=1, source_target_pairs={{0,8},{1,9},{2,10},{3,11},{4,12},{5,13},{6,14},{7,15},{8,0},{9,1},... | collective-permute-start | bytes 32 | tf_op jit(solution)/shard_map/ppermute | solution.py:41
  90.2 4.0 %collective-permute-start.16 = (f32[4,16,128]{2,1,0:T(8,128)S(1)}, f32[4,16,128]{2,1,0:T(8,128)S(1)}, u32[]{:S(2)}, u32[]{:S(2)}) collective-permute-start(f32[4,16,128]{2,1,0:T(8,128)S(1)} %dynamic-slice_add_fusion), channel_id=1, source_target_pairs={{0,1},{1,0},{2,3},{3,2},{4,5},{5,4},{6,7},{7,6},{8,11},{9,10},{10,... | collective-permute-start | bytes 98312 | tf_op jit(solution)/shard_map/ppermute | solution.py:41
  94.2 2.8 %collective-permute-start.17 = (f32[4,16,128]{2,1,0:T(8,128)S(1)}, f32[4,16,128]{2,1,0:T(8,128)S(1)}, u32[]{:S(2)}, u32[]{:S(2)}) collective-permute-start(f32[4,16,128]{2,1,0:T(8,128)S(1)} %add.118), channel_id=1, source_target_pairs={{0,3},{1,2},{2,1},{3,0},{4,7},{5,6},{6,5},{7,4},{8,9},{9,8},{10,11... | collective-permute-start | bytes 98312 | tf_op jit(solution)/shard_map/ppermute | solution.py:41
  96.9 2.8 %collective-permute-start.18 = (f32[4,16,128]{2,1,0:T(8,128)S(1)}, f32[4,16,128]{2,1,0:T(8,128)S(1)}, u32[]{:S(2)}, u32[]{:S(2)}) collective-permute-start(f32[4,16,128]{2,1,0:T(8,128)S(1)} %add.119), channel_id=1, source_target_pairs={{0,4},{1,5},{2,6},{3,7},{4,0},{5,1},{6,2},{7,3},{8,12},{9,13},{10,... | collective-permute-start | bytes 98312 | tf_op jit(solution)/shard_map/ppermute | solution.py:41
  99.8 5.1 %collective-permute-start.21 = (bf16[9,16,128]{2,1,0:T(8,128)(2,1)S(1)}, bf16[9,16,128]{2,1,0:T(8,128)(2,1)S(1)}, u32[]{:S(2)}, u32[]{:S(2)}) collective-permute-start(bf16[9,16,128]{2,1,0:T(8,128)(2,1)S(1)} %get-tuple-element.24), channel_id=1, source_target_pairs={{0,68},{1,69},{2,70},{3,71},{4,64},{5,65},{6,66},{7,67},{8,76},{9,... | collective-permute-start | bytes 110600 | tf_op jit(solution)/shard_map/ppermute | solution.py:41
  100.9 8.6 %collective-permute-start.19 = (f32[4,16,128]{2,1,0:T(8,128)S(1)}, f32[4,16,128]{2,1,0:T(8,128)S(1)}, u32[]{:S(2)}, u32[]{:S(2)}) collective-permute-start(f32[4,16,128]{2,1,0:T(8,128)S(1)} %get-tuple-element.16), channel_id=1, source_target_pairs={{0,8},{1,9},{2,10},{3,11},{4,12},{5,13},{6,14},{7,15},{8,0},{9,1},... | collective-permute-start | bytes 98312 | tf_op jit(solution)/shard_map/ppermute | solution.py:41
  104.9 4.5 %collective-permute-start.22 = (bf16[2,9,16,128]{3,2,1,0:T(8,128)(2,1)S(1)}, bf16[2,9,16,128]{3,2,1,0:T(8,128)(2,1)S(1)}, u32[]{:S(2)}, u32[]{:S(2)}) collective-permute-start(bf16[2,9,16,128]{3,2,1,0:T(8,128)(2,1)S(1)} %pad_maximum_fusion.2), channel_id=1, source_target_pairs={{0,16},{1,17},{2,18},{3,19},{4,20},{5,21},{6,22},{7,23},{8,56},{9,... | collective-permute-start | bytes 221192 | tf_op jit(solution)/shard_map/ppermute | solution.py:41
  109.4 4.5 %collective-permute-start.23 = (bf16[4,9,16,128]{3,2,1,0:T(8,128)(2,1)S(1)}, bf16[4,9,16,128]{3,2,1,0:T(8,128)(2,1)S(1)}, u32[]{:S(2)}, u32[]{:S(2)}) collective-permute-start(bf16[4,9,16,128]{3,2,1,0:T(8,128)(2,1)S(1)} %pad_maximum_fusion.1), channel_id=1, source_target_pairs={{0,48},{1,49},{2,50},{3,51},{4,52},{5,53},{6,54},{7,55},{8,24},{9,... | collective-permute-start | bytes 442376 | tf_op jit(solution)/shard_map/ppermute | solution.py:41
  115.3 7.0 %collective-permute-start.24 = (f32[2,32,32]{1,2,0:T(8,128)S(1)}, f32[2,32,32]{1,2,0:T(8,128)S(1)}, u32[]{:S(2)}, u32[]{:S(2)}) collective-permute-start(f32[2,32,32]{1,2,0:T(8,128)S(1)} %fusion.8), channel_id=1, source_target_pairs={{0,8},{1,9},{2,10},{3,11},{4,12},{5,13},{6,14},{7,15},{8,0},{9,1},... | collective-permute-start | bytes 24584 | tf_op jit(solution)/shard_map/ppermute | solution.py:41
  (14 other events, 86.1 us)
